TPU v7x, 32 devices: a whole 2x2x4 slice. The times are simulated.
32 devices in a mesh: pairs: 2 (over x), rows: 16 (over z, y, core).
Axes of the slice: x: 2, y: 2, z: 4, core: 2. Of those that a mesh axis runs over, the one named last changes fastest.
Arguments:
- frames: bfloat16 [2, 512, 3072], P(None, ('pairs', 'rows')), parts along dimension 1, may hold values from -6 to 6
- conv_weight: bfloat16 [864, 128], replicated, may hold values from -0.21875 to 0.21875
- conv_bias: float32 [128], replicated, may hold values from -3 to 3
- proj_weight: bfloat16 [128, 256], replicated, may hold values from -0.5 to 0.5
- target_row: int32 [12, 4096], P(None, ('pairs', 'rows')), parts along dimension 1, may hold values from 0 to 127
- target_col: int32 [12, 4096], P(None, ('pairs', 'rows')), parts along dimension 1, may hold values from 0 to 15
- cotangent: bfloat16 [3888, 4096], P(None, ('pairs', 'rows')), parts along dimension 1, may hold values from -1.5 to 1.5
Outputs:
- lookups: bfloat16 [3888, 4096], P(None, ('pairs', 'rows')), parts along dimension 1
- grad_input: bfloat16 [2, 512, 3072], P(None, ('pairs', 'rows')), parts along dimension 1
- grad_conv: float32 [1728, 128], P('pairs'), parts along dimension 0
- grad_bias: float32 [256], P('pairs'), parts along dimension 0
- grad_proj: float32 [256, 256], P('pairs'), parts along dimension 0
There are 2 independent parts, one for each index of `pairs`. A program takes and returns all parts, laid end to end along the dimension named above; an argument that names none is the same for every part. Nothing has to cross between parts.
Inputs may be any that keep to these rules, and one draw needn't show every extreme that they name: `target_row`: row of a cell of the feature grid. `target_col`: column of a cell of the feature grid.
All inputs are finite; a program needn't handle non-finite values.
Results may differ from a plain program's by a relative error of at most 0.018.
Values may be sent and summed in bfloat16 or wider, within the bound.
No kernel may reach another device: no remote copies, remote signals or barrier semaphores. Data moves between devices by JAX's collectives and lax.ppermute only.
A program may use at most 128 MiB of HBM per device.

v0:
```python
import math

import jax
import jax.numpy as jnp
from jax import lax
from jax.sharding import PartitionSpec as P

C = 256
C0 = 96
LEVELS = 4
RADIUS = 4
ITERS = 12
RD = 8
WC = 16
PACK = 170
LOOKS = 3888


def shifted(value, axis, by):
    devices = lax.axis_size(axis)
    pairs = [(i, i + by) for i in range(devices) if 0 <= i + by < devices]
    return lax.ppermute(value, axis, pairs)


def encode_patches(padded, out_rows):
    taps = [
        padded[:, row_tap : row_tap + 2 * out_rows : 2, col_tap : col_tap + 2 * WC : 2, :]
        for row_tap in range(3)
        for col_tap in range(3)
    ]
    return jnp.concatenate(taps, axis=-1)


def scatter_taps(grad_patches, out_rows):
    summed = jnp.zeros((2, 2 * out_rows + 1, 2 * WC + 2, C0), jnp.float32)
    for row_tap in range(3):
        for col_tap in range(3):
            summed = summed.at[
                :, row_tap : row_tap + 2 * out_rows : 2, col_tap : col_tap + 2 * WC : 2, :
            ].add(grad_patches[:, :, :, row_tap, col_tap, :])
    return summed


def pool_levels(grid_map):
    shard_count = grid_map.shape[0]
    parts_list = []
    for level_no in range(LEVELS):
        factor = 2**level_no
        pooled = (
            grid_map.astype(jnp.float32)
            .reshape(shard_count, RD // factor, factor, WC // factor, factor, C)
            .mean(axis=(2, 4))
        )
        parts_list.append(
            pooled.astype(jnp.bfloat16).reshape(shard_count, RD // factor * (WC // factor), C)
        )
    return jnp.concatenate(parts_list, axis=1).reshape(shard_count * PACK, C)


def spread_levels(own_cells):
    shard_count = own_cells.shape[0]
    summed = jnp.zeros((shard_count, RD, WC, C), jnp.float32)
    offset = 0
    for level_no in range(LEVELS):
        factor = 2**level_no
        level_rows = RD // factor
        level_cols = WC // factor
        segment = own_cells[:, offset : offset + level_rows * level_cols].reshape(
            shard_count, level_rows, 1, level_cols, 1, C
        )
        spread = jnp.broadcast_to(
            segment, (shard_count, level_rows, factor, level_cols, factor, C)
        ).reshape(shard_count, RD, WC, C)
        summed = summed + spread / (factor * factor)
        offset = offset + level_rows * level_cols
    return summed.reshape(shard_count * RD * WC, C)


def split_levels(volume, device_count, pixels):
    packed = volume.reshape(device_count, PACK, pixels)
    level_grids = []
    offset = 0
    for level_no in range(LEVELS):
        factor = 2**level_no
        level_rows = RD // factor
        level_cols = WC // factor
        segment = packed[:, offset : offset + level_rows * level_cols, :]
        level_grids.append(segment.reshape(device_count * level_rows, level_cols, pixels))
        offset = offset + level_rows * level_cols
    return level_grids


def join_levels(level_grads, device_count, pixels):
    parts_list = []
    for level_no in range(LEVELS):
        factor = 2**level_no
        parts_list.append(
            level_grads[level_no].reshape(device_count, RD // factor * (WC // factor), pixels)
        )
    return jnp.concatenate(parts_list, axis=1).reshape(device_count * PACK, pixels)


def per_device(frames, conv_weight, conv_bias, proj_weight, target_row, target_col, cotangent):
    device_count = lax.axis_size("rows")
    pixels = RD * WC
    span = 2 * RADIUS + 1
    above_row = shifted(frames[:, -1:, :], "rows", 1)
    extended = jnp.concatenate([above_row, frames], axis=1).reshape(2, 2 * RD + 1, 2 * WC, C0)
    padded = jnp.pad(extended, ((0, 0), (0, 0), (1, 1), (0, 0)))
    patches = encode_patches(padded, RD).reshape(2 * pixels, 9 * C0)
    preact = jnp.dot(patches, conv_weight, preferred_element_type=jnp.float32) + conv_bias
    hidden = jnp.maximum(preact, 0.0).astype(jnp.bfloat16)
    features = jnp.dot(hidden, proj_weight, preferred_element_type=jnp.float32).astype(jnp.bfloat16)
    first_map = features[:pixels]
    second_map = features[pixels:]
    base_rows = lax.all_gather(second_map, "rows", axis=0, tiled=True)
    pyramid = pool_levels(base_rows.reshape(device_count, RD, WC, C))
    inv_root = 1.0 / math.sqrt(C)
    volume = lax.dot_general(
        pyramid, first_map, (((1,), (1,)), ((), ())), preferred_element_type=jnp.float32
    )
    level_grids = split_levels(volume, device_count, pixels)
    offsets = jnp.arange(span, dtype=jnp.int32) - RADIUS
    cot_iters = cotangent.reshape(ITERS, LEVELS, span, span, pixels)

    def lookup_step(running, inputs):
        row_now, col_now, cot_now = inputs
        looked_parts = []
        updated = []
        for level_no in range(LEVELS):
            factor = 2**level_no
            grid_now = level_grids[level_no]
            grid_rows = grid_now.shape[0]
            grid_cols = grid_now.shape[1]
            rows_hit = (
                jnp.arange(grid_rows, dtype=jnp.int32)[None, :, None]
                == (row_now // factor)[None, None, :] + offsets[:, None, None]
            )
            cols_hit = (
                jnp.arange(grid_cols, dtype=jnp.int32)[None, :, None]
                == (col_now // factor)[None, None, :] + offsets[:, None, None]
            ).astype(jnp.float32)
            band_rows = jnp.einsum(
                "yup,uvp->yvp",
                rows_hit.astype(jnp.float32),
                grid_now,
                precision=lax.Precision.HIGHEST,
                preferred_element_type=jnp.float32,
            )
            looked_parts.append(jnp.sum(band_rows[:, None, :, :] * cols_hit[None, :, :, :], axis=2))
            cot_level = cot_now[level_no].astype(jnp.float32)
            spread_cols = jnp.sum(cot_level[:, :, None, :] * cols_hit[None, :, :, :], axis=1)
            grad_term = jnp.einsum(
                "yup,yvp->uvp",
                rows_hit.astype(jnp.bfloat16),
                spread_cols.astype(jnp.bfloat16),
                preferred_element_type=jnp.float32,
            )
            updated.append(running[level_no] + grad_term)
        return (tuple(updated), jnp.stack(looked_parts, 0))

    start_grads = tuple((jnp.zeros(grid_now.shape, jnp.float32) for grid_now in level_grids))
    level_grads, looked_all = lax.scan(
        lookup_step, start_grads, (target_row, target_col, cot_iters)
    )
    lookups = (looked_all.reshape(LOOKS, pixels) * inv_root).astype(jnp.bfloat16)
    grad_volume = join_levels(level_grads, device_count, pixels).astype(jnp.bfloat16)
    grad_first = (
        lax.dot_general(
            grad_volume, pyramid, (((0,), (0,)), ((), ())), preferred_element_type=jnp.float32
        )
        * inv_root
    )
    partial_value = jnp.dot(grad_volume, first_map, preferred_element_type=jnp.float32) * inv_root
    rounded = lax.optimization_barrier(partial_value.astype(jnp.bfloat16)).astype(jnp.float32)
    spread_all = spread_levels(rounded.reshape(device_count, PACK, C))
    grad_second = lax.psum_scatter(
        spread_all.astype(jnp.bfloat16), "rows", scatter_dimension=0, tiled=True
    ).astype(jnp.float32)
    grad_feats = jnp.concatenate([grad_first, grad_second], axis=0).astype(jnp.bfloat16)
    grad_proj = lax.dot_general(
        hidden, grad_feats, (((0,), (0,)), ((), ())), preferred_element_type=jnp.float32
    )
    grad_hidden = lax.dot_general(
        grad_feats, proj_weight, (((1,), (1,)), ((), ())), preferred_element_type=jnp.float32
    )
    grad_preact = jnp.where(preact > 0.0, grad_hidden, 0.0).astype(jnp.bfloat16)
    grad_bias = jnp.sum(grad_preact.astype(jnp.float32), axis=0)
    grad_conv = lax.dot_general(
        patches, grad_preact, (((0,), (0,)), ((), ())), preferred_element_type=jnp.float32
    )
    grad_patches = lax.dot_general(
        grad_preact, conv_weight, (((1,), (1,)), ((), ())), preferred_element_type=jnp.float32
    ).reshape(2, RD, WC, 3, 3, C0)
    grad_padded = scatter_taps(grad_patches, RD)
    top_row = grad_padded[:, 0:1, 1 : 2 * WC + 1, :].reshape(2, 1, 2 * WC * C0)
    from_below = shifted(top_row, "rows", -1)
    own_grad = grad_padded[:, 1:, 1 : 2 * WC + 1, :].reshape(2, 2 * RD, 2 * WC * C0)
    own_grad = own_grad.at[:, -1:, :].add(from_below)
    grad_input = own_grad.astype(jnp.bfloat16)
    reduced = (
        lax.psum(grad_conv.astype(jnp.bfloat16), "rows").astype(jnp.float32),
        lax.psum(grad_bias.astype(jnp.bfloat16), "rows").astype(jnp.float32),
        lax.psum(grad_proj.astype(jnp.bfloat16), "rows").astype(jnp.float32),
    )
    return (lookups, grad_input, reduced[0], reduced[1], reduced[2])


def solution(mesh):
    return jax.shard_map(
        per_device,
        mesh=mesh,
        in_specs=(
            P(None, ("pairs", "rows"), None),
            P(),
            P(),
            P(),
            P(None, ("pairs", "rows")),
            P(None, ("pairs", "rows")),
            P(None, ("pairs", "rows")),
        ),
        out_specs=(
            P(None, ("pairs", "rows")),
            P(None, ("pairs", "rows"), None),
            P("pairs", None),
            P("pairs"),
            P("pairs", None),
        ),
        check_vma=False,
    )
```

profile of v0, /device:TPU:0, one launch (start us, length us, event | category | flops | bytes accessed | tf_op | source)
XLA Modules:
  0.0 609.1 jit_solution(12910428172026836186)
XLA Ops:
  8.2 2.4 collective-permute-start
  22.0 40.6 %all-gather.2.cloned.1.call-done = bf16[2048,256]{1,0:T(8,128)(2,1)} async-done(((bf16[128,256]{1,0:T(8,128)(2,1)}), bf16[2048,256]{1,0:T(8,128)(2,1)}) %all-gather.2.cloned.1.call-update) | async-done | bytes 1048592 | tf_op jit(solution)/shard_map/all_gather | solution.py:116
  62.6 3.1 reshape.716
  65.6 3.3 reduce_sum.147
  70.7 2.3 reduce_sum.148
  83.1 250.8 %while.24 = (s32[]{:T(128)}, f32[128,16,128]{0,1,2:T(8,128)S(1)}, f32[64,8,128]{0,1,2:T(8,128)}, f32[32,4,128]{0,1,2:T(4,128)}, f32[16,2,128]{0,1,2:T(2,128)}, /...) while((s32[]{:T(128)}, f32[128,16,128]{0,1,2:T(8,128)S(1)}, ...), condition=%wide.region_12.13_spmd.clone.clone, body=%wide.region_3.12_spmd.clone.clone.sunk | while | flops 46540044 | bytes 8804426 | solution.py:163
  121.1 2.2 fusion.100
  142.1 2.2 fusion.100
  163.0 2.2 fusion.100
  183.9 2.2 fusion.100
  204.8 2.2 fusion.100
  225.7 2.2 fusion.100
  246.6 2.2 fusion.100
  267.6 2.2 fusion.100
  288.5 2.2 fusion.100
  309.4 2.2 fusion.100
  342.9 2.5 div.111
  347.2 3.1 div.115
  350.3 3.6 fusion.25
  354.9 2.4 multiply_convert_fusion
  360.5 49.9 %reduce-scatter.2.cloned.1.call-done = bf16[128,256]{1,0:T(8,128)(2,1)} async-done(((bf16[2048,256]{1,0:T(8,128)(2,1)}), bf16[128,256]{1,0:T(8,128)(2,1)}) %reduce-scatter.2.cloned.1.call-update) | async-done | bytes 65552 | tf_op jit(solution)/shard_map/reduce_scatter | solution.py:177
  416.2 6.6 %scatter_fusion = f32[2,17,34,96]{3,0,2,1:T(2,128)S(1)} fusion(f32[2,17,34,96]{3,0,2,1:T(2,128)S(1)} %broadcast_in_dim.109, s32[128]{0:T(128)S(1)} %reshape.721, f32[128,2,96]{2,1,0:T(2,128)S(1)} %copy.120), kind=kCustom, calls=%fused_computation | custom fusion | flops 24576 | bytes 295936 | tf_op jit(solution)/shard_map/scatter-add | solution.py:40
  422.9 6.6 %scatter_fusion.1 = f32[2,17,34,96]{3,0,2,1:T(2,128)S(1)} fusion(f32[2,17,34,96]{3,0,2,1:T(2,128)S(1)} %scatter_fusion, s32[128]{0:T(128)S(1)} %reshape.727, f32[128,2,96]{2,1,0:T(2,128)S(1)} %copy.121), kind=kCustom, calls=%fused_computation.1 | custom fusion | flops 24576 | bytes 295936 | tf_op jit(solution)/shard_map/scatter-add | solution.py:40
  429.5 6.6 %scatter_fusion.2 = f32[2,17,34,96]{3,0,2,1:T(2,128)S(1)} fusion(f32[2,17,34,96]{3,0,2,1:T(2,128)S(1)} %scatter_fusion.1, s32[128]{0:T(128)S(1)} %reshape.733, f32[128,2,96]{2,1,0:T(2,128)S(1)} %copy.122), kind=kCustom, calls=%fused_computation.2 | custom fusion | flops 24576 | bytes 295936 | tf_op jit(solution)/shard_map/scatter-add | solution.py:40
  436.1 6.6 %scatter_fusion.3 = f32[2,17,34,96]{3,0,2,1:T(2,128)S(1)} fusion(f32[2,17,34,96]{3,0,2,1:T(2,128)S(1)} %scatter_fusion.2, s32[128]{0:T(128)S(1)} %reshape.739, f32[128,2,96]{2,1,0:T(2,128)S(1)} %copy.123), kind=kCustom, calls=%fused_computation.3 | custom fusion | flops 24576 | bytes 295936 | tf_op jit(solution)/shard_map/scatter-add | solution.py:40
  442.8 6.6 %scatter_fusion.4 = f32[2,17,34,96]{3,0,2,1:T(2,128)S(1)} fusion(f32[2,17,34,96]{3,0,2,1:T(2,128)S(1)} %scatter_fusion.3, s32[128]{0:T(128)S(1)} %reshape.745, f32[128,2,96]{2,1,0:T(2,128)S(1)} %copy.124), kind=kCustom, calls=%fused_computation.4 | custom fusion | flops 24576 | bytes 295936 | tf_op jit(solution)/shard_map/scatter-add | solution.py:40
  449.4 6.6 %scatter_fusion.5 = f32[2,17,34,96]{3,0,2,1:T(2,128)S(1)} fusion(f32[2,17,34,96]{3,0,2,1:T(2,128)S(1)} %scatter_fusion.4, s32[128]{0:T(128)S(1)} %reshape.751, f32[128,2,96]{2,1,0:T(2,128)S(1)} %copy.125), kind=kCustom, calls=%fused_computation.5 | custom fusion | flops 24576 | bytes 295936 | tf_op jit(solution)/shard_map/scatter-add | solution.py:40
  456.0 6.6 %scatter_fusion.6 = f32[2,17,34,96]{3,0,2,1:T(2,128)S(1)} fusion(f32[2,17,34,96]{3,0,2,1:T(2,128)S(1)} %scatter_fusion.5, s32[128]{0:T(128)S(1)} %reshape.757, f32[128,2,96]{2,1,0:T(2,128)S(1)} %copy.126), kind=kCustom, calls=%fused_computation.6 | custom fusion | flops 24576 | bytes 295936 | tf_op jit(solution)/shard_map/scatter-add | solution.py:40
  462.7 6.6 %scatter_fusion.7 = f32[2,17,34,96]{3,0,2,1:T(2,128)S(1)} fusion(f32[2,17,34,96]{3,0,2,1:T(2,128)S(1)} %scatter_fusion.6, s32[128]{0:T(128)S(1)} %reshape.763, f32[128,2,96]{2,1,0:T(2,128)S(1)} %copy.127), kind=kCustom, calls=%fused_computation.7 | custom fusion | flops 24576 | bytes 295936 | tf_op jit(solution)/shard_map/scatter-add | solution.py:40
  469.3 6.6 %scatter_fusion.8 = f32[2,17,34,96]{3,0,2,1:T(2,128)S(1)} fusion(f32[2,17,34,96]{3,0,2,1:T(2,128)S(1)} %scatter_fusion.7, s32[128]{0:T(128)S(1)} %reshape.769, f32[128,2,96]{2,1,0:T(2,128)S(1)} %copy.128), kind=kCustom, calls=%fused_computation.8 | custom fusion | flops 24576 | bytes 295936 | tf_op jit(solution)/shard_map/scatter-add | solution.py:40
  478.6 32.5 %psum.22 = bf16[128]{0:T(256)(128)(2,1)S(1)} all-reduce(bf16[128]{0:T(256)(128)(2,1)S(1)} %get-tuple-element.484), channel_id=1, replica_groups=mesh['pairs'=2,'rows'=16] {'rows'}, use_global_device_ids=true, to_apply=%region_25.26 | all-reduce | flops 128 | bytes 512 | tf_op jit(solution)/shard_map/psum | solution.py:203
  512.7 86.6 %all-reduce.4.cloned.1.call-done = (bf16[864,128]{1,0:T(8,128)(2,1)}, bf16[128,256]{1,0:T(8,128)(2,1)}) async-done(((bf16[864,128]{1,0:T(8,128)(2,1)}, bf16[128,256]{1,0:T(8,128)(2,1)}), (bf16[864,128]{1,0:T(8,128)(2,1)}, bf16[128,256]{1,0:T(8,128)(2,1)})) %all-reduce.4.cloned.1.call-update) | async-done | bytes 286736 | tf_op jit(solution)/shard_map/psum | solution.py:202
  (815 shorter events, 278.5 us)
Async XLA Ops:
  7.2 10.8 %copy-start = (bf16[864,128]{1,0:T(8,128)(2,1)S(1)}, bf16[864,128]{1,0:T(8,128)(2,1)}, u32[]{:S(2)}) copy-start(bf16[864,128]{1,0:T(8,128)(2,1)} %param.12) | copy-start | bytes 663556
  7.2 10.8 %copy-start.35 = (f32[128]{0:T(128)S(1)}, f32[128]{0:T(128)}, u32[]{:S(2)}) copy-start(f32[128]{0:T(128)} %param.13) | copy-start | bytes 1540
  7.2 55.4 %all-gather.2.cloned.1.call-start = ((), (), s32[]{:S(2)}) async-start(), calls=%async_computation.1 | async-start | bytes 1114112 | tf_op jit(solution)/shard_map/all_gather | solution.py:116
  8.2 3.2 collective-permute-start
  12.4 6.5 %copy-start.27 = (bf16[128,256]{1,0:T(8,128)(2,1)S(1)}, bf16[128,256]{1,0:T(8,128)(2,1)}, u32[]{:S(2)}) copy-start(bf16[128,256]{1,0:T(8,128)(2,1)} %param.14) | copy-start | bytes 196612
  12.7 7.2 %copy-start.15 = (bf16[3888,128]{1,0:T(8,128)(2,1)S(1)}, bf16[3888,128]{1,0:T(8,128)(2,1)}, u32[]{:S(2)}) copy-start(bf16[3888,128]{1,0:T(8,128)(2,1)} %param.17) | copy-start | bytes 2985988
  19.1 57.4 %copy-start.19 = (bf16[256,256]{1,0:T(8,128)(2,1)}, bf16[256,256]{1,0:T(8,128)(2,1)S(1)}, u32[]{:S(2)}) copy-start(bf16[256,256]{1,0:T(8,128)(2,1)S(1)} %convolution_convert_fusion.1) | copy-start | bytes 393220
  19.8 390.6 %reduce-scatter.2.cloned.1.call-start = ((), (), s32[]{:S(2)}) async-start(), calls=%async_computation.2 | async-start | bytes 1114112 | tf_op jit(solution)/shard_map/reduce_scatter | solution.py:177
  69.0 7.5 %copy-start.21 = (bf16[16,32,256]{2,1,0:T(8,128)(2,1)}, bf16[16,32,256]{2,1,0:T(8,128)(2,1)S(1)}, u32[]{:S(2)}) copy-start(bf16[16,32,256]{2,1,0:T(8,128)(2,1)S(1)} %fusion.32) | copy-start | bytes 786436
  86.2 8.0 %copy-start.16 = (s32[9,128]{1,0:T(8,128)S(1)}, s32[9,128]{1,0:T(8,128)}, u32[]{:S(2)}) copy-start(s32[9,128]{1,0:T(8,128)} %get-tuple-element.621) | copy-start | bytes 13828 | tf_op jit(solution)/shard_map/while
  90.1 6.2 %copy-start.17 = (s32[9,128]{1,0:T(8,128)S(1)}, s32[9,128]{1,0:T(8,128)}, u32[]{:S(2)}) copy-start(s32[9,128]{1,0:T(8,128)} %get-tuple-element.622) | copy-start | bytes 13828 | tf_op jit(solution)/shard_map/while
  106.9 8.0 %copy-start.16 = (s32[9,128]{1,0:T(8,128)S(1)}, s32[9,128]{1,0:T(8,128)}, u32[]{:S(2)}) copy-start(s32[9,128]{1,0:T(8,128)} %get-tuple-element.621) | copy-start | bytes 13828 | tf_op jit(solution)/shard_map/while
  127.8 8.0 %copy-start.16 = (s32[9,128]{1,0:T(8,128)S(1)}, s32[9,128]{1,0:T(8,128)}, u32[]{:S(2)}) copy-start(s32[9,128]{1,0:T(8,128)} %get-tuple-element.621) | copy-start | bytes 13828 | tf_op jit(solution)/shard_map/while
  148.8 8.0 %copy-start.16 = (s32[9,128]{1,0:T(8,128)S(1)}, s32[9,128]{1,0:T(8,128)}, u32[]{:S(2)}) copy-start(s32[9,128]{1,0:T(8,128)} %get-tuple-element.621) | copy-start | bytes 13828 | tf_op jit(solution)/shard_map/while
  152.7 6.2 %copy-start.17 = (s32[9,128]{1,0:T(8,128)S(1)}, s32[9,128]{1,0:T(8,128)}, u32[]{:S(2)}) copy-start(s32[9,128]{1,0:T(8,128)} %get-tuple-element.622) | copy-start | bytes 13828 | tf_op jit(solution)/shard_map/while
  169.7 8.0 %copy-start.16 = (s32[9,128]{1,0:T(8,128)S(1)}, s32[9,128]{1,0:T(8,128)}, u32[]{:S(2)}) copy-start(s32[9,128]{1,0:T(8,128)} %get-tuple-element.621) | copy-start | bytes 13828 | tf_op jit(solution)/shard_map/while
  190.6 8.0 %copy-start.16 = (s32[9,128]{1,0:T(8,128)S(1)}, s32[9,128]{1,0:T(8,128)}, u32[]{:S(2)}) copy-start(s32[9,128]{1,0:T(8,128)} %get-tuple-element.621) | copy-start | bytes 13828 | tf_op jit(solution)/shard_map/while
  194.5 6.2 %copy-start.17 = (s32[9,128]{1,0:T(8,128)S(1)}, s32[9,128]{1,0:T(8,128)}, u32[]{:S(2)}) copy-start(s32[9,128]{1,0:T(8,128)} %get-tuple-element.622) | copy-start | bytes 13828 | tf_op jit(solution)/shard_map/while
  211.5 8.0 %copy-start.16 = (s32[9,128]{1,0:T(8,128)S(1)}, s32[9,128]{1,0:T(8,128)}, u32[]{:S(2)}) copy-start(s32[9,128]{1,0:T(8,128)} %get-tuple-element.621) | copy-start | bytes 13828 | tf_op jit(solution)/shard_map/while
  232.4 8.0 %copy-start.16 = (s32[9,128]{1,0:T(8,128)S(1)}, s32[9,128]{1,0:T(8,128)}, u32[]{:S(2)}) copy-start(s32[9,128]{1,0:T(8,128)} %get-tuple-element.621) | copy-start | bytes 13828 | tf_op jit(solution)/shard_map/while
  253.3 8.0 %copy-start.16 = (s32[9,128]{1,0:T(8,128)S(1)}, s32[9,128]{1,0:T(8,128)}, u32[]{:S(2)}) copy-start(s32[9,128]{1,0:T(8,128)} %get-tuple-element.621) | copy-start | bytes 13828 | tf_op jit(solution)/shard_map/while
  274.3 8.0 %copy-start.16 = (s32[9,128]{1,0:T(8,128)S(1)}, s32[9,128]{1,0:T(8,128)}, u32[]{:S(2)}) copy-start(s32[9,128]{1,0:T(8,128)} %get-tuple-element.621) | copy-start | bytes 13828 | tf_op jit(solution)/shard_map/while
  278.2 6.2 %copy-start.17 = (s32[9,128]{1,0:T(8,128)S(1)}, s32[9,128]{1,0:T(8,128)}, u32[]{:S(2)}) copy-start(s32[9,128]{1,0:T(8,128)} %get-tuple-element.622) | copy-start | bytes 13828 | tf_op jit(solution)/shard_map/while
  295.2 8.0 %copy-start.16 = (s32[9,128]{1,0:T(8,128)S(1)}, s32[9,128]{1,0:T(8,128)}, u32[]{:S(2)}) copy-start(s32[9,128]{1,0:T(8,128)} %get-tuple-element.621) | copy-start | bytes 13828 | tf_op jit(solution)/shard_map/while
  299.1 6.2 %copy-start.17 = (s32[9,128]{1,0:T(8,128)S(1)}, s32[9,128]{1,0:T(8,128)}, u32[]{:S(2)}) copy-start(s32[9,128]{1,0:T(8,128)} %get-tuple-element.622) | copy-start | bytes 13828 | tf_op jit(solution)/shard_map/while
  316.1 8.0 %copy-start.16 = (s32[9,128]{1,0:T(8,128)S(1)}, s32[9,128]{1,0:T(8,128)}, u32[]{:S(2)}) copy-start(s32[9,128]{1,0:T(8,128)} %get-tuple-element.621) | copy-start | bytes 13828 | tf_op jit(solution)/shard_map/while
  354.0 245.3 %all-reduce.4.cloned.1.call-start = ((), (), s32[]{:S(2)}) async-start(), calls=%async_computation.3 | async-start | bytes 573440 | tf_op jit(solution)/shard_map/psum | solution.py:202
  358.9 51.6 %copy-start.14 = (f32[256,128]{1,0:T(8,128)S(1)}, f32[256,128]{1,0:T(8,128)}, u32[]{:S(2)}) copy-start(f32[256,128]{1,0:T(8,128)} %copy-done.13) | copy-start | bytes 393220
  358.9 51.6 %copy-start.28 = (bf16[128,256]{1,0:T(8,128)(2,1)S(1)}, bf16[128,256]{1,0:T(8,128)(2,1)}, u32[]{:S(2)}) copy-start(bf16[128,256]{1,0:T(8,128)(2,1)} %param.14) | copy-start | bytes 196612
  358.9 52.6 %copy-start.7 = (bf16[2,8,16,864]{3,2,1,0:T(8,128)(2,1)S(1)}, bf16[2,8,16,864]{3,2,1,0:T(8,128)(2,1)}, u32[]{:S(2)}) copy-start(bf16[2,8,16,864]{3,2,1,0:T(8,128)(2,1)} %copy-done.6) | copy-start | bytes 1327108
  416.2 61.1 %copy-start.29 = (bf16[128,256]{1,0:T(8,128)(2,1)S(1)}, bf16[128,256]{1,0:T(8,128)(2,1)}, u32[]{:S(2)}) copy-start(bf16[128,256]{1,0:T(8,128)(2,1)} %reduce-scatter.2.cloned.1.call-done) | copy-start | bytes 196612
  476.0 35.6 %collective-permute-start.1 = (f32[2,1,3072]{2,1,0:T(1,128)S(1)}, f32[2,1,3072]{2,1,0:T(1,128)S(1)}, u32[]{:S(2)}, u32[]{:S(2)}) collective-permute-start(f32[2,1,3072]{2,1,0:T(1,128)S(1)} %reshape.781), channel_id=1, source_target_pairs={{1,0},{2,1},{3,2},{4,3},{5,4},{6,5},{7,6},{8,7},{9,8},{10,9},{11,1... | collective-permute-start | bytes 73736 | tf_op jit(solution)/shard_map/ppermute | solution.py:22
  (121 other events, 369.5 us)
Sparse Core Ops, SparseCore 0:
  20.0 42.5 all-gather.1
  354.1 56.3 reduce-scatter.1
  511.8 87.4 all-reduce.3
where the time goes:
time: 614 us; the launch traced here: 609 us
  waiting for transfers between devices  178 us (29%)
  matrix products  145 us (24%)
  other arithmetic  141 us (23%)
  local copies, waits for them, and re-layouts  91.7 us (15%)
  blocking collectives  32.5 us (5%)
  between operations  14.6 us (2%)
    psum x1, waiting for transfers between devices, per_device(): lax.psum(grad_conv.astype(jnp.bfloat16), 'rows').astype(jnp.float32)  86.6 us
    dot_general x48, matrix products, lookup_step(): jnp.einsum('yup,uvp->yvp', rows_hit.astype(jnp.float32), grid_now, precis...  86.3 us
    scatter-add x9, other arithmetic, scatter_taps(): summed = summed.at[:, row_tap:row_tap + 2 * out_rows:2, col_tap:col_tap +...  59.6 us
    dot_general x48, matrix products, lookup_step(): jnp.einsum('yup,yvp->uvp', rows_hit.astype(jnp.bfloat16), spread_cols.ast...  50.9 us
    reduce_scatter x1, waiting for transfers between devices, per_device(): lax.psum_scatter(spread_all.astype(jnp.bfloat16), 'rows', scatter_dimensi...  49.9 us
    all_gather x1, waiting for transfers between devices, per_device(): base_rows = lax.all_gather(second_map, 'rows', axis=0, tiled=True)  40.6 us
    psum x1, blocking collectives, per_device(): lax.psum(grad_bias.astype(jnp.bfloat16), 'rows').astype(jnp.float32)  32.5 us
    convert_element_type x48, local copies, waits for them, and re-layouts, lookup_step(): spread_cols.astype(jnp.bfloat16)  20.9 us
  transfers between devices with their start and end apart: 5, of which 4 were waited for; matrix products, arithmetic and copies ran while one was open for 2% of the time, Pallas kernels for 0%

commit v1 on v0

v1 whole, which is shorter than its diff:
```python
import functools

import jax
import jax.numpy as jnp
from jax import lax
from jax.experimental import pallas as pl
from jax.experimental.pallas import tpu as pltpu
from jax.sharding import PartitionSpec as P

C = 256
C1 = 128
C0 = 96
LEVELS = 4
SPAN = 9
ITERS = 12
RD = 8
WC = 16
LOOKS = 3888
PIX = RD * WC
WIN = 384
F32 = jnp.float32
BF16 = jnp.bfloat16
VMEM = pltpu.CompilerParams(vmem_limit_bytes=56 * 1024 * 1024)

def dot(a, b):
    return jnp.dot(a, b, preferred_element_type=F32)

def dot_nt(a, b):
    return lax.dot_general(a, b, (((1,), (1,)), ((), ())), preferred_element_type=F32)

def dot_tn(a, b):
    return lax.dot_general(a, b, (((0,), (0,)), ((), ())), preferred_element_type=F32)

def iota(shape, dim):
    return lax.broadcasted_iota(jnp.int32, shape, dim)

def pick(tile, index):
    return jnp.take_along_axis(tile, index, axis=0, mode="promise_in_bounds")

def pool_matrix(ny):
    parts = []
    for level in range(1, LEVELS):
        shape = (ny >> level, ny)
        hit = iota(shape, 0) == (iota(shape, 1) >> level)
        parts.append(jnp.where(hit, 0.25**level, 0.0))
    return jnp.concatenate(parts, axis=0).astype(BF16)

def spread_matrix(ny):
    parts = []
    for level in range(1, LEVELS):
        shape = (ny, ny >> level)
        hit = (iota(shape, 0) >> level) == iota(shape, 1)
        parts.append(jnp.where(hit, 0.25**level, 0.0))
    return jnp.concatenate(parts, axis=1).astype(BF16)

def lane_row(ref, step):
    return jnp.broadcast_to(ref[pl.ds(step, 1), :], (8, PIX))

def place_columns(source, offset, cols):
    values = list(source)
    bit = 1
    while bit < cols:
        taken = (offset & bit) != 0
        last = 2 * bit >= cols
        size = len(values)
        moved = []
        for k in range(size + bit):
            if last and not 4 <= k < cols + 4:
                moved.append(None)
                continue
            here = values[k] if k < size else None
            back = values[k - bit] if 0 <= k - bit < size else None
            here = jnp.zeros((8, PIX), F32) if here is None else here
            back = jnp.zeros((8, PIX), F32) if back is None else back
            moved.append(jnp.where(taken, back, here))
        values = moved
        bit *= 2
    return values[4 : cols + 4]

def window_columns(source, offset, cols):
    zero = jnp.zeros((8, PIX), F32)
    values = [zero] * 4 + list(source) + [zero] * 4
    bit = cols // 2
    while bit >= 1:
        taken = (offset & bit) != 0
        values = [jnp.where(taken, values[k + bit], values[k]) for k in range(bit + 8)]
        bit //= 2
    return values

def scatter_kernel(ny, row_ref, col_ref, cot_ref, w_ref, grad_ref, grad_t_ref, wv_ref, cot, *sums):
    sub = iota((8, PIX), 0)
    cot[...] = cot_ref[...].astype(F32)
    for level in range(LEVELS):
        sums[level][...] = jnp.zeros(sums[level].shape, F32)
    wv_ref[...] = jnp.zeros(wv_ref.shape, BF16)
    for tap in range(3):
        lanes = slice(tap * C1, tap * C1 + C1)
        rows = w_ref[tap * 288 : tap * 288 + 288, :]
        wv_ref[0, 0:192, lanes] = rows[96:288]
        wv_ref[1, 96:384, lanes] = rows
        wv_ref[2, 32:320, lanes] = rows

    def step(t, carry):
        row_all, col_all = lane_row(row_ref, t), lane_row(col_ref, t)
        for level in range(LEVELS):
            cols, tiles = WC >> level, ny >> (level + 3)
            base = t * 324 + level * 81
            start = (row_all >> level) + 4
            col = col_all >> level
            shift, tile_at = start & 7, start >> 3
            body = [cot[pl.ds(base + dx, 8, stride=SPAN), :] for dx in range(SPAN)]
            tail = [
                jnp.broadcast_to(cot[pl.ds(base + 72 + dx, 1), :], (8, PIX)) for dx in range(SPAN)
            ]
            body = place_columns(body, col, cols)
            tail = place_columns(tail, col, cols)
            index = (sub - shift) & 7
            upper, lower, edge = sub >= shift, sub < shift, sub == shift
            hits = [tile_at == k for k in range(tiles + 1)]
            for v in range(cols):
                turned = pick(body[v], index)
                high = jnp.where(upper, turned, 0.0)
                low = jnp.where(lower, turned, jnp.where(edge, tail[v], 0.0))
                for k in range(tiles):
                    term = jnp.where(hits[k + 1], high, jnp.where(hits[k], low, 0.0))
                    sums[level][v, 8 * k : 8 * k + 8, :] += term
        return carry

    lax.fori_loop(0, ITERS, step, 0)
    spread = spread_matrix(ny)
    for pair in range(WC // 2):
        stacked = jnp.concatenate(
            [sums[level][pair >> (level - 1)] for level in range(1, LEVELS)], axis=0
        ).astype(BF16)
        added = dot(spread, stacked)
        for v in (2 * pair, 2 * pair + 1):
            total = sums[0][v] + added
            grad_ref[v] = total.astype(BF16)
            grad_t_ref[:, v * ny : v * ny + ny] = total.T.astype(BF16)

def scatter(ny, target_row, target_col, cotangent, conv_weight):
    return pl.pallas_call(
        functools.partial(scatter_kernel, ny),
        out_shape=(
            jax.ShapeDtypeStruct((WC, ny, PIX), BF16),
            jax.ShapeDtypeStruct((PIX, WC * ny), BF16),
            jax.ShapeDtypeStruct((3, WIN, WIN), BF16),
        ),
        scratch_shapes=[pltpu.VMEM((LOOKS, PIX), F32)]
        + [pltpu.VMEM((WC >> level, ny >> level, PIX), F32) for level in range(LEVELS)],
        compiler_params=VMEM,
        cost_estimate=pl.CostEstimate(flops=10**9, bytes_accessed=4 * 10**6, transcendentals=0),
        name="scatter",
    )(target_row, target_col, cotangent, conv_weight)

def lookup_kernel(ny, row_ref, col_ref, hid_ref, first_ref, proj_ref, out_ref, looked, *volumes):
    sub = iota((8, PIX), 0)
    first, proj = first_ref[...], proj_ref[...]
    pool = pool_matrix(ny)
    zero = jnp.zeros((8, PIX), F32)
    for level in range(LEVELS):
        for v in range(WC >> level):
            volumes[level][v, 0:8, :] = zero
            volumes[level][v, 8 + (ny >> level) :, :] = zero
    held = [None] * LEVELS
    for v in range(WC):
        second = dot(hid_ref[v], proj).astype(BF16)
        volumes[0][v, 8 : 8 + ny, :] = dot_nt(second, first) * (1.0 / 16.0)
        pooled = dot(pool, second)
        at = 0
        for level in range(1, LEVELS):
            part = pooled[at : at + (ny >> level)]
            at += ny >> level
            held[level] = part if v % (1 << level) == 0 else held[level] + part
            if (v + 1) % (1 << level) == 0:
                volumes[level][v >> level, 8 : 8 + (ny >> level), :] = dot_nt(
                    held[level].astype(BF16), first
                ) * (1.0 / 16.0)

    def step(t, carry):
        row_all, col_all = lane_row(row_ref, t), lane_row(col_ref, t)
        for level in range(LEVELS):
            cols, tiles = WC >> level, ny >> (level + 3)
            base = t * 324 + level * 81
            start = (row_all >> level) + 4
            col = col_all >> level
            shift, tile_at = start & 7, start >> 3
            index = (sub + shift) & 7
            upper = sub >= shift
            beyond = tile_at >= tiles
            body, tail = [], []
            for v in range(cols):
                held = [volumes[level][v, 8 * k : 8 * k + 8, :] for k in range(tiles + 2)]
                for k in range(2):
                    held[k] = jnp.where(beyond, held[tiles + k], held[k])
                bit = tiles // 2
                while bit >= 1:
                    taken = (tile_at & bit) != 0
                    held = [jnp.where(taken, held[k + bit], held[k]) for k in range(bit + 1)]
                    bit //= 2
                body.append(pick(jnp.where(upper, held[0], held[1]), index))
                tail.append(pick(held[1], shift))
            body = window_columns(body, col, cols)
            tail = window_columns(tail, col, cols)
            for dx in range(SPAN):
                looked[pl.ds(base + dx, 8, stride=SPAN), :] = body[dx]
                looked[pl.ds(base + 72 + dx, 1), :] = tail[dx][0:1]
        return carry

    lax.fori_loop(0, ITERS, step, 0)
    out_ref[...] = looked[...].astype(BF16)

def lookup(ny, target_row, target_col, hid, first, proj_weight):
    return pl.pallas_call(
        functools.partial(lookup_kernel, ny),
        out_shape=jax.ShapeDtypeStruct((LOOKS, PIX), BF16),
        scratch_shapes=[pltpu.VMEM((LOOKS, PIX), F32)]
        + [pltpu.VMEM((WC >> level, (ny >> level) + 16, PIX), F32) for level in range(LEVELS)],
        compiler_params=VMEM,
        cost_estimate=pl.CostEstimate(flops=10**9, bytes_accessed=4 * 10**6, transcendentals=0),
        name="lookup",
    )(target_row, target_col, hid, first, proj_weight)


def reverse_bits(value, bits):
    total = 0
    for bit in range(bits):
        total = total | (((value >> bit) & 1) << (bits - 1 - bit))
    return total


def window_of(c):
    if c == 0:
        return 0, 0
    return (1, 192 * (c - 1)) if c % 2 else (2, 192 * c - 128)


def row_pick(me, count, bits, half, parity):
    shape = (count * RD, count * RD)
    row, at = iota(shape, 0), iota(shape, 1)
    place = reverse_bits((row >> 3) ^ me, bits) * (2 * RD) + 2 * (row & 7) + parity
    return jnp.where(place == at + half * count * RD, 1.0, 0.0).astype(BF16)


def own_pick(shift, parity):
    shape = (2 * RD, 2 * RD)
    row, at = iota(shape, 0) - shift, iota(shape, 1)
    hit = (row >= 0) & (row < RD) & (at == 2 * row + parity)
    return jnp.where(hit, 1.0, 0.0).astype(BF16)


def pixel_pick(transposed):
    a, b = iota((PIX, PIX), 0), iota((PIX, PIX), 1)
    a, b = (b, a) if transposed else (a, b)
    return jnp.where(a == (b & 7) * WC + (b >> 3), 1.0, 0.0).astype(BF16)


def taps_outer(weights):
    return jnp.concatenate([weights[:, 0:C1], weights[:, 2 * C1 : 3 * C1]], axis=1)


def main_kernel(
    count, bits, share, me_ref, near_ref, far_ref, own_ref, halo_ref, wv_ref, bias_ref, proj_ref,
    grad_ref, grad_t_ref, sums_ref, hid_ref, first_ref, first_grad_ref, even, odd, moved, pre0, wsum
):
    ny = count * RD
    ext = ny + 2 * RD
    me = me_ref[0]
    picks = [[row_pick(me, count, bits, half, parity) for half in range(2)] for parity in range(2)]
    own = own_ref[...]
    for parity, dest in ((0, even), (1, odd)):
        for j in range(8):
            lanes = slice(j * WIN, j * WIN + WIN)
            dest[0:ny, lanes] = (
                dot(picks[parity][0], near_ref[:, lanes]) + dot(picks[parity][1], far_ref[:, lanes])
            ).astype(BF16)
    even[ny:ext, :] = dot(own_pick(0, 0), own).astype(BF16)
    tail = dot(own_pick(1, 1), own)
    top = jnp.broadcast_to(halo_ref[...].astype(F32), tail.shape)
    odd[ny:ext, :] = jnp.where(iota(tail.shape, 0) == 0, top, tail).astype(BF16)

    bias = bias_ref[...]
    moved[0:8, :] = jnp.zeros((8, 2 * C1), F32)
    for c in range(WC):
        variant, start = window_of(c)
        lanes = slice(start, start + WIN)
        inner = dot(even[:, lanes], wv_ref[variant, :, C1 : 2 * C1])
        outer = dot(odd[:, lanes], taps_outer(wv_ref[variant]))
        moved[8 : 8 + ext, :] = outer
        preact = inner[0:ny] + outer[0:ny, C1:] + moved[7 : 7 + ny, 0:C1] + bias
        hid_ref[c] = jnp.maximum(preact, 0.0).astype(BF16)
        pre0[8 * c : 8 * c + 8, :] = (
            inner[ny : ny + 8]
            + outer[ny : ny + 8, 0:C1]
            + moved[8 + ny + 1 : 8 + ny + 9, C1:]
            + bias
        )

    proj = proj_ref[...]
    hid0 = dot(pixel_pick(False), jnp.maximum(pre0[...], 0.0).astype(BF16)).astype(BF16)
    first = dot(hid0, proj).astype(BF16)
    first_ref[...] = first
    mixed = (dot(grad_t_ref[...], hid_ref[...].reshape(WC * ny, C1)) * (1.0 / 16.0)).astype(BF16)
    grad_first = dot(mixed, proj).astype(BF16)
    grad_proj = dot_tn(mixed, first) + dot_tn(hid0, grad_first)
    pre_grad0 = dot(pixel_pick(True), dot_nt(grad_first, proj).astype(BF16))
    pre_grad0 = jnp.where(pre0[...] > 0.0, pre_grad0, 0.0)
    first_grad_ref[...] = pre_grad0.astype(BF16)
    pre0[...] = pre_grad0
    fold = (dot_nt(first, proj) * (1.0 / 16.0)).astype(BF16)

    bias_sum = jnp.sum(pre_grad0, axis=0, keepdims=True)
    totals_in, totals_out = [None] * 3, [None] * 3
    zeros8 = jnp.zeros((8, C1), F32)
    previous = None
    for c in range(WC):
        variant, start = window_of(c)
        lanes = slice(start, start + WIN)
        grad = jnp.where(hid_ref[c].astype(F32) > 0.0, dot(grad_ref[c], fold), 0.0)
        own_grad = pre0[8 * c : 8 * c + 8, :]
        bias_sum = bias_sum + jnp.sum(grad, axis=0, keepdims=True)
        moved[0:ny, 0:C1] = grad
        moved[ny : ny + 8, 0:C1] = zeros8
        shifted_grad = moved[1 : 1 + ny, 0:C1]
        moved[ny : ny + 8, C1:] = zeros8
        moved[ny + 8 : ny + 16, C1:] = zeros8
        moved[ny + 1 : ny + 9, C1:] = own_grad
        late = moved[ny : ny + 16, C1:]
        inner = jnp.concatenate([grad, own_grad, zeros8], axis=0).astype(BF16)
        outer = jnp.concatenate(
            [
                jnp.concatenate([shifted_grad, own_grad, zeros8], axis=0),
                jnp.concatenate([grad, late], axis=0),
            ],
            axis=1,
        ).astype(BF16)
        part_in = dot_tn(inner, even[:, lanes])
        part_out = dot_tn(outer, odd[:, lanes])
        if totals_in[variant] is None:
            totals_in[variant], totals_out[variant] = part_in, part_out
        else:
            totals_in[variant] = totals_in[variant] + part_in
            totals_out[variant] = totals_out[variant] + part_out
        if c % 2:
            for d in range(count):
                pair = [g[8 * d : 8 * d + 8] for g in (previous, grad)]
                sums_ref[reverse_bits(d, bits), 8 * (c - 1) : 8 * (c + 1), :] = jnp.concatenate(
                    pair, axis=0
                ).astype(BF16)
        previous = grad

    wsum[9 * C0 + 2 * C1 :, :] = jnp.zeros((count * share - 9 * C0 - 2 * C1, C1), F32)
    for tap in range(3):
        if tap == 1:
            parts = totals_in
        else:
            at = 0 if tap == 0 else C1
            parts = [t[at : at + C1] for t in totals_out]
        parts = [p.T for p in parts]
        whole = parts[1][96:384] + parts[2][32:320]
        wsum[tap * 288 : tap * 288 + 96, :] = whole[0:96]
        wsum[tap * 288 + 96 : tap * 288 + 288, :] = whole[96:288] + parts[0][0:192]
    wsum[9 * C0 : 9 * C0 + C1, :] = grad_proj[:, 0:C1]
    wsum[9 * C0 + C1 : 9 * C0 + 2 * C1, :] = grad_proj[:, C1:]
    wsum[9 * C0 + 2 * C1 : 9 * C0 + 2 * C1 + 1, :] = bias_sum
    for p in range(count):
        sums_ref[p, PIX : PIX + share, :] = wsum[share * p : share * p + share, :].astype(BF16)


def whole(*shape):
    return pl.BlockSpec(shape, lambda: (0,) * len(shape))


def main(count, bits, share, me, near, far, own, halo, wv, bias, proj_weight, grad, grad_t):
    ny = count * RD
    ext = ny + 2 * RD
    vmem = pl.BlockSpec(memory_space=pltpu.VMEM)
    return pl.pallas_call(
        functools.partial(main_kernel, count, bits, share),
        in_specs=[pl.BlockSpec(memory_space=pltpu.SMEM)] + [vmem] * 9,
        out_shape=(
            jax.ShapeDtypeStruct((count, PIX + share, C1), BF16),
            jax.ShapeDtypeStruct((WC, ny, C1), BF16),
            jax.ShapeDtypeStruct((PIX, C), BF16),
            jax.ShapeDtypeStruct((PIX, C1), BF16),
        ),
        scratch_shapes=[
            pltpu.VMEM((ext, 2 * WC * C0), BF16),
            pltpu.VMEM((ext, 2 * WC * C0), BF16),
            pltpu.VMEM((ext + 16, 2 * C1), F32),
            pltpu.VMEM((PIX, C1), F32),
            pltpu.VMEM((count * share, C1), F32),
        ],
        compiler_params=VMEM,
        cost_estimate=pl.CostEstimate(flops=4 * 10**9, bytes_accessed=6 * 10**6, transcendentals=0),
        name="features",
    )(me, near, far, own, halo, wv, bias, proj_weight, grad, grad_t)


def input_kernel(first_ref, second_ref, border_ref, wv_ref, out_ref, sides, full):
    last = iota((8, C1), 0) == 7
    border = border_ref[...].astype(F32)
    grads = [first_ref[...].astype(F32), second_ref[...].astype(F32)]

    def stacked(columns):
        here, both = [], []
        for c in columns:
            for f in range(2):
                own = grads[f][8 * c : 8 * c + 8]
                below = jnp.broadcast_to(border[f * WC + c : f * WC + c + 1], (8, C1))
                here.append(own)
                both.append(
                    jnp.concatenate([own, jnp.where(last, below, pltpu.roll(own, 7, 0))], axis=1)
                )
        return jnp.concatenate(here, axis=0).astype(BF16), jnp.concatenate(both, axis=0).astype(BF16)

    def spread(columns, variant):
        here, both = stacked(columns)
        weights = wv_ref[variant]
        outer = jnp.concatenate([weights[:, 2 * C1 : 3 * C1], weights[:, 0:C1]], axis=1)
        return dot_nt(here, weights[:, C1 : 2 * C1]), dot_nt(both, outer)

    odd = spread(range(1, WC, 2), 1)
    even = spread(range(2, WC, 2), 2)
    edge = spread([0], 0)
    for parity in range(2):
        for q in range(8):
            sides[parity, :, q * WIN : q * WIN + WIN] = odd[parity][16 * q : 16 * q + 16]
        for q in range(1, 8):
            sides[parity, :, q * WIN - 128 : q * WIN + 256] += even[parity][16 * q - 16 : 16 * q]
        sides[parity, :, 0:WIN] += edge[parity]
        for f in range(2):
            for j in range(2 * WC * C0 // 128):
                lanes = slice(128 * j, 128 * j + 128)
                full[f, j, pl.ds(parity, 8, stride=2), :] = sides[parity, 8 * f : 8 * f + 8, lanes]
    for f in range(2):
        for j in range(2 * WC * C0 // 128):
            out_ref[f, :, 128 * j : 128 * j + 128] = full[f, j].astype(BF16)


def input_grad(first_grad, second_grad, border, wv):
    return pl.pallas_call(
        input_kernel,
        out_shape=jax.ShapeDtypeStruct((2, 2 * RD, 2 * WC * C0), BF16),
        scratch_shapes=[
            pltpu.VMEM((2, 2 * RD, 2 * WC * C0), F32),
            pltpu.VMEM((2, 2 * WC * C0 // 128, 2 * RD, 128), F32),
        ],
        compiler_params=VMEM,
        cost_estimate=pl.CostEstimate(flops=10**8, bytes_accessed=10**6, transcendentals=0),
        name="input_grad",
    )(first_grad, second_grad, border, wv)


def final_kernel(count, bits, share, me_ref, near_ref, far_ref, conv_ref, bias_ref, proj_ref, wsum):
    turned = reverse_bits(me_ref[0], bits)
    for half, ref in ((0, near_ref), (1, far_ref)):
        for j in range(count // 2):
            at = (turned ^ (half * (count // 2) + j)) * share
            wsum[pl.ds(pl.multiple_of(at, 16), share), :] = ref[j].astype(F32)
    conv_ref[...] = wsum[0 : 9 * C0, :]
    proj_ref[:, 0:C1] = wsum[9 * C0 : 9 * C0 + C1, :]
    proj_ref[:, C1:] = wsum[9 * C0 + C1 : 9 * C0 + 2 * C1, :]
    bias_ref[...] = wsum[9 * C0 + 2 * C1 : 9 * C0 + 2 * C1 + 1, :]


def final(count, bits, share, me, near, far):
    vmem = pl.BlockSpec(memory_space=pltpu.VMEM)
    return pl.pallas_call(
        functools.partial(final_kernel, count, bits, share),
        in_specs=[pl.BlockSpec(memory_space=pltpu.SMEM), vmem, vmem],
        out_shape=(
            jax.ShapeDtypeStruct((9 * C0, C1), F32),
            jax.ShapeDtypeStruct((1, C1), F32),
            jax.ShapeDtypeStruct((C1, C), F32),
        ),
        scratch_shapes=[pltpu.VMEM((count * share, C1), F32)],
        compiler_params=VMEM,
        name="weight_grads",
    )(me, near, far)


def swap(value, bit, count):
    return lax.ppermute(value, "rows", [(i, i ^ bit) for i in range(count)])


def per_device(frames, conv_weight, conv_bias, proj_weight, target_row, target_col, cotangent):
    count = lax.axis_size("rows")
    bits = count.bit_length() - 1
    ny = count * RD
    me = lax.axis_index("rows").astype(jnp.int32)
    me_word = me.reshape(1)
    share = -(-(9 * C0 + 2 * C1 + 1) // (16 * count)) * 16

    halo = lax.ppermute(frames[0, 2 * RD - 1 :], "rows", [(i, i + 1) for i in range(count - 1)])
    near = frames[1]
    far = None
    for bit in reversed(range(bits)):
        if far is not None:
            near = jnp.concatenate([near, far], axis=0)
        far = swap(near, 1 << bit, count)
    grad, grad_t, wv = scatter(ny, target_row, target_col, cotangent, conv_weight)
    sums, hid, first, first_grad = main(
        count, bits, share, me_word, near, far, frames[0], halo, wv,
        conv_bias.reshape(1, C1), proj_weight, grad, grad_t,
    )
    for bit in range(bits):
        half = sums.shape[0] // 2
        mine = (me >> bit) & 1
        kept = lax.dynamic_slice_in_dim(sums, mine * half, half, 0)
        sent = lax.dynamic_slice_in_dim(sums, (1 - mine) * half, half, 0)
        sums = (kept.astype(F32) + swap(sent, 1 << bit, count).astype(F32)).astype(BF16)
    second_grad = sums[0, :PIX]
    tops = jnp.concatenate([first_grad, second_grad], axis=0).reshape(2 * WC, RD, C1)[:, 0]
    border = lax.ppermute(tops, "rows", [(i + 1, i) for i in range(count - 1)])
    near = sums[:, PIX:]
    far = None
    for bit in reversed(range(bits)):
        if far is not None:
            near = jnp.concatenate([near, far], axis=0)
        far = swap(near, 1 << bit, count)
    grad_conv, grad_bias, grad_proj = final(count, bits, share, me_word, near, far)
    grad_input = input_grad(first_grad, second_grad, border, wv)
    lookups = lookup(ny, target_row, target_col, hid, first, proj_weight)
    return lookups, grad_input, grad_conv, grad_bias.reshape(C1), grad_proj


def solution(mesh):
    split = P(None, ("pairs", "rows"))
    return jax.shard_map(
        per_device,
        mesh=mesh,
        in_specs=(P(None, ("pairs", "rows"), None), P(), P(), P(), split, split, split),
        out_specs=(
            split,
            P(None, ("pairs", "rows"), None),
            P("pairs", None),
            P("pairs"),
            P("pairs", None),
        ),
        check_vma=False,
    )
```

time: 614 us -> 99.4 us (0.16)
  matrix products: 145 us -> 0 us
  waiting for transfers between devices: 178 us -> 37.3 us
  other arithmetic: 141 us -> 0.36 us
  local copies, waits for them, and re-layouts: 91.7 us -> 5.87 us
  blocking collectives: 32.5 us -> 0 us
  Pallas kernels: 0 us -> 27.7 us
  starting transfers between devices: 3.77 us -> 25.8 us
  between operations: 14.6 us -> 0.83 us
    dot_general x105 -> x0, matrix products: 145 us -> none  [the longest x48 86.3 us: lookup_step(): jnp.einsum('yup,uvp->yvp', rows_hit.astype(jnp.float32), grid_now, precis...]
    psum x1 -> x0, waiting for transfers between devices: 86.6 us -> none  [per_device(): lax.psum(grad_conv.astype(jnp.bfloat16), 'rows').astype(jnp.float32)]
    scatter-add x9 -> x0, other arithmetic: 59.6 us -> none  [scatter_taps(): summed = summed.at[:, row_tap:row_tap + 2 * out_rows:2, col_tap:col_tap +...]
    reduce_scatter x1 -> x0, waiting for transfers between devices: 49.9 us -> none  [per_device(): lax.psum_scatter(spread_all.astype(jnp.bfloat16), 'rows', scatter_dimensi...]
    all_gather x1 -> x0, waiting for transfers between devices: 40.6 us -> none  [per_device(): base_rows = lax.all_gather(second_map, 'rows', axis=0, tiled=True)]
    ppermute x2 -> x14, waiting for transfers between devices: 0.83 us -> 37.3 us  [the longest x12 37.3 us: swap(): return lax.ppermute(value, 'rows', [(i, i ^ bit) for i in range(count)])]
    psum x1 -> x0, blocking collectives: 32.5 us -> none  [per_device(): lax.psum(grad_bias.astype(jnp.bfloat16), 'rows').astype(jnp.float32)]
    convert_element_type x71 -> x4, other arithmetic: 31.7 us -> 0.23 us  [per_device(): (kept.astype(F32) + swap(sent, 1 << bit, count).astype(F32)).astype(BF16)]
  transfers between devices with their start and end apart: 5 -> 14, of which waited for: 4 -> 10; matrix products, arithmetic and copies ran while one was open for 2% -> 1% of each run, Pallas kernels for 0% -> 15%
where the time goes in v1:
time: 99.4 us; the launch traced here: 97.9 us
  waiting for transfers between devices  37.3 us (38%)
  Pallas kernels  27.7 us (28%)
  starting transfers between devices  25.8 us (26%)
  local copies, waits for them, and re-layouts  5.87 us (6%)
    ppermute x12, waiting for transfers between devices, swap(): return lax.ppermute(value, 'rows', [(i, i ^ bit) for i in range(count)])  37.3 us
    ppermute x12, starting transfers between devices, swap(): return lax.ppermute(value, 'rows', [(i, i ^ bit) for i in range(count)])  22.1 us
    pallas_call x1, Pallas kernels, main(): pl.pallas_call(functools.partial(main_kernel, count, bits, share), in_spe...  10.8 us
    pallas_call x1, Pallas kernels, lookup(): pl.pallas_call(functools.partial(lookup_kernel, ny), out_shape=jax.ShapeD...  6.78 us
    pallas_call x1, Pallas kernels, scatter(): pl.pallas_call(functools.partial(scatter_kernel, ny), out_shape=(jax.Shap...  5.96 us
    ppermute x1, starting transfers between devices, per_device(): lax.ppermute(frames[0, 2 * RD - 1:], 'rows', [(i, i + 1) for i in range(c...  2.33 us
    pallas_call x1, Pallas kernels, input_grad(): pl.pallas_call(input_kernel, out_shape=jax.ShapeDtypeStruct((2, 2 * RD, 2...  2.32 us
    unnamed x19, local copies, waits for them, and re-layouts  2.2 us
  transfers between devices with their start and end apart: 14, of which 10 were waited for; matrix products, arithmetic and copies ran while one was open for 1% of the time, Pallas kernels for 15%

profile of v1, /device:TPU:0, one launch (start us, length us, event | category | flops | bytes accessed | tf_op | source)
XLA Modules:
  0.0 97.9 jit_solution(13091529187998738855)
XLA Ops:
  0.6 1.6 %slice_bitcast_fusion = (bf16[16,3072]{1,0:T(8,128)(2,1)}, bf16[16,3072]{1,0:T(8,128)(2,1)S(1)}) fusion(bf16[2,16,3072]{2,1,0:T(8,128)(2,1)} %param.7), kind=kLoop, calls=%fused_computation.8 | loop fusion | bytes 393216 | tf_op jit(solution)/shard_map/squeeze | solution.py:504
  2.2 4.0 %collective-permute-start = (bf16[16,3072]{1,0:T(8,128)(2,1)S(1)}, bf16[16,3072]{1,0:T(8,128)(2,1)S(1)}, u32[]{:S(2)}, u32[]{:S(2)}) collective-permute-start(bf16[16,3072]{1,0:T(8,128)(2,1)S(1)} %get-tuple-element.26), channel_id=1, source_target_pairs={{0,8},{1,9},{2,10},{3,11},{4,12},{5,13},{6,14},{7,15},{8,0},{9,1},... | collective-permute-start | bytes 294920 | tf_op jit(solution)/shard_map/ppermute | solution.py:484
  6.3 4.9 %collective-permute-done = bf16[16,3072]{1,0:T(8,128)(2,1)S(1)} collective-permute-done((bf16[16,3072]{1,0:T(8,128)(2,1)S(1)}, bf16[16,3072]{1,0:T(8,128)(2,1)S(1)}, u32[]{:S(2)}, u32[]{:S(2)}) %collective-permute-start) | collective-permute-done | bytes 98336 | tf_op jit(solution)/shard_map/ppermute | solution.py:484
  11.2 0.8 collective-permute-start.1
  12.0 5.4 %collective-permute-done.1 = bf16[32,3072]{1,0:T(8,128)(2,1)S(1)} collective-permute-done((bf16[32,3072]{1,0:T(8,128)(2,1)S(1)}, bf16[32,3072]{1,0:T(8,128)(2,1)S(1)}, u32[]{:S(2)}, u32[]{:S(2)}) %collective-permute-start.1) | collective-permute-done | bytes 196640 | tf_op jit(solution)/shard_map/ppermute | solution.py:484
  17.4 1.3 %collective-permute-start.2 = (bf16[64,3072]{1,0:T(8,128)(2,1)S(1)}, bf16[64,3072]{1,0:T(8,128)(2,1)S(1)}, u32[]{:S(2)}, u32[]{:S(2)}) collective-permute-start(bf16[64,3072]{1,0:T(8,128)(2,1)S(1)} %pad_maximum_fusion.1), channel_id=1, source_target_pairs={{0,2},{1,3},{2,0},{3,1},{4,6},{5,7},{6,4},{7,5},{8,10},{9,11},{10,... | collective-permute-start | bytes 1179656 | tf_op jit(solution)/shard_map/ppermute | solution.py:484
  18.7 8.1 %collective-permute-done.2 = bf16[64,3072]{1,0:T(8,128)(2,1)S(1)} collective-permute-done((bf16[64,3072]{1,0:T(8,128)(2,1)S(1)}, bf16[64,3072]{1,0:T(8,128)(2,1)S(1)}, u32[]{:S(2)}, u32[]{:S(2)}) %collective-permute-start.2) | collective-permute-done | bytes 393248 | tf_op jit(solution)/shard_map/ppermute | solution.py:484
  27.0 0.9 slice_bitcast_fusion.3
  27.8 2.3 %collective-permute-start.4 = (bf16[1,3072]{1,0:T(2,128)(2,1)S(1)}, bf16[1,3072]{1,0:T(2,128)(2,1)S(1)}, u32[]{:S(2)}, u32[]{:S(2)}) collective-permute-start(bf16[1,3072]{1,0:T(2,128)(2,1)S(1)} %slice_bitcast_fusion.3), channel_id=1, source_target_pairs={{0,1},{1,2},{2,3},{3,4},{4,5},{5,6},{6,7},{7,8},{8,9},{9,10},{10,1... | collective-permute-start | bytes 18440 | tf_op jit(solution)/shard_map/ppermute | solution.py:495
  30.2 6.0 %scatter.1 = (bf16[16,128,128]{2,1,0:T(8,128)(2,1)}, bf16[128,2048]{1,0:T(8,128)(2,1)}, bf16[3,384,384]{2,1,0:T(8,128)(2,1)}) custom-call(s32[12,128]{1,0:T(8,128)} %row_ref.3, s32[12,128]{1,0:T(8,128)} %col_ref.3, bf16[3888,128]{1,0:T(8,128)(2,1)} %cot_ref.1, bf16[864,128]{1,0:T(8,128)(2,1)} %w_ref.1), custom_call_target="tpu_custom_call" | custom-call | flops 1000000000 | bytes 4000000 | tf_op jit(solution)/shard_map/scatter/pallas_call | solution.py:142
  37.1 10.8 %features.1 = (bf16[16,208,128]{2,1,0:T(8,128)(2,1)}, bf16[16,128,128]{2,1,0:T(8,128)(2,1)}, bf16[128,256]{1,0:T(8,128)(2,1)}, bf16[128,128]{1,0:T(8,128)(2,1)}) custom-call(s32[1]{0:T(128)} %bitcast.me_ref, bf16[128,3072]{1,0:T(8,128)(2,1)} %copy-done.1, bf16[128,3072]{1,0:T(8,128)(2,1)} %copy-done.7, bf16[16,3072]{1,0:T(8,128)(2,1)} %get-tuple-element.25.own_ref, ...), custom_call_target="tpu_custom_call" | custom-call | flops 4000000000 | bytes 6000000 | tf_op jit(solution)/shard_map/features/pallas_call | solution.py:378
  47.9 1.1 %constant_dynamic-slice_fusion.3 = bf16[8,208,128]{2,1,0:T(8,128)(2,1)S(1)} fusion(bf16[16,208,128]{2,1,0:T(8,128)(2,1)} %get-tuple-element.21, s32[]{:T(128)S(6)} %select_n.25), kind=kLoop, calls=%fused_computation.19 | loop fusion | bytes 851972 | tf_op jit(solution)/shard_map/dynamic_slice | solution.py:511
  49.0 1.1 %collective-permute-start.5 = (bf16[8,208,128]{2,1,0:T(8,128)(2,1)S(1)}, bf16[8,208,128]{2,1,0:T(8,128)(2,1)S(1)}, u32[]{:S(2)}, u32[]{:S(2)}) collective-permute-start(bf16[8,208,128]{2,1,0:T(8,128)(2,1)S(1)} %constant_dynamic-slice_fusion.3), channel_id=1, source_target_pairs={{0,1},{1,0},{2,3},{3,2},{4,5},{5,4},{6,7},{7,6},{8,9},{9,8},{10,11... | collective-permute-start | bytes 1277960 | tf_op jit(solution)/shard_map/ppermute | solution.py:484
  50.1 1.4 %collective-permute-done.5 = bf16[8,208,128]{2,1,0:T(8,128)(2,1)S(1)} collective-permute-done((bf16[8,208,128]{2,1,0:T(8,128)(2,1)S(1)}, bf16[8,208,128]{2,1,0:T(8,128)(2,1)S(1)}, u32[]{:S(2)}, u32[]{:S(2)}) %collective-permute-start.5) | collective-permute-done | bytes 426016 | tf_op jit(solution)/shard_map/ppermute | solution.py:484
  51.6 2.5 %collective-permute-start.6 = (bf16[4,208,128]{2,1,0:T(8,128)(2,1)S(1)}, bf16[4,208,128]{2,1,0:T(8,128)(2,1)S(1)}, u32[]{:S(2)}, u32[]{:S(2)}) collective-permute-start(bf16[4,208,128]{2,1,0:T(8,128)(2,1)S(1)} %constant_dynamic-slice_fusion.2), channel_id=1, source_target_pairs={{0,2},{1,3},{2,0},{3,1},{4,6},{5,7},{6,4},{7,5},{8,10},{9,11},{10,... | collective-permute-start | bytes 638984 | tf_op jit(solution)/shard_map/ppermute | solution.py:484
  54.1 5.8 %collective-permute-done.6 = bf16[4,208,128]{2,1,0:T(8,128)(2,1)S(1)} collective-permute-done((bf16[4,208,128]{2,1,0:T(8,128)(2,1)S(1)}, bf16[4,208,128]{2,1,0:T(8,128)(2,1)S(1)}, u32[]{:S(2)}, u32[]{:S(2)}) %collective-permute-start.6) | collective-permute-done | bytes 213024 | tf_op jit(solution)/shard_map/ppermute | solution.py:484
  60.0 2.6 %collective-permute-start.7 = (bf16[2,208,128]{2,1,0:T(8,128)(2,1)S(1)}, bf16[2,208,128]{2,1,0:T(8,128)(2,1)S(1)}, u32[]{:S(2)}, u32[]{:S(2)}) collective-permute-start(bf16[2,208,128]{2,1,0:T(8,128)(2,1)S(1)} %constant_dynamic-slice_fusion.1), channel_id=1, source_target_pairs={{0,4},{1,5},{2,6},{3,7},{4,0},{5,1},{6,2},{7,3},{8,12},{9,13},{10,... | collective-permute-start | bytes 319496 | tf_op jit(solution)/shard_map/ppermute | solution.py:484
  62.6 2.9 %collective-permute-done.7 = bf16[2,208,128]{2,1,0:T(8,128)(2,1)S(1)} collective-permute-done((bf16[2,208,128]{2,1,0:T(8,128)(2,1)S(1)}, bf16[2,208,128]{2,1,0:T(8,128)(2,1)S(1)}, u32[]{:S(2)}, u32[]{:S(2)}) %collective-permute-start.7) | collective-permute-done | bytes 106528 | tf_op jit(solution)/shard_map/ppermute | solution.py:484
  65.6 3.1 %collective-permute-start.8 = (bf16[1,208,128]{2,1,0:T(8,128)(2,1)S(1)}, bf16[1,208,128]{2,1,0:T(8,128)(2,1)S(1)}, u32[]{:S(2)}, u32[]{:S(2)}) collective-permute-start(bf16[1,208,128]{2,1,0:T(8,128)(2,1)S(1)} %constant_dynamic-slice_fusion), channel_id=1, source_target_pairs={{0,8},{1,9},{2,10},{3,11},{4,12},{5,13},{6,14},{7,15},{8,0},{9,1},... | collective-permute-start | bytes 159752 | tf_op jit(solution)/shard_map/ppermute | solution.py:484
  68.6 2.1 %collective-permute-done.8 = bf16[1,208,128]{2,1,0:T(8,128)(2,1)S(1)} collective-permute-done((bf16[1,208,128]{2,1,0:T(8,128)(2,1)S(1)}, bf16[1,208,128]{2,1,0:T(8,128)(2,1)S(1)}, u32[]{:S(2)}, u32[]{:S(2)}) %collective-permute-start.8) | collective-permute-done | bytes 53280 | tf_op jit(solution)/shard_map/ppermute | solution.py:484
  70.8 3.1 %collective-permute-start.10 = (bf16[1,80,128]{2,1,0:T(8,128)(2,1)S(1)}, bf16[1,80,128]{2,1,0:T(8,128)(2,1)S(1)}, u32[]{:S(2)}, u32[]{:S(2)}) collective-permute-start(bf16[1,80,128]{2,1,0:T(8,128)(2,1)S(1)} %slice.26), channel_id=1, source_target_pairs={{0,8},{1,9},{2,10},{3,11},{4,12},{5,13},{6,14},{7,15},{8,0},{9,1},... | collective-permute-start | bytes 61448 | tf_op jit(solution)/shard_map/ppermute | solution.py:484
  73.9 1.8 %collective-permute-done.10 = bf16[1,80,128]{2,1,0:T(8,128)(2,1)S(1)} collective-permute-done((bf16[1,80,128]{2,1,0:T(8,128)(2,1)S(1)}, bf16[1,80,128]{2,1,0:T(8,128)(2,1)S(1)}, u32[]{:S(2)}, u32[]{:S(2)}) %collective-permute-start.10) | collective-permute-done | bytes 20512 | tf_op jit(solution)/shard_map/ppermute | solution.py:484
  75.7 2.0 %collective-permute-start.11 = (bf16[2,80,128]{2,1,0:T(8,128)(2,1)S(1)}, bf16[2,80,128]{2,1,0:T(8,128)(2,1)S(1)}, u32[]{:S(2)}, u32[]{:S(2)}) collective-permute-start(bf16[2,80,128]{2,1,0:T(8,128)(2,1)S(1)} %pad_maximum_fusion.5), channel_id=1, source_target_pairs={{0,4},{1,5},{2,6},{3,7},{4,0},{5,1},{6,2},{7,3},{8,12},{9,13},{10,... | collective-permute-start | bytes 122888 | tf_op jit(solution)/shard_map/ppermute | solution.py:484
  77.7 2.0 %collective-permute-done.11 = bf16[2,80,128]{2,1,0:T(8,128)(2,1)S(1)} collective-permute-done((bf16[2,80,128]{2,1,0:T(8,128)(2,1)S(1)}, bf16[2,80,128]{2,1,0:T(8,128)(2,1)S(1)}, u32[]{:S(2)}, u32[]{:S(2)}) %collective-permute-start.11) | collective-permute-done | bytes 40992 | tf_op jit(solution)/shard_map/ppermute | solution.py:484
  79.7 1.6 %collective-permute-start.12 = (bf16[4,80,128]{2,1,0:T(8,128)(2,1)S(1)}, bf16[4,80,128]{2,1,0:T(8,128)(2,1)S(1)}, u32[]{:S(2)}, u32[]{:S(2)}) collective-permute-start(bf16[4,80,128]{2,1,0:T(8,128)(2,1)S(1)} %pad_maximum_fusion.4), channel_id=1, source_target_pairs={{0,2},{1,3},{2,0},{3,1},{4,6},{5,7},{6,4},{7,5},{8,10},{9,11},{10,... | collective-permute-start | bytes 245768 | tf_op jit(solution)/shard_map/ppermute | solution.py:484
  81.3 2.9 %collective-permute-done.12 = bf16[4,80,128]{2,1,0:T(8,128)(2,1)S(1)} collective-permute-done((bf16[4,80,128]{2,1,0:T(8,128)(2,1)S(1)}, bf16[4,80,128]{2,1,0:T(8,128)(2,1)S(1)}, u32[]{:S(2)}, u32[]{:S(2)}) %collective-permute-start.12) | collective-permute-done | bytes 81952 | tf_op jit(solution)/shard_map/ppermute | solution.py:484
  84.3 1.3 %collective-permute-start.9 = (bf16[32,128]{1,0:T(8,128)(2,1)S(1)}, bf16[32,128]{1,0:T(8,128)(2,1)S(1)}, u32[]{:S(2)}, u32[]{:S(2)}) collective-permute-start(bf16[32,128]{1,0:T(8,128)(2,1)S(1)} %bitcast.16), channel_id=1, source_target_pairs={{1,0},{2,1},{3,2},{4,3},{5,4},{6,5},{7,6},{8,7},{9,8},{10,9},{11,1... | collective-permute-start | bytes 24584 | tf_op jit(solution)/shard_map/ppermute | solution.py:515
  85.6 6.8 %lookup.1 = bf16[3888,128]{1,0:T(8,128)(2,1)} custom-call(s32[12,128]{1,0:T(8,128)} %row_ref.3, s32[12,128]{1,0:T(8,128)} %col_ref.3, bf16[16,128,128]{2,1,0:T(8,128)(2,1)} %get-tuple-element.18.hid_ref, bf16[128,256]{1,0:T(8,128)(2,1)} %get-tuple-element.19.first_ref, bf16[128,256]{1,0:T(8,128)(2,1)} %proj_ref.3), custom_call_target="tpu_custom_call" | custom-call | flops 1000000000 | bytes 4000000 | tf_op jit(solution)/shard_map/lookup/pallas_call | solution.py:214
  92.5 0.6 copy-done.6
  93.0 2.3 %input_grad.1 = bf16[2,16,3072]{2,1,0:T(8,128)(2,1)} custom-call(bf16[128,128]{1,0:T(8,128)(2,1)} %get-tuple-element.20.first_ref, bf16[128,128]{1,0:T(8,128)(2,1)} %copy-done.3, bf16[32,128]{1,0:T(8,128)(2,1)} %copy-done.6, bf16[3,384,384]{2,1,0:T(8,128)(2,1)} %get-tuple-element.15.wv_ref), custom_call_target="tpu_custom_call" | custom-call | flops 100000000 | bytes 1000000 | tf_op jit(solution)/shard_map/input_grad/pallas_call | solution.py:442
  95.4 0.7 copy-done.4
  96.0 1.9 %weight_grads.1 = (f32[864,128]{1,0:T(8,128)}, f32[1,128]{1,0:T(1,128)}, f32[128,256]{1,0:T(8,128)}) custom-call(s32[1]{0:T(128)} %bitcast.me_ref, bf16[8,80,128]{2,1,0:T(8,128)(2,1)} %copy-done.2, bf16[8,80,128]{2,1,0:T(8,128)(2,1)} %copy-done.4), custom_call_target="tpu_custom_call" | custom-call | tf_op jit(solution)/shard_map/weight_grads/pallas_call | solution.py:469
  (40 shorter events, 1.5 us)
Async XLA Ops:
  2.2 8.9 %collective-permute-start = (bf16[16,3072]{1,0:T(8,128)(2,1)S(1)}, bf16[16,3072]{1,0:T(8,128)(2,1)S(1)}, u32[]{:S(2)}, u32[]{:S(2)}) collective-permute-start(bf16[16,3072]{1,0:T(8,128)(2,1)S(1)} %get-tuple-element.26), channel_id=1, source_target_pairs={{0,8},{1,9},{2,10},{3,11},{4,12},{5,13},{6,14},{7,15},{8,0},{9,1},... | collective-permute-start | bytes 294920 | tf_op jit(solution)/shard_map/ppermute | solution.py:484
  11.2 6.2 %collective-permute-start.1 = (bf16[32,3072]{1,0:T(8,128)(2,1)S(1)}, bf16[32,3072]{1,0:T(8,128)(2,1)S(1)}, u32[]{:S(2)}, u32[]{:S(2)}) collective-permute-start(bf16[32,3072]{1,0:T(8,128)(2,1)S(1)} %pad_maximum_fusion.2), channel_id=1, source_target_pairs={{0,4},{1,5},{2,6},{3,7},{4,0},{5,1},{6,2},{7,3},{8,12},{9,13},{10,... | collective-permute-start | bytes 589832 | tf_op jit(solution)/shard_map/ppermute | solution.py:484
  17.4 9.4 %collective-permute-start.2 = (bf16[64,3072]{1,0:T(8,128)(2,1)S(1)}, bf16[64,3072]{1,0:T(8,128)(2,1)S(1)}, u32[]{:S(2)}, u32[]{:S(2)}) collective-permute-start(bf16[64,3072]{1,0:T(8,128)(2,1)S(1)} %pad_maximum_fusion.1), channel_id=1, source_target_pairs={{0,2},{1,3},{2,0},{3,1},{4,6},{5,7},{6,4},{7,5},{8,10},{9,11},{10,... | collective-permute-start | bytes 1179656 | tf_op jit(solution)/shard_map/ppermute | solution.py:484
  26.9 9.3 %copy-start.1 = (bf16[128,3072]{1,0:T(8,128)(2,1)}, bf16[128,3072]{1,0:T(8,128)(2,1)S(1)}, u32[]{:S(2)}) copy-start(bf16[128,3072]{1,0:T(8,128)(2,1)S(1)} %pad_maximum_fusion.near_ref) | copy-start | bytes 2359300
  26.9 9.3 %collective-permute-start.3 = (bf16[128,3072]{1,0:T(8,128)(2,1)S(1)}, bf16[128,3072]{1,0:T(8,128)(2,1)S(1)}, u32[]{:S(2)}, u32[]{:S(2)}) collective-permute-start(bf16[128,3072]{1,0:T(8,128)(2,1)S(1)} %pad_maximum_fusion.near_ref), channel_id=1, source_target_pairs={{0,1},{1,0},{2,3},{3,2},{4,5},{5,4},{6,7},{7,6},{8,9},{9,8},{10,11... | collective-permute-start | bytes 2359304 | tf_op jit(solution)/shard_map/ppermute | solution.py:484
  27.8 8.3 %collective-permute-start.4 = (bf16[1,3072]{1,0:T(2,128)(2,1)S(1)}, bf16[1,3072]{1,0:T(2,128)(2,1)S(1)}, u32[]{:S(2)}, u32[]{:S(2)}) collective-permute-start(bf16[1,3072]{1,0:T(2,128)(2,1)S(1)} %slice_bitcast_fusion.3), channel_id=1, source_target_pairs={{0,1},{1,2},{2,3},{3,4},{4,5},{5,6},{6,7},{7,8},{8,9},{9,10},{10,1... | collective-permute-start | bytes 18440 | tf_op jit(solution)/shard_map/ppermute | solution.py:495
  36.1 0.6 copy-start.8
  36.2 0.9 copy-start.7
  47.9 3.6 %copy-start = (bf16[16,208,128]{2,1,0:T(8,128)(2,1)S(1)}, bf16[16,208,128]{2,1,0:T(8,128)(2,1)}, u32[]{:S(2)}) copy-start(bf16[16,208,128]{2,1,0:T(8,128)(2,1)} %get-tuple-element.21) | copy-start | bytes 2555908
  49.0 2.5 %collective-permute-start.5 = (bf16[8,208,128]{2,1,0:T(8,128)(2,1)S(1)}, bf16[8,208,128]{2,1,0:T(8,128)(2,1)S(1)}, u32[]{:S(2)}, u32[]{:S(2)}) collective-permute-start(bf16[8,208,128]{2,1,0:T(8,128)(2,1)S(1)} %constant_dynamic-slice_fusion.3), channel_id=1, source_target_pairs={{0,1},{1,0},{2,3},{3,2},{4,5},{5,4},{6,7},{7,6},{8,9},{9,8},{10,11... | collective-permute-start | bytes 1277960 | tf_op jit(solution)/shard_map/ppermute | solution.py:484
  51.6 8.3 %collective-permute-start.6 = (bf16[4,208,128]{2,1,0:T(8,128)(2,1)S(1)}, bf16[4,208,128]{2,1,0:T(8,128)(2,1)S(1)}, u32[]{:S(2)}, u32[]{:S(2)}) collective-permute-start(bf16[4,208,128]{2,1,0:T(8,128)(2,1)S(1)} %constant_dynamic-slice_fusion.2), channel_id=1, source_target_pairs={{0,2},{1,3},{2,0},{3,1},{4,6},{5,7},{6,4},{7,5},{8,10},{9,11},{10,... | collective-permute-start | bytes 638984 | tf_op jit(solution)/shard_map/ppermute | solution.py:484
  54.1 30.2 %copy-start.5 = (bf16[128,128]{1,0:T(8,128)(2,1)S(1)}, bf16[128,128]{1,0:T(8,128)(2,1)}, u32[]{:S(2)}) copy-start(bf16[128,128]{1,0:T(8,128)(2,1)} %get-tuple-element.20.first_ref) | copy-start | bytes 98308
  60.0 5.5 %collective-permute-start.7 = (bf16[2,208,128]{2,1,0:T(8,128)(2,1)S(1)}, bf16[2,208,128]{2,1,0:T(8,128)(2,1)S(1)}, u32[]{:S(2)}, u32[]{:S(2)}) collective-permute-start(bf16[2,208,128]{2,1,0:T(8,128)(2,1)S(1)} %constant_dynamic-slice_fusion.1), channel_id=1, source_target_pairs={{0,4},{1,5},{2,6},{3,7},{4,0},{5,1},{6,2},{7,3},{8,12},{9,13},{10,... | collective-permute-start | bytes 319496 | tf_op jit(solution)/shard_map/ppermute | solution.py:484
  65.6 5.2 %collective-permute-start.8 = (bf16[1,208,128]{2,1,0:T(8,128)(2,1)S(1)}, bf16[1,208,128]{2,1,0:T(8,128)(2,1)S(1)}, u32[]{:S(2)}, u32[]{:S(2)}) collective-permute-start(bf16[1,208,128]{2,1,0:T(8,128)(2,1)S(1)} %constant_dynamic-slice_fusion), channel_id=1, source_target_pairs={{0,8},{1,9},{2,10},{3,11},{4,12},{5,13},{6,14},{7,15},{8,0},{9,1},... | collective-permute-start | bytes 159752 | tf_op jit(solution)/shard_map/ppermute | solution.py:484
  70.8 4.9 %collective-permute-start.10 = (bf16[1,80,128]{2,1,0:T(8,128)(2,1)S(1)}, bf16[1,80,128]{2,1,0:T(8,128)(2,1)S(1)}, u32[]{:S(2)}, u32[]{:S(2)}) collective-permute-start(bf16[1,80,128]{2,1,0:T(8,128)(2,1)S(1)} %slice.26), channel_id=1, source_target_pairs={{0,8},{1,9},{2,10},{3,11},{4,12},{5,13},{6,14},{7,15},{8,0},{9,1},... | collective-permute-start | bytes 61448 | tf_op jit(solution)/shard_map/ppermute | solution.py:484
  75.7 4.0 %collective-permute-start.11 = (bf16[2,80,128]{2,1,0:T(8,128)(2,1)S(1)}, bf16[2,80,128]{2,1,0:T(8,128)(2,1)S(1)}, u32[]{:S(2)}, u32[]{:S(2)}) collective-permute-start(bf16[2,80,128]{2,1,0:T(8,128)(2,1)S(1)} %pad_maximum_fusion.5), channel_id=1, source_target_pairs={{0,4},{1,5},{2,6},{3,7},{4,0},{5,1},{6,2},{7,3},{8,12},{9,13},{10,... | collective-permute-start | bytes 122888 | tf_op jit(solution)/shard_map/ppermute | solution.py:484
  79.7 4.5 %collective-permute-start.12 = (bf16[4,80,128]{2,1,0:T(8,128)(2,1)S(1)}, bf16[4,80,128]{2,1,0:T(8,128)(2,1)S(1)}, u32[]{:S(2)}, u32[]{:S(2)}) collective-permute-start(bf16[4,80,128]{2,1,0:T(8,128)(2,1)S(1)} %pad_maximum_fusion.4), channel_id=1, source_target_pairs={{0,2},{1,3},{2,0},{3,1},{4,6},{5,7},{6,4},{7,5},{8,10},{9,11},{10,... | collective-permute-start | bytes 245768 | tf_op jit(solution)/shard_map/ppermute | solution.py:484
  81.3 11.2 %copy-start.3 = (bf16[128,128]{1,0:T(8,128)(2,1)}, bf16[128,128]{1,0:T(8,128)(2,1)S(1)}, u32[]{:S(2)}) copy-start(bf16[128,128]{1,0:T(8,128)(2,1)S(1)} %slice_bitcast_fusion.2.second_ref) | copy-start | bytes 98308
  84.2 8.2 %copy-start.2 = (bf16[8,80,128]{2,1,0:T(8,128)(2,1)}, bf16[8,80,128]{2,1,0:T(8,128)(2,1)S(1)}, u32[]{:S(2)}) copy-start(bf16[8,80,128]{2,1,0:T(8,128)(2,1)S(1)} %pad_maximum_fusion.3.near_ref) | copy-start | bytes 491524
  84.2 11.1 %collective-permute-start.13 = (bf16[8,80,128]{2,1,0:T(8,128)(2,1)S(1)}, bf16[8,80,128]{2,1,0:T(8,128)(2,1)S(1)}, u32[]{:S(2)}, u32[]{:S(2)}) collective-permute-start(bf16[8,80,128]{2,1,0:T(8,128)(2,1)S(1)} %pad_maximum_fusion.3.near_ref), channel_id=1, source_target_pairs={{0,1},{1,0},{2,3},{3,2},{4,5},{5,4},{6,7},{7,6},{8,9},{9,8},{10,11... | collective-permute-start | bytes 491528 | tf_op jit(solution)/shard_map/ppermute | solution.py:484
  84.3 8.1 %collective-permute-start.9 = (bf16[32,128]{1,0:T(8,128)(2,1)S(1)}, bf16[32,128]{1,0:T(8,128)(2,1)S(1)}, u32[]{:S(2)}, u32[]{:S(2)}) collective-permute-start(bf16[32,128]{1,0:T(8,128)(2,1)S(1)} %bitcast.16), channel_id=1, source_target_pairs={{1,0},{2,1},{3,2},{4,3},{5,4},{6,5},{7,6},{8,7},{9,8},{10,9},{11,1... | collective-permute-start | bytes 24584 | tf_op jit(solution)/shard_map/ppermute | solution.py:515
  92.4 0.6 copy-start.6
  95.4 0.7 copy-start.4

commit v2 on v1

--- a/solution.py
+++ b/solution.py
@@ -260,8 +260,9 @@
 
 
 def main_kernel(
-    count, bits, share, me_ref, near_ref, far_ref, own_ref, halo_ref, wv_ref, bias_ref, proj_ref,
-    grad_ref, grad_t_ref, sums_ref, hid_ref, first_ref, first_grad_ref, even, odd, moved, pre0, wsum
+    count, bits, quarter, me_ref, near_ref, far_ref, own_ref, halo_ref, wv_ref, bias_ref, proj_ref,
+    grad_ref, grad_t_ref, kept_ref, sent_ref, hid_ref, first_ref, first_grad_ref, even, odd, moved, pre0,
+    wsum, pair
 ):
     ny = count * RD
     ext = ny + 2 * RD
@@ -312,7 +313,6 @@
     bias_sum = jnp.sum(pre_grad0, axis=0, keepdims=True)
     totals_in, totals_out = [None] * 3, [None] * 3
     zeros8 = jnp.zeros((8, C1), F32)
-    previous = None
     for c in range(WC):
         variant, start = window_of(c)
         lanes = slice(start, start + WIN)
@@ -341,15 +341,19 @@
         else:
             totals_in[variant] = totals_in[variant] + part_in
             totals_out[variant] = totals_out[variant] + part_out
+        pair[c % 2] = grad
         if c % 2:
-            for d in range(count):
-                pair = [g[8 * d : 8 * d + 8] for g in (previous, grad)]
-                sums_ref[reverse_bits(d, bits), 8 * (c - 1) : 8 * (c + 1), :] = jnp.concatenate(
-                    pair, axis=0
+            for place in range(count):
+                row = pl.multiple_of((reverse_bits(place, bits) ^ me) * RD, RD)
+                rows = [pair[k, pl.ds(row, RD), :] for k in range(2)]
+                dest = (kept_ref, sent_ref)[place // (count // 2)]
+                block = place % (count // 4)
+                at = PIX * block + RD * (c - 1)
+                dest[place // (count // 4) % 2, at : at + 2 * RD, :] = jnp.concatenate(
+                    rows, axis=0
                 ).astype(BF16)
-        previous = grad
-
-    wsum[9 * C0 + 2 * C1 :, :] = jnp.zeros((count * share - 9 * C0 - 2 * C1, C1), F32)
+
+    wsum[9 * C0 + 2 * C1 :, :] = jnp.zeros((4 * quarter - 9 * C0 - 2 * C1, C1), F32)
     for tap in range(3):
         if tap == 1:
             parts = totals_in
@@ -363,23 +367,22 @@
     wsum[9 * C0 : 9 * C0 + C1, :] = grad_proj[:, 0:C1]
     wsum[9 * C0 + C1 : 9 * C0 + 2 * C1, :] = grad_proj[:, C1:]
     wsum[9 * C0 + 2 * C1 : 9 * C0 + 2 * C1 + 1, :] = bias_sum
-    for p in range(count):
-        sums_ref[p, PIX : PIX + share, :] = wsum[share * p : share * p + share, :].astype(BF16)
-
-
-def whole(*shape):
-    return pl.BlockSpec(shape, lambda: (0,) * len(shape))
-
-
-def main(count, bits, share, me, near, far, own, halo, wv, bias, proj_weight, grad, grad_t):
+    for place in range(4):
+        row = pl.multiple_of((place ^ reverse_bits(me & 3, 2)) * quarter, 16)
+        dest = (kept_ref, sent_ref)[place // 2]
+        dest[place % 2, PIX * count // 4 :, :] = wsum[pl.ds(row, quarter), :].astype(BF16)
+
+
+def main(count, bits, quarter, me, near, far, own, halo, wv, bias, proj_weight, grad, grad_t):
     ny = count * RD
     ext = ny + 2 * RD
     vmem = pl.BlockSpec(memory_space=pltpu.VMEM)
     return pl.pallas_call(
-        functools.partial(main_kernel, count, bits, share),
+        functools.partial(main_kernel, count, bits, quarter),
         in_specs=[pl.BlockSpec(memory_space=pltpu.SMEM)] + [vmem] * 9,
         out_shape=(
-            jax.ShapeDtypeStruct((count, PIX + share, C1), BF16),
+            jax.ShapeDtypeStruct((2, PIX * count // 4 + quarter, C1), BF16),
+            jax.ShapeDtypeStruct((2, PIX * count // 4 + quarter, C1), BF16),
             jax.ShapeDtypeStruct((WC, ny, C1), BF16),
             jax.ShapeDtypeStruct((PIX, C), BF16),
             jax.ShapeDtypeStruct((PIX, C1), BF16),
@@ -389,7 +392,8 @@
             pltpu.VMEM((ext, 2 * WC * C0), BF16),
             pltpu.VMEM((ext + 16, 2 * C1), F32),
             pltpu.VMEM((PIX, C1), F32),
-            pltpu.VMEM((count * share, C1), F32),
+            pltpu.VMEM((4 * quarter, C1), F32),
+            pltpu.VMEM((2, ny, C1), F32),
         ],
         compiler_params=VMEM,
         cost_estimate=pl.CostEstimate(flops=4 * 10**9, bytes_accessed=6 * 10**6, transcendentals=0),
@@ -452,29 +456,29 @@
     )(first_grad, second_grad, border, wv)
 
 
-def final_kernel(count, bits, share, me_ref, near_ref, far_ref, conv_ref, bias_ref, proj_ref, wsum):
-    turned = reverse_bits(me_ref[0], bits)
-    for half, ref in ((0, near_ref), (1, far_ref)):
-        for j in range(count // 2):
-            at = (turned ^ (half * (count // 2) + j)) * share
-            wsum[pl.ds(pl.multiple_of(at, 16), share), :] = ref[j].astype(F32)
+def final_kernel(quarter, me_ref, near_ref, far_ref, conv_ref, bias_ref, proj_ref, wsum):
+    turned = reverse_bits(me_ref[0] & 3, 2)
+    for place in range(4):
+        ref = (near_ref, far_ref)[place // 2]
+        row = pl.multiple_of((place ^ turned) * quarter, 16)
+        wsum[pl.ds(row, quarter), :] = ref[place % 2].astype(F32)
     conv_ref[...] = wsum[0 : 9 * C0, :]
     proj_ref[:, 0:C1] = wsum[9 * C0 : 9 * C0 + C1, :]
     proj_ref[:, C1:] = wsum[9 * C0 + C1 : 9 * C0 + 2 * C1, :]
     bias_ref[...] = wsum[9 * C0 + 2 * C1 : 9 * C0 + 2 * C1 + 1, :]
 
 
-def final(count, bits, share, me, near, far):
+def final(quarter, me, near, far):
     vmem = pl.BlockSpec(memory_space=pltpu.VMEM)
     return pl.pallas_call(
-        functools.partial(final_kernel, count, bits, share),
+        functools.partial(final_kernel, quarter),
         in_specs=[pl.BlockSpec(memory_space=pltpu.SMEM), vmem, vmem],
         out_shape=(
             jax.ShapeDtypeStruct((9 * C0, C1), F32),
             jax.ShapeDtypeStruct((1, C1), F32),
             jax.ShapeDtypeStruct((C1, C), F32),
         ),
-        scratch_shapes=[pltpu.VMEM((count * share, C1), F32)],
+        scratch_shapes=[pltpu.VMEM((4 * quarter, C1), F32)],
         compiler_params=VMEM,
         name="weight_grads",
     )(me, near, far)
@@ -482,46 +486,53 @@
 
 def swap(value, bit, count):
     return lax.ppermute(value, "rows", [(i, i ^ bit) for i in range(count)])
+
+
+def plus(a, b):
+    return (a.astype(F32) + b.astype(F32)).astype(BF16)
 
 
 def per_device(frames, conv_weight, conv_bias, proj_weight, target_row, target_col, cotangent):
     count = lax.axis_size("rows")
     bits = count.bit_length() - 1
     ny = count * RD
-    me = lax.axis_index("rows").astype(jnp.int32)
-    me_word = me.reshape(1)
-    share = -(-(9 * C0 + 2 * C1 + 1) // (16 * count)) * 16
-
+    me_word = lax.axis_index("rows").astype(jnp.int32).reshape(1)
+    quarter = -(-(9 * C0 + 2 * C1 + 1) // 64) * 16
+
+    blocks = {0: frames[1]}
+    for wave in range(1, bits):
+        for mask in reversed(range(2, count, 2)):
+            if mask.bit_count() == wave:
+                bit = mask & -mask
+                blocks[mask] = swap(blocks[mask ^ bit], bit, count)
     halo = lax.ppermute(frames[0, 2 * RD - 1 :], "rows", [(i, i + 1) for i in range(count - 1)])
-    near = frames[1]
-    far = None
-    for bit in reversed(range(bits)):
-        if far is not None:
-            near = jnp.concatenate([near, far], axis=0)
-        far = swap(near, 1 << bit, count)
     grad, grad_t, wv = scatter(ny, target_row, target_col, cotangent, conv_weight)
-    sums, hid, first, first_grad = main(
-        count, bits, share, me_word, near, far, frames[0], halo, wv,
+    near = jnp.concatenate(
+        [blocks[2 * reverse_bits(k, bits - 1)] for k in range(count // 2)], axis=0
+    )
+    near, grad, halo = lax.optimization_barrier((near, grad, halo))
+    far = swap(near, 1, count)
+    kept, sent, hid, first, first_grad = main(
+        count, bits, quarter, me_word, near, far, frames[0], halo, wv,
         conv_bias.reshape(1, C1), proj_weight, grad, grad_t,
     )
-    for bit in range(bits):
-        half = sums.shape[0] // 2
-        mine = (me >> bit) & 1
-        kept = lax.dynamic_slice_in_dim(sums, mine * half, half, 0)
-        sent = lax.dynamic_slice_in_dim(sums, (1 - mine) * half, half, 0)
-        sums = (kept.astype(F32) + swap(sent, 1 << bit, count).astype(F32)).astype(BF16)
-    second_grad = sums[0, :PIX]
-    tops = jnp.concatenate([first_grad, second_grad], axis=0).reshape(2 * WC, RD, C1)[:, 0]
+
+    other = swap(sent, 1, count)
+    other = plus(kept[0], other[0]), swap(plus(kept[1], other[1]), 2, count)
+    lookups = lookup(ny, target_row, target_col, hid, first, proj_weight)
+    total = plus(*other)
+    total, lookups = lax.optimization_barrier((total, lookups))
+    pixels, weights = total[: PIX * count // 4], total[PIX * count // 4 :]
+    for bit in range(2, bits):
+        half = pixels.shape[0] // 2
+        other = swap(jnp.concatenate([pixels[half:], weights], axis=0), 1 << bit, count)
+        pixels, weights = plus(pixels[:half], other[:half]), plus(weights, other[half:])
+    near = jnp.stack([weights, swap(weights, 2, count)])
+    tops = jnp.concatenate([first_grad, pixels], axis=0).reshape(2 * WC, RD, C1)[:, 0]
     border = lax.ppermute(tops, "rows", [(i + 1, i) for i in range(count - 1)])
-    near = sums[:, PIX:]
-    far = None
-    for bit in reversed(range(bits)):
-        if far is not None:
-            near = jnp.concatenate([near, far], axis=0)
-        far = swap(near, 1 << bit, count)
-    grad_conv, grad_bias, grad_proj = final(count, bits, share, me_word, near, far)
-    grad_input = input_grad(first_grad, second_grad, border, wv)
-    lookups = lookup(ny, target_row, target_col, hid, first, proj_weight)
+    grad_input = input_grad(first_grad, pixels, border, wv)
+    far = swap(near, 1, count)
+    grad_conv, grad_bias, grad_proj = final(quarter, me_word, near, far)
     return lookups, grad_input, grad_conv, grad_bias.reshape(C1), grad_proj
 
 

time: 99.4 us -> 82.1 us (0.83)
  the two profiles are of different devices: /device:TPU:0 before, /device:TPU:1 now
where the time goes in v2:
time: 82.1 us; the launch traced here: 81.7 us
  Pallas kernels  28 us (34%)
  waiting for transfers between devices  28 us (34%)
  starting transfers between devices  19.1 us (23%)
  local copies, waits for them, and re-layouts  4.52 us (6%)
  other arithmetic  1.18 us (1%)
  between operations  0.87 us (1%)
    ppermute x14, waiting for transfers between devices, swap(): return lax.ppermute(value, 'rows', [(i, i ^ bit) for i in range(count)])  25.1 us
    ppermute x14, starting transfers between devices, swap(): return lax.ppermute(value, 'rows', [(i, i ^ bit) for i in range(count)])  13.5 us
    pallas_call x1, Pallas kernels, main(): pl.pallas_call(functools.partial(main_kernel, count, bits, quarter), in_s...  11 us
    pallas_call x1, Pallas kernels, lookup(): pl.pallas_call(functools.partial(lookup_kernel, ny), out_shape=jax.ShapeD...  6.83 us
    pallas_call x1, Pallas kernels, scatter(): pl.pallas_call(functools.partial(scatter_kernel, ny), out_shape=(jax.Shap...  5.99 us
    ppermute x1, starting transfers between devices, per_device(): lax.ppermute(frames[0, 2 * RD - 1:], 'rows', [(i, i + 1) for i in range(c...  3.54 us
    ppermute x1, waiting for transfers between devices, per_device(): border = lax.ppermute(tops, 'rows', [(i + 1, i) for i in range(count - 1)])  2.96 us
    unnamed x28, local copies, waits for them, and re-layouts  2.84 us
  transfers between devices with their start and end apart: 16, of which 9 were waited for; matrix products, arithmetic and copies ran while one was open for 0% of the time, Pallas kernels for 19%

profile of v2, /device:TPU:1, one launch (start us, length us, event | category | flops | bytes accessed | tf_op | source)
XLA Modules:
  0.0 81.7 jit_solution(5525298861139142953)
XLA Ops:
  0.6 1.6 %slice_bitcast_fusion = (bf16[16,3072]{1,0:T(8,128)(2,1)}, bf16[16,3072]{1,0:T(8,128)(2,1)S(1)}) fusion(bf16[2,16,3072]{2,1,0:T(8,128)(2,1)} %param.7), kind=kLoop, calls=%fused_computation.11 | loop fusion | bytes 393216 | tf_op jit(solution)/shard_map/squeeze | solution.py:516
  2.3 2.1 %collective-permute-start.3 = (bf16[16,3072]{1,0:T(8,128)(2,1)S(1)}, bf16[16,3072]{1,0:T(8,128)(2,1)S(1)}, u32[]{:S(2)}, u32[]{:S(2)}) collective-permute-start(bf16[16,3072]{1,0:T(8,128)(2,1)S(1)} %get-tuple-element.38), channel_id=1, source_target_pairs={{0,2},{1,3},{2,0},{3,1},{4,6},{5,7},{6,4},{7,5},{8,10},{9,11},{10,... | collective-permute-start | bytes 294920 | tf_op jit(solution)/shard_map/ppermute | solution.py:488
  4.3 1.3 %collective-permute-start.1 = (bf16[16,3072]{1,0:T(8,128)(2,1)S(1)}, bf16[16,3072]{1,0:T(8,128)(2,1)S(1)}, u32[]{:S(2)}, u32[]{:S(2)}) collective-permute-start(bf16[16,3072]{1,0:T(8,128)(2,1)S(1)} %get-tuple-element.38), channel_id=1, source_target_pairs={{0,4},{1,5},{2,6},{3,7},{4,0},{5,1},{6,2},{7,3},{8,12},{9,13},{10,... | collective-permute-start | bytes 294920 | tf_op jit(solution)/shard_map/ppermute | solution.py:488
  5.6 2.3 %collective-permute-start = (bf16[16,3072]{1,0:T(8,128)(2,1)S(1)}, bf16[16,3072]{1,0:T(8,128)(2,1)S(1)}, u32[]{:S(2)}, u32[]{:S(2)}) collective-permute-start(bf16[16,3072]{1,0:T(8,128)(2,1)S(1)} %get-tuple-element.38), channel_id=1, source_target_pairs={{0,8},{1,9},{2,10},{3,11},{4,12},{5,13},{6,14},{7,15},{8,0},{9,1},... | collective-permute-start | bytes 294920 | tf_op jit(solution)/shard_map/ppermute | solution.py:488
  8.0 3.5 %collective-permute-start.7 = (bf16[1,3072]{1,0:T(2,128)(2,1)S(1)}, bf16[1,3072]{1,0:T(2,128)(2,1)S(1)}, u32[]{:S(2)}, u32[]{:S(2)}) collective-permute-start(bf16[1,3072]{1,0:T(2,128)(2,1)S(1)} %slice_bitcast_fusion.2), channel_id=1, source_target_pairs={{0,1},{1,2},{2,3},{3,4},{4,5},{5,6},{6,7},{7,8},{8,9},{9,10},{10,1... | collective-permute-start | bytes 18440 | tf_op jit(solution)/shard_map/ppermute | solution.py:508
  11.5 6.0 %scatter.1 = (bf16[16,128,128]{2,1,0:T(8,128)(2,1)}, bf16[128,2048]{1,0:T(8,128)(2,1)}, bf16[3,384,384]{2,1,0:T(8,128)(2,1)}) custom-call(s32[12,128]{1,0:T(8,128)} %row_ref.3, s32[12,128]{1,0:T(8,128)} %col_ref.3, bf16[3888,128]{1,0:T(8,128)(2,1)} %cot_ref.1, bf16[864,128]{1,0:T(8,128)(2,1)} %w_ref.1), custom_call_target="tpu_custom_call" | custom-call | flops 1000000000 | bytes 4000000 | tf_op jit(solution)/shard_map/scatter/pallas_call | solution.py:142
  17.5 1.1 %collective-permute-start.4 = (bf16[16,3072]{1,0:T(8,128)(2,1)S(1)}, bf16[16,3072]{1,0:T(8,128)(2,1)S(1)}, u32[]{:S(2)}, u32[]{:S(2)}) collective-permute-start(bf16[16,3072]{1,0:T(8,128)(2,1)S(1)} %collective-permute-done), channel_id=1, source_target_pairs={{0,2},{1,3},{2,0},{3,1},{4,6},{5,7},{6,4},{7,5},{8,10},{9,11},{10,... | collective-permute-start | bytes 294920 | tf_op jit(solution)/shard_map/ppermute | solution.py:488
  18.8 0.3 collective-permute-start.5
  19.2 4.0 %collective-permute-done.2 = bf16[16,3072]{1,0:T(8,128)(2,1)S(1)} collective-permute-done((bf16[16,3072]{1,0:T(8,128)(2,1)S(1)}, bf16[16,3072]{1,0:T(8,128)(2,1)S(1)}, u32[]{:S(2)}, u32[]{:S(2)}) %collective-permute-start.2) | collective-permute-done | bytes 98336 | tf_op jit(solution)/shard_map/ppermute | solution.py:488
  23.2 0.6 collective-permute-start.6
  23.9 3.6 %collective-permute-done.6 = bf16[16,3072]{1,0:T(8,128)(2,1)S(1)} collective-permute-done((bf16[16,3072]{1,0:T(8,128)(2,1)S(1)}, bf16[16,3072]{1,0:T(8,128)(2,1)S(1)}, u32[]{:S(2)}, u32[]{:S(2)}) %collective-permute-start.6) | collective-permute-done | bytes 98336 | tf_op jit(solution)/shard_map/ppermute | solution.py:488
  27.5 1.0 %collective-permute-start.8 = (bf16[128,3072]{1,0:T(8,128)(2,1)S(1)}, bf16[128,3072]{1,0:T(8,128)(2,1)S(1)}, u32[]{:S(2)}, u32[]{:S(2)}) collective-permute-start(bf16[128,3072]{1,0:T(8,128)(2,1)S(1)} %constant_dynamic-update-slice_fusion.near_ref), channel_id=1, source_target_pairs={{0,1},{1,0},{2,3},{3,2},{4,5},{5,4},{6,7},{7,6},{8,9},{9,8},{10,11... | collective-permute-start | bytes 2359304 | tf_op jit(solution)/shard_map/ppermute | solution.py:488
  28.5 1.9 %collective-permute-done.8.far_ref = bf16[128,3072]{1,0:T(8,128)(2,1)S(1)} collective-permute-done((bf16[128,3072]{1,0:T(8,128)(2,1)S(1)}, bf16[128,3072]{1,0:T(8,128)(2,1)S(1)}, u32[]{:S(2)}, u32[]{:S(2)}) %collective-permute-start.8) | collective-permute-done | bytes 786464 | tf_op jit(solution)/shard_map/ppermute | solution.py:488
  30.4 0.9 %copy-done.8 = bf16[128,3072]{1,0:T(8,128)(2,1)} copy-done((bf16[128,3072]{1,0:T(8,128)(2,1)}, bf16[128,3072]{1,0:T(8,128)(2,1)S(1)}, u32[]{:S(2)}) %copy-start.8) | copy-done | bytes 786456
  31.4 11.0 %features.1 = (bf16[2,800,128]{2,1,0:T(8,128)(2,1)}, bf16[2,800,128]{2,1,0:T(8,128)(2,1)}, bf16[16,128,128]{2,1,0:T(8,128)(2,1)}, bf16[128,256]{1,0:T(8,128)(2,1)}, bf16[128,128]{1,0:T(8,128)(2,1)}) custom-call(s32[1]{0:T(128)} %bitcast.me_ref, bf16[128,3072]{1,0:T(8,128)(2,1)} %copy-done.6, bf16[128,3072]{1,0:T(8,128)(2,1)} %copy-done.8, ...), custom_call_target="tpu_custom_call" | custom-call | flops 4000000000 | bytes 6000000 | tf_op jit(solution)/shard_map/features/pallas_call | solution.py:380
  42.4 0.3 collective-permute-start.9
  42.7 1.6 %collective-permute-done.9 = bf16[2,800,128]{2,1,0:T(8,128)(2,1)S(1)} collective-permute-done((bf16[2,800,128]{2,1,0:T(8,128)(2,1)}, bf16[2,800,128]{2,1,0:T(8,128)(2,1)S(1)}, u32[]{:S(2)}, u32[]{:S(2)}) %collective-permute-start.9) | collective-permute-done | bytes 409632 | tf_op jit(solution)/shard_map/ppermute | solution.py:488
  44.3 1.0 %fusion.2 = bf16[800,128]{1,0:T(8,128)(2,1)S(1)} fusion(bf16[2,800,128]{2,1,0:T(8,128)(2,1)S(1)} %collective-permute-done.9, bf16[2,800,128]{2,1,0:T(8,128)(2,1)} %get-tuple-element.27), kind=kLoop, calls=%fused_computation.5 | loop fusion | flops 409600 | bytes 614400 | tf_op jit(solution)/shard_map/convert_element_type | solution.py:492
  45.3 0.6 collective-permute-start.10
  46.0 6.8 %lookup.1 = bf16[3888,128]{1,0:T(8,128)(2,1)} custom-call(s32[12,128]{1,0:T(8,128)} %row_ref.3, s32[12,128]{1,0:T(8,128)} %col_ref.3, bf16[16,128,128]{2,1,0:T(8,128)(2,1)} %get-tuple-element.29.hid_ref, bf16[128,256]{1,0:T(8,128)(2,1)} %get-tuple-element.30.first_ref, bf16[128,256]{1,0:T(8,128)(2,1)} %proj_ref.3), custom_call_target="tpu_custom_call" | custom-call | flops 1000000000 | bytes 4000000 | tf_op jit(solution)/shard_map/lookup/pallas_call | solution.py:214
  53.0 4.6 %collective-permute-done.11 = bf16[544,128]{1,0:T(8,128)(2,1)S(1)} collective-permute-done((bf16[544,128]{1,0:T(8,128)(2,1)S(1)}, bf16[544,128]{1,0:T(8,128)(2,1)S(1)}, u32[]{:S(2)}, u32[]{:S(2)}) %collective-permute-start.11) | collective-permute-done | bytes 139296 | tf_op jit(solution)/shard_map/ppermute | solution.py:488
  57.8 6.9 %collective-permute-done.12 = bf16[416,128]{1,0:T(8,128)(2,1)S(1)} collective-permute-done((bf16[416,128]{1,0:T(8,128)(2,1)S(1)}, bf16[416,128]{1,0:T(8,128)(2,1)S(1)}, u32[]{:S(2)}, u32[]{:S(2)}) %collective-permute-start.12) | collective-permute-done | bytes 106528 | tf_op jit(solution)/shard_map/ppermute | solution.py:488
  64.7 0.9 %collective-permute-start.14 = (bf16[288,128]{1,0:T(8,128)(2,1)S(1)}, bf16[288,128]{1,0:T(8,128)(2,1)S(1)}, u32[]{:S(2)}, u32[]{:S(2)}) collective-permute-start(bf16[288,128]{1,0:T(8,128)(2,1)S(1)} %add_convert_fusion.2), channel_id=1, source_target_pairs={{0,2},{1,3},{2,0},{3,1},{4,6},{5,7},{6,4},{7,5},{8,10},{9,11},{10,... | collective-permute-start | bytes 221192 | tf_op jit(solution)/shard_map/ppermute | solution.py:488
  65.7 2.3 %collective-permute-done.14 = bf16[288,128]{1,0:T(8,128)(2,1)S(1)} collective-permute-done((bf16[288,128]{1,0:T(8,128)(2,1)S(1)}, bf16[288,128]{1,0:T(8,128)(2,1)S(1)}, u32[]{:S(2)}, u32[]{:S(2)}) %collective-permute-start.14) | collective-permute-done | bytes 73760 | tf_op jit(solution)/shard_map/ppermute | solution.py:488
  68.0 2.5 %collective-permute-start.15 = (bf16[2,288,128]{2,1,0:T(8,128)(2,1)S(1)}, bf16[2,288,128]{2,1,0:T(8,128)(2,1)S(1)}, u32[]{:S(2)}, u32[]{:S(2)}) collective-permute-start(bf16[2,288,128]{2,1,0:T(8,128)(2,1)S(1)} %pad_maximum_fusion.near_ref), channel_id=1, source_target_pairs={{0,1},{1,0},{2,3},{3,2},{4,5},{5,4},{6,7},{7,6},{8,9},{9,8},{10,11... | collective-permute-start | bytes 442376 | tf_op jit(solution)/shard_map/ppermute | solution.py:488
  70.6 0.6 copy-done.3
  71.2 2.0 %collective-permute-start.13 = (bf16[32,128]{1,0:T(8,128)(2,1)S(1)}, bf16[32,128]{1,0:T(8,128)(2,1)S(1)}, u32[]{:S(2)}, u32[]{:S(2)}) collective-permute-start(bf16[32,128]{1,0:T(8,128)(2,1)S(1)} %bitcast.27), channel_id=1, source_target_pairs={{1,0},{2,1},{3,2},{4,3},{5,4},{6,5},{7,6},{8,7},{9,8},{10,9},{11,1... | collective-permute-start | bytes 24584 | tf_op jit(solution)/shard_map/ppermute | solution.py:532
  73.3 3.0 %collective-permute-done.13.border_ref = bf16[32,128]{1,0:T(8,128)(2,1)S(1)} collective-permute-done((bf16[32,128]{1,0:T(8,128)(2,1)S(1)}, bf16[32,128]{1,0:T(8,128)(2,1)S(1)}, u32[]{:S(2)}, u32[]{:S(2)}) %collective-permute-start.13) | collective-permute-done | bytes 8224 | tf_op jit(solution)/shard_map/ppermute | solution.py:532
  76.2 0.6 copy-done.7
  76.8 2.3 %input_grad.1 = bf16[2,16,3072]{2,1,0:T(8,128)(2,1)} custom-call(bf16[128,128]{1,0:T(8,128)(2,1)} %get-tuple-element.32.first_ref, bf16[128,128]{1,0:T(8,128)(2,1)} %copy-done.3, bf16[32,128]{1,0:T(8,128)(2,1)} %copy-done.7, bf16[3,384,384]{2,1,0:T(8,128)(2,1)} %get-tuple-element.24.wv_ref), custom_call_target="tpu_custom_call" | custom-call | flops 100000000 | bytes 1000000 | tf_op jit(solution)/shard_map/input_grad/pallas_call | solution.py:446
  79.1 0.7 copy-done.4
  79.8 1.9 %weight_grads.1 = (f32[864,128]{1,0:T(8,128)}, f32[1,128]{1,0:T(1,128)}, f32[128,256]{1,0:T(8,128)}) custom-call(s32[1]{0:T(128)} %bitcast.me_ref, bf16[2,288,128]{2,1,0:T(8,128)(2,1)} %copy-done, bf16[2,288,128]{2,1,0:T(8,128)(2,1)} %copy-done.4), custom_call_target="tpu_custom_call" | custom-call | tf_op jit(solution)/shard_map/weight_grads/pallas_call | solution.py:473
  (48 shorter events, 0.7 us)
Async XLA Ops:
  0.6 7.3 %copy-start.1 = (bf16[2,16,3072]{2,1,0:T(8,128)(2,1)S(1)}, bf16[2,16,3072]{2,1,0:T(8,128)(2,1)}, u32[]{:S(2)}) copy-start(bf16[2,16,3072]{2,1,0:T(8,128)(2,1)} %param.7) | copy-start | bytes 589828
  2.3 21.5 %collective-permute-start.3 = (bf16[16,3072]{1,0:T(8,128)(2,1)S(1)}, bf16[16,3072]{1,0:T(8,128)(2,1)S(1)}, u32[]{:S(2)}, u32[]{:S(2)}) collective-permute-start(bf16[16,3072]{1,0:T(8,128)(2,1)S(1)} %get-tuple-element.38), channel_id=1, source_target_pairs={{0,2},{1,3},{2,0},{3,1},{4,6},{5,7},{6,4},{7,5},{8,10},{9,11},{10,... | collective-permute-start | bytes 294920 | tf_op jit(solution)/shard_map/ppermute | solution.py:488
  4.3 14.5 %collective-permute-start.1 = (bf16[16,3072]{1,0:T(8,128)(2,1)S(1)}, bf16[16,3072]{1,0:T(8,128)(2,1)S(1)}, u32[]{:S(2)}, u32[]{:S(2)}) collective-permute-start(bf16[16,3072]{1,0:T(8,128)(2,1)S(1)} %get-tuple-element.38), channel_id=1, source_target_pairs={{0,4},{1,5},{2,6},{3,7},{4,0},{5,1},{6,2},{7,3},{8,12},{9,13},{10,... | collective-permute-start | bytes 294920 | tf_op jit(solution)/shard_map/ppermute | solution.py:488
  5.6 11.9 %collective-permute-start = (bf16[16,3072]{1,0:T(8,128)(2,1)S(1)}, bf16[16,3072]{1,0:T(8,128)(2,1)S(1)}, u32[]{:S(2)}, u32[]{:S(2)}) collective-permute-start(bf16[16,3072]{1,0:T(8,128)(2,1)S(1)} %get-tuple-element.38), channel_id=1, source_target_pairs={{0,8},{1,9},{2,10},{3,11},{4,12},{5,13},{6,14},{7,15},{8,0},{9,1},... | collective-permute-start | bytes 294920 | tf_op jit(solution)/shard_map/ppermute | solution.py:488
  8.0 19.5 %collective-permute-start.7 = (bf16[1,3072]{1,0:T(2,128)(2,1)S(1)}, bf16[1,3072]{1,0:T(2,128)(2,1)S(1)}, u32[]{:S(2)}, u32[]{:S(2)}) collective-permute-start(bf16[1,3072]{1,0:T(2,128)(2,1)S(1)} %slice_bitcast_fusion.2), channel_id=1, source_target_pairs={{0,1},{1,2},{2,3},{3,4},{4,5},{5,6},{6,7},{7,8},{8,9},{9,10},{10,1... | collective-permute-start | bytes 18440 | tf_op jit(solution)/shard_map/ppermute | solution.py:508
  17.5 6.3 %collective-permute-start.4 = (bf16[16,3072]{1,0:T(8,128)(2,1)S(1)}, bf16[16,3072]{1,0:T(8,128)(2,1)S(1)}, u32[]{:S(2)}, u32[]{:S(2)}) collective-permute-start(bf16[16,3072]{1,0:T(8,128)(2,1)S(1)} %collective-permute-done), channel_id=1, source_target_pairs={{0,2},{1,3},{2,0},{3,1},{4,6},{5,7},{6,4},{7,5},{8,10},{9,11},{10,... | collective-permute-start | bytes 294920 | tf_op jit(solution)/shard_map/ppermute | solution.py:488
  18.6 4.6 %collective-permute-start.2 = (bf16[16,3072]{1,0:T(8,128)(2,1)S(1)}, bf16[16,3072]{1,0:T(8,128)(2,1)S(1)}, u32[]{:S(2)}, u32[]{:S(2)}) collective-permute-start(bf16[16,3072]{1,0:T(8,128)(2,1)S(1)} %collective-permute-done), channel_id=1, source_target_pairs={{0,4},{1,5},{2,6},{3,7},{4,0},{5,1},{6,2},{7,3},{8,12},{9,13},{10,... | collective-permute-start | bytes 294920 | tf_op jit(solution)/shard_map/ppermute | solution.py:488
  18.8 5.1 %collective-permute-start.5 = (bf16[16,3072]{1,0:T(8,128)(2,1)S(1)}, bf16[16,3072]{1,0:T(8,128)(2,1)S(1)}, u32[]{:S(2)}, u32[]{:S(2)}) collective-permute-start(bf16[16,3072]{1,0:T(8,128)(2,1)S(1)} %collective-permute-done.1), channel_id=1, source_target_pairs={{0,2},{1,3},{2,0},{3,1},{4,6},{5,7},{6,4},{7,5},{8,10},{9,11},{10,... | collective-permute-start | bytes 294920 | tf_op jit(solution)/shard_map/ppermute | solution.py:488
  23.2 4.3 %collective-permute-start.6 = (bf16[16,3072]{1,0:T(8,128)(2,1)S(1)}, bf16[16,3072]{1,0:T(8,128)(2,1)S(1)}, u32[]{:S(2)}, u32[]{:S(2)}) collective-permute-start(bf16[16,3072]{1,0:T(8,128)(2,1)S(1)} %collective-permute-done.2), channel_id=1, source_target_pairs={{0,2},{1,3},{2,0},{3,1},{4,6},{5,7},{6,4},{7,5},{8,10},{9,11},{10,... | collective-permute-start | bytes 294920 | tf_op jit(solution)/shard_map/ppermute | solution.py:488
  27.5 3.0 %copy-start.6 = (bf16[128,3072]{1,0:T(8,128)(2,1)}, bf16[128,3072]{1,0:T(8,128)(2,1)S(1)}, u32[]{:S(2)}) copy-start(bf16[128,3072]{1,0:T(8,128)(2,1)S(1)} %constant_dynamic-update-slice_fusion.near_ref) | copy-start | bytes 2359300
  27.5 2.9 %copy-start.9 = (bf16[1,3072]{1,0:T(2,128)(2,1)}, bf16[1,3072]{1,0:T(2,128)(2,1)S(1)}, u32[]{:S(2)}) copy-start(bf16[1,3072]{1,0:T(2,128)(2,1)S(1)} %collective-permute-done.7.halo_ref) | copy-start | bytes 18436
  27.5 2.9 %collective-permute-start.8 = (bf16[128,3072]{1,0:T(8,128)(2,1)S(1)}, bf16[128,3072]{1,0:T(8,128)(2,1)S(1)}, u32[]{:S(2)}, u32[]{:S(2)}) collective-permute-start(bf16[128,3072]{1,0:T(8,128)(2,1)S(1)} %constant_dynamic-update-slice_fusion.near_ref), channel_id=1, source_target_pairs={{0,1},{1,0},{2,3},{3,2},{4,5},{5,4},{6,7},{7,6},{8,9},{9,8},{10,11... | collective-permute-start | bytes 2359304 | tf_op jit(solution)/shard_map/ppermute | solution.py:488
  30.4 0.9 %copy-start.8 = (bf16[128,3072]{1,0:T(8,128)(2,1)}, bf16[128,3072]{1,0:T(8,128)(2,1)S(1)}, u32[]{:S(2)}) copy-start(bf16[128,3072]{1,0:T(8,128)(2,1)S(1)} %collective-permute-done.8.far_ref) | copy-start | bytes 2359300
  42.4 2.0 %collective-permute-start.9 = (bf16[2,800,128]{2,1,0:T(8,128)(2,1)}, bf16[2,800,128]{2,1,0:T(8,128)(2,1)S(1)}, u32[]{:S(2)}, u32[]{:S(2)}) collective-permute-start(bf16[2,800,128]{2,1,0:T(8,128)(2,1)} %get-tuple-element.28), channel_id=1, source_target_pairs={{0,1},{1,0},{2,3},{3,2},{4,5},{5,4},{6,7},{7,6},{8,9},{9,8},{10,11... | collective-permute-start | bytes 1228808 | tf_op jit(solution)/shard_map/ppermute | solution.py:488
  45.3 7.5 %collective-permute-start.10 = (bf16[800,128]{1,0:T(8,128)(2,1)S(1)}, bf16[800,128]{1,0:T(8,128)(2,1)S(1)}, u32[]{:S(2)}, u32[]{:S(2)}) collective-permute-start(bf16[800,128]{1,0:T(8,128)(2,1)S(1)} %fusion.2), channel_id=1, source_target_pairs={{0,2},{1,3},{2,0},{3,1},{4,6},{5,7},{6,4},{7,5},{8,10},{9,11},{10,... | collective-permute-start | bytes 614408 | tf_op jit(solution)/shard_map/ppermute | solution.py:488
  46.0 6.8 %copy-start.2 = (bf16[2,800,128]{2,1,0:T(8,128)(2,1)S(1)}, bf16[2,800,128]{2,1,0:T(8,128)(2,1)}, u32[]{:S(2)}) copy-start(bf16[2,800,128]{2,1,0:T(8,128)(2,1)} %get-tuple-element.27) | copy-start | bytes 1228804
  52.9 4.7 %collective-permute-start.11 = (bf16[544,128]{1,0:T(8,128)(2,1)S(1)}, bf16[544,128]{1,0:T(8,128)(2,1)S(1)}, u32[]{:S(2)}, u32[]{:S(2)}) collective-permute-start(bf16[544,128]{1,0:T(8,128)(2,1)S(1)} %concatenate.13), channel_id=1, source_target_pairs={{0,4},{1,5},{2,6},{3,7},{4,0},{5,1},{6,2},{7,3},{8,12},{9,13},{10,... | collective-permute-start | bytes 417800 | tf_op jit(solution)/shard_map/ppermute | solution.py:488
  57.7 7.0 %collective-permute-start.12 = (bf16[416,128]{1,0:T(8,128)(2,1)S(1)}, bf16[416,128]{1,0:T(8,128)(2,1)S(1)}, u32[]{:S(2)}, u32[]{:S(2)}) collective-permute-start(bf16[416,128]{1,0:T(8,128)(2,1)S(1)} %pad_maximum_fusion.1), channel_id=1, source_target_pairs={{0,8},{1,9},{2,10},{3,11},{4,12},{5,13},{6,14},{7,15},{8,0},{9,1},... | collective-permute-start | bytes 319496 | tf_op jit(solution)/shard_map/ppermute | solution.py:488
  64.7 3.3 %collective-permute-start.14 = (bf16[288,128]{1,0:T(8,128)(2,1)S(1)}, bf16[288,128]{1,0:T(8,128)(2,1)S(1)}, u32[]{:S(2)}, u32[]{:S(2)}) collective-permute-start(bf16[288,128]{1,0:T(8,128)(2,1)S(1)} %add_convert_fusion.2), channel_id=1, source_target_pairs={{0,2},{1,3},{2,0},{3,1},{4,6},{5,7},{6,4},{7,5},{8,10},{9,11},{10,... | collective-permute-start | bytes 221192 | tf_op jit(solution)/shard_map/ppermute | solution.py:488
  68.0 11.1 %copy-start = (bf16[2,288,128]{2,1,0:T(8,128)(2,1)}, bf16[2,288,128]{2,1,0:T(8,128)(2,1)S(1)}, u32[]{:S(2)}) copy-start(bf16[2,288,128]{2,1,0:T(8,128)(2,1)S(1)} %pad_maximum_fusion.near_ref) | copy-start | bytes 442372
  68.0 2.6 %copy-start.5 = (bf16[128,128]{1,0:T(8,128)(2,1)S(1)}, bf16[128,128]{1,0:T(8,128)(2,1)}, u32[]{:S(2)}) copy-start(bf16[128,128]{1,0:T(8,128)(2,1)} %get-tuple-element.32.first_ref) | copy-start | bytes 98308
  68.0 11.1 %collective-permute-start.15 = (bf16[2,288,128]{2,1,0:T(8,128)(2,1)S(1)}, bf16[2,288,128]{2,1,0:T(8,128)(2,1)S(1)}, u32[]{:S(2)}, u32[]{:S(2)}) collective-permute-start(bf16[2,288,128]{2,1,0:T(8,128)(2,1)S(1)} %pad_maximum_fusion.near_ref), channel_id=1, source_target_pairs={{0,1},{1,0},{2,3},{3,2},{4,5},{5,4},{6,7},{7,6},{8,9},{9,8},{10,11... | collective-permute-start | bytes 442376 | tf_op jit(solution)/shard_map/ppermute | solution.py:488
  70.6 0.6 copy-start.3
  71.2 5.0 %collective-permute-start.13 = (bf16[32,128]{1,0:T(8,128)(2,1)S(1)}, bf16[32,128]{1,0:T(8,128)(2,1)S(1)}, u32[]{:S(2)}, u32[]{:S(2)}) collective-permute-start(bf16[32,128]{1,0:T(8,128)(2,1)S(1)} %bitcast.27), channel_id=1, source_target_pairs={{1,0},{2,1},{3,2},{4,3},{5,4},{6,5},{7,6},{8,7},{9,8},{10,9},{11,1... | collective-permute-start | bytes 24584 | tf_op jit(solution)/shard_map/ppermute | solution.py:532
  76.2 0.6 copy-start.7
  79.1 0.7 copy-start.4

commit v3 on v2

v3 whole, which is shorter than its diff:
```python
import functools

import jax
import jax.numpy as jnp
from jax import lax
from jax.experimental import pallas as pl
from jax.experimental.pallas import tpu as pltpu
from jax.sharding import PartitionSpec as P

C = 256
C1 = 128
C0 = 96
LEVELS = 4
SPAN = 9
ITERS = 12
RD = 8
WC = 16
LOOKS = 3888
PIX = RD * WC
WIN = 384
BLOCK = PIX + 2 * WC
CHUNKS = [slice(k * LOOKS // 3, (k + 1) * LOOKS // 3) for k in range(3)]
F32 = jnp.float32
BF16 = jnp.bfloat16


def vmem_of(ny):
    return pltpu.CompilerParams(vmem_limit_bytes=(8 + ny * 3 // 16) * 1024 * 1024)

def dot(a, b):
    return jnp.dot(a, b, preferred_element_type=F32)

def dot_nt(a, b):
    return lax.dot_general(a, b, (((1,), (1,)), ((), ())), preferred_element_type=F32)

def dot_tn(a, b):
    return lax.dot_general(a, b, (((0,), (0,)), ((), ())), preferred_element_type=F32)

def iota(shape, dim):
    return lax.broadcasted_iota(jnp.int32, shape, dim)

def pick(tile, index):
    return jnp.take_along_axis(tile, index, axis=0, mode="promise_in_bounds")

def pool_matrix(ny):
    parts = []
    for level in range(1, LEVELS):
        shape = (ny >> level, ny)
        hit = iota(shape, 0) == (iota(shape, 1) >> level)
        parts.append(jnp.where(hit, 0.25**level, 0.0))
    return jnp.concatenate(parts, axis=0).astype(BF16)

def spread_matrix(ny):
    parts = []
    for level in range(1, LEVELS):
        shape = (ny, ny >> level)
        hit = (iota(shape, 0) >> level) == iota(shape, 1)
        parts.append(jnp.where(hit, 0.25**level, 0.0))
    return jnp.concatenate(parts, axis=1).astype(BF16)

def identity():
    return jnp.where(iota((C1, C1), 0) == iota((C1, C1), 1), 1.0, 0.0).astype(BF16)


def lane_row(ref, step):
    return jnp.broadcast_to(ref[pl.ds(step, 1), :], (8, PIX))

def place_columns(source, offset, cols):
    values = list(source)
    bit = 1
    while bit < cols:
        taken = (offset & bit) != 0
        last = 2 * bit >= cols
        size = len(values)
        moved = []
        for k in range(size + bit):
            if last and not 4 <= k < cols + 4:
                moved.append(None)
                continue
            here = values[k] if k < size else None
            back = values[k - bit] if 0 <= k - bit < size else None
            here = jnp.zeros((8, PIX), F32) if here is None else here
            back = jnp.zeros((8, PIX), F32) if back is None else back
            moved.append(jnp.where(taken, back, here))
        values = moved
        bit *= 2
    return values[4 : cols + 4]

def window_columns(source, offset, cols):
    zero = jnp.zeros((8, PIX), F32)
    values = [zero] * 4 + list(source) + [zero] * 4
    bit = cols // 2
    while bit >= 1:
        taken = (offset & bit) != 0
        values = [jnp.where(taken, values[k + bit], values[k]) for k in range(bit + 8)]
        bit //= 2
    return values

def scatter_kernel(
    ny, row_ref, col_ref, cot_hbm, w_ref, grad_ref, grad_t_ref, wv_ref, cot_in, cot, packed, sems, *sums
):
    sub = iota((8, PIX), 0)
    loads = [
        pltpu.make_async_copy(cot_hbm.at[part], cot_in.at[part], sems.at[k])
        for k, part in enumerate(CHUNKS)
    ]
    for load in loads:
        load.start()
    for level in range(LEVELS):
        sums[level][...] = jnp.zeros(sums[level].shape, F32)
    wv_ref[...] = jnp.zeros(wv_ref.shape, BF16)
    for tap in range(3):
        lanes = slice(tap * C1, tap * C1 + C1)
        rows = w_ref[tap * 288 : tap * 288 + 288, :]
        wv_ref[0, 32:320, lanes] = rows
        wv_ref[1, 96:384, lanes] = rows

    def step(t, carry):
        row_all, col_all = lane_row(row_ref, t), lane_row(col_ref, t)
        for level in range(LEVELS):
            cols, tiles = WC >> level, ny >> (level + 3)
            base = t * 324 + level * 81
            start = (row_all >> level) + 4
            col = col_all >> level
            shift, tile_at = start & 7, start >> 3
            body = [cot[pl.ds(base + dx, 8, stride=SPAN), :] for dx in range(SPAN)]
            tail = [
                jnp.broadcast_to(cot[pl.ds(base + 72 + dx, 1), :], (8, PIX)) for dx in range(SPAN)
            ]
            body = place_columns(body, col, cols)
            tail = place_columns(tail, col, cols)
            index = (sub - shift) & 7
            upper, lower, edge = sub >= shift, sub < shift, sub == shift
            hits = [tile_at == k for k in range(tiles + 1)]
            for v in range(cols):
                turned = pick(body[v], index)
                high = jnp.where(upper, turned, 0.0)
                low = jnp.where(lower, turned, jnp.where(edge, tail[v], 0.0))
                for k in range(tiles):
                    term = jnp.where(hits[k + 1], high, jnp.where(hits[k], low, 0.0))
                    sums[level][v, 8 * k : 8 * k + 8, :] += term
        return carry

    for k, part in enumerate(CHUNKS):
        loads[k].wait()
        cot[part, :] = cot_in[part, :].astype(F32)
        lax.fori_loop(4 * k, 4 * k + 4, step, 0)
    at = 0
    for level in range(1, LEVELS):
        for pair in range(WC // 2):
            packed[at : at + (ny >> level), pair * PIX : pair * PIX + PIX] = sums[level][
                pair >> (level - 1)
            ].astype(BF16)
        at += ny >> level
    added = dot(spread_matrix(ny), packed[...])
    for v in range(WC):
        lanes = slice(v // 2 * PIX, v // 2 * PIX + PIX)
        grad_ref[v] = (sums[0][v] + added[:, lanes]).astype(BF16)
    grad_t_ref[...] = dot_nt(identity(), grad_ref[...].reshape(WC * ny, PIX)).astype(BF16)

def scatter(ny, target_row, target_col, cotangent, conv_weight):
    vmem = pl.BlockSpec(memory_space=pltpu.VMEM)
    return pl.pallas_call(
        functools.partial(scatter_kernel, ny),
        out_shape=(
            jax.ShapeDtypeStruct((WC, ny, PIX), BF16),
            jax.ShapeDtypeStruct((PIX, WC * ny), BF16),
            jax.ShapeDtypeStruct((2, WIN, WIN), BF16),
        ),
        in_specs=[vmem, vmem, pl.BlockSpec(memory_space=pl.ANY), vmem],
        scratch_shapes=[
            pltpu.VMEM((LOOKS, PIX), BF16),
            pltpu.VMEM((LOOKS, PIX), F32),
            pltpu.VMEM((ny * 7 // 8, WC // 2 * PIX), BF16),
            pltpu.SemaphoreType.DMA((3,)),
        ]
        + [pltpu.VMEM((WC >> level, ny >> level, PIX), F32) for level in range(LEVELS)],
        compiler_params=vmem_of(ny),
        cost_estimate=pl.CostEstimate(flops=10**9, bytes_accessed=4 * 10**6, transcendentals=0),
        name="scatter",
    )(target_row, target_col, cotangent, conv_weight)

def lookup_kernel(
    ny, row_ref, col_ref, hid_ref, first_ref, proj_ref, out_hbm, looked, out, second, wide, pooled,
    sems, *volumes
):
    sub = iota((8, PIX), 0)
    first = first_ref[...]
    zero = jnp.zeros((8, PIX), F32)
    for level in range(LEVELS):
        for v in range(WC >> level):
            volumes[level][v, 0:8, :] = zero
            volumes[level][v, 8 + (ny >> level) :, :] = zero
    second[...] = dot(hid_ref[...].reshape(WC * ny, C1), proj_ref[...]).astype(BF16)
    for v in range(WC):
        wide[:, v * C : v * C + C] = second[v * ny : v * ny + ny, :]
    means = dot(pool_matrix(ny), wide[...])
    at = done = 0
    for level in range(1, LEVELS):
        size = ny >> level
        for v in range(WC >> level):
            first_at = v << level
            total = means[done : done + size, first_at * C : first_at * C + C]
            for k in range(first_at + 1, first_at + (1 << level)):
                total = total + means[done : done + size, k * C : k * C + C]
            pooled[at : at + size, :] = total.astype(BF16)
            at += size
        done += size
    scores = dot_nt(second[...], first) * (1.0 / 16.0)
    for v in range(WC):
        volumes[0][v, 8 : 8 + ny, :] = scores[v * ny : v * ny + ny]
    scores = dot_nt(pooled[...], first) * (1.0 / 16.0)
    at = 0
    for level in range(1, LEVELS):
        size = ny >> level
        for v in range(WC >> level):
            volumes[level][v, 8 : 8 + size, :] = scores[at : at + size]
            at += size

    def step(t, carry):
        row_all, col_all = lane_row(row_ref, t), lane_row(col_ref, t)
        for level in range(LEVELS):
            cols, tiles = WC >> level, ny >> (level + 3)
            base = t * 324 + level * 81
            start = (row_all >> level) + 4
            col = col_all >> level
            shift, tile_at = start & 7, start >> 3
            index = (sub + shift) & 7
            upper = sub >= shift
            beyond = tile_at >= tiles
            body, tail = [], []
            for v in range(cols):
                held = [volumes[level][v, 8 * k : 8 * k + 8, :] for k in range(tiles + 2)]
                for k in range(2):
                    held[k] = jnp.where(beyond, held[tiles + k], held[k])
                bit = tiles // 2
                while bit >= 1:
                    taken = (tile_at & bit) != 0
                    held = [jnp.where(taken, held[k + bit], held[k]) for k in range(bit + 1)]
                    bit //= 2
                body.append(pick(jnp.where(upper, held[0], held[1]), index))
                tail.append(pick(held[1], shift))
            body = window_columns(body, col, cols)
            tail = window_columns(tail, col, cols)
            for dx in range(SPAN):
                looked[pl.ds(base + dx, 8, stride=SPAN), :] = body[dx]
                looked[pl.ds(base + 72 + dx, 1), :] = tail[dx][0:1]
        return carry

    stores = []
    for k, part in enumerate(CHUNKS):
        lax.fori_loop(4 * k, 4 * k + 4, step, 0)
        out[part, :] = looked[part, :].astype(BF16)
        stores.append(pltpu.make_async_copy(out.at[part], out_hbm.at[part], sems.at[k]))
        stores[k].start()
    for store in stores:
        store.wait()

def lookup(ny, target_row, target_col, hid, first, proj_weight):
    return pl.pallas_call(
        functools.partial(lookup_kernel, ny),
        out_shape=jax.ShapeDtypeStruct((LOOKS, PIX), BF16),
        out_specs=pl.BlockSpec(memory_space=pl.ANY),
        scratch_shapes=[
            pltpu.VMEM((LOOKS, PIX), F32),
            pltpu.VMEM((LOOKS, PIX), BF16),
            pltpu.VMEM((WC * ny, C), BF16),
            pltpu.VMEM((ny, WC * C), BF16),
            pltpu.VMEM((ny * 21 // 4, C), BF16),
            pltpu.SemaphoreType.DMA((3,)),
        ]
        + [pltpu.VMEM((WC >> level, (ny >> level) + 16, PIX), F32) for level in range(LEVELS)],
        compiler_params=vmem_of(ny),
        cost_estimate=pl.CostEstimate(flops=10**9, bytes_accessed=4 * 10**6, transcendentals=0),
        name="lookup",
    )(target_row, target_col, hid, first, proj_weight)


def reverse_bits(value, bits):
    total = 0
    for bit in range(bits):
        total = total | (((value >> bit) & 1) << (bits - 1 - bit))
    return total


def row_pick(me, count, bits):
    shape = (3 * count * RD, 2 * count * RD)
    row, at = iota(shape, 0), iota(shape, 1)
    kind, row = row // (count * RD), row % (count * RD)
    line = 2 * row + jnp.where(kind == 2, -1, kind)
    place = reverse_bits(((line >> 4) & (count - 1)) ^ me, bits) * (2 * RD) + (line & 15)
    return jnp.where((place == at) & (line >= 0), 1.0, 0.0).astype(BF16)


def own_pick():
    shape = (6 * RD, 2 * RD)
    row, at = iota(shape, 0), iota(shape, 1)
    kind, row = row >> 4, row & 15
    line = 2 * row + jnp.where(kind == 2, -1, kind)
    return jnp.where((line == at) & (row < RD), 1.0, 0.0).astype(BF16)


def pixel_pick(transposed):
    a, b = iota((PIX, PIX), 0), iota((PIX, PIX), 1)
    a, b = (b, a) if transposed else (a, b)
    return jnp.where(a == (b & 7) * WC + (b >> 3), 1.0, 0.0).astype(BF16)


def main_kernel(
    count, bits, quarter, me_ref, near_ref, far_ref, own_ref, halo_ref, wv_ref, bias_ref, proj_ref,
    grad_ref, grad_t_ref, kept_ref, sent_ref, sums_kept_ref, sums_sent_ref, hid_ref, first_ref,
    first_grad_ref, views, inner, grads, rows_out, turned, pre0, below, wsum
):
    ny = count * RD
    span = 8 * ny
    me = me_ref[0]

    def place_rows(start, step, lanes_of):
        for q in range(8):
            rows = slice(start + step * q, start + step * q + step)
            after = slice(start + step * (q + 1), start + step * (q + 2))
            value = lanes_of(slice(q * WIN, q * WIN + WIN))
            for kind in range(3):
                part = value[step * kind : step * kind + step]
                views[kind, 1, rows, :] = part
                views[kind, 0, rows, 128:WIN] = part[:, 0:256]
                if q == 0:
                    views[kind, 0, rows, 0:128] = jnp.zeros((step, 128), BF16)
                if q < 7:
                    views[kind, 0, after, 0:128] = part[:, 256:WIN]

    picks = row_pick(me, count, bits)
    own_picks = own_pick()
    at_halo = iota((6 * RD, WIN), 0) == 4 * RD

    def owned(lanes):
        top = jnp.broadcast_to(halo_ref[:, lanes].astype(F32), (6 * RD, WIN))
        return jnp.where(at_halo, top, dot(own_picks, own_ref[:, lanes])).astype(BF16)

    place_rows(span, 2 * RD, owned)

    def gathered(lanes):
        rows = jnp.concatenate([near_ref[:, lanes], far_ref[:, lanes]], axis=0)
        return dot(picks, rows).astype(BF16)

    place_rows(0, ny, gathered)

    bias = bias_ref[...]
    for g in range(2):
        inner[...] = (
            dot(views[0, g], wv_ref[g, :, C1 : 2 * C1])
            + dot(views[1, g], wv_ref[g, :, 2 * C1 : 3 * C1])
            + dot(views[2, g], wv_ref[g, :, 0:C1])
            + bias
        )
        for q in range(8):
            c = 2 * q + g
            hid_ref[c] = jnp.maximum(inner[q * ny : q * ny + ny, :], 0.0).astype(BF16)
            row = span + 2 * RD * q
            pre0[8 * c : 8 * c + 8, :] = inner[row : row + 8, :]

    proj = proj_ref[...]
    hid0 = dot(pixel_pick(False), jnp.maximum(pre0[...], 0.0).astype(BF16)).astype(BF16)
    first = dot(hid0, proj).astype(BF16)
    first_ref[...] = first
    fold = (dot_nt(first, proj) * (1.0 / 16.0)).astype(BF16)
    mixed = (dot(grad_t_ref[...], hid_ref[...].reshape(WC * ny, C1)) * (1.0 / 16.0)).astype(BF16)
    grad_first = dot(mixed, proj).astype(BF16)
    grad_proj = dot_tn(mixed, first) + dot_tn(hid0, grad_first)
    pre_grad0 = dot(pixel_pick(True), dot_nt(grad_first, proj).astype(BF16))
    pre_grad0 = jnp.where(pre0[...] > 0.0, pre_grad0, 0.0)
    first_grad_ref[...] = pre_grad0.astype(BF16)
    pre0[...] = pre_grad0

    one = identity()
    bias_sum = jnp.sum(pre_grad0, axis=0, keepdims=True)
    zeros8 = jnp.zeros((8, C1), F32)
    all_grads = dot(grad_ref[...].reshape(WC * ny, PIX), fold)
    for g in range(2):
        for q in range(8):
            c = 2 * q + g
            grad = jnp.where(hid_ref[c].astype(F32) > 0.0, all_grads[c * ny : c * ny + ny], 0.0)
            bias_sum = bias_sum + jnp.sum(grad, axis=0, keepdims=True)
            grads[c, 0:ny, :] = grad
            grads[c, ny : ny + 8, :] = zeros8
            rows_out[g, q * ny : q * ny + ny, :] = grad.astype(BF16)
            own_grad = jnp.concatenate([pre_grad0[8 * c : 8 * c + 8], zeros8], axis=0)
            row = span + 2 * RD * q
            rows_out[g, row : row + 2 * RD, :] = own_grad.astype(BF16)
        turned[g] = dot_nt(one, rows_out[g]).astype(BF16)

    first_tops = pre0[pl.ds(0, WC, stride=RD), :]
    for place in range(count):
        device = reverse_bits(place, bits) ^ me
        row = pl.multiple_of(device * RD, RD)
        dest = (kept_ref, sent_ref)[place // (count // 2)]
        group = place // (count // 4) % 2
        at = BLOCK * (place % (count // 4))
        for c in range(0, WC, 2):
            dest[group, at + RD * c : at + RD * c + 2 * RD, :] = jnp.concatenate(
                [grads[c, pl.ds(row, RD), :], grads[c + 1, pl.ds(row, RD), :]], axis=0
            ).astype(BF16)
        for c in range(WC):
            below[c : c + 1, :] = grads[c, pl.ds(row + RD, 1), :]
        dest[group, at + PIX : at + PIX + WC, :] = below[...].astype(BF16)
        dest[group, at + PIX + WC : at + BLOCK, :] = jnp.where(
            device + 1 == me, first_tops, 0.0
        ).astype(BF16)

    parts = [[dot(turned[g], views[kind, g]) for g in range(2)] for kind in range(3)]
    wsum[9 * C0 + 2 * C1 :, :] = jnp.zeros((4 * quarter - 9 * C0 - 2 * C1, C1), F32)
    for tap in range(3):
        left, right = parts[(tap - 1) % 3]
        wsum[tap * 288 : tap * 288 + 288, :] = left.T[32:320] + right.T[96:384]
    wsum[9 * C0 : 9 * C0 + C1, :] = grad_proj[:, 0:C1]
    wsum[9 * C0 + C1 : 9 * C0 + 2 * C1, :] = grad_proj[:, C1:]
    wsum[9 * C0 + 2 * C1 : 9 * C0 + 2 * C1 + 1, :] = bias_sum
    for place in range(4):
        row = pl.multiple_of((place ^ reverse_bits(me & 3, 2)) * quarter, 16)
        dest = (sums_kept_ref, sums_sent_ref)[place // 2]
        dest[place % 2] = wsum[pl.ds(row, quarter), :].astype(BF16)


def main(count, bits, quarter, me, near, far, own, halo, wv, bias, proj_weight, grad, grad_t):
    ny = count * RD
    rows = 8 * ny + PIX
    vmem = pl.BlockSpec(memory_space=pltpu.VMEM)
    pixels, sums = (2, BLOCK * count // 4, C1), (2, quarter, C1)
    return pl.pallas_call(
        functools.partial(main_kernel, count, bits, quarter),
        in_specs=[pl.BlockSpec(memory_space=pltpu.SMEM)] + [vmem] * 9,
        out_shape=(
            jax.ShapeDtypeStruct(pixels, BF16),
            jax.ShapeDtypeStruct(pixels, BF16),
            jax.ShapeDtypeStruct(sums, BF16),
            jax.ShapeDtypeStruct(sums, BF16),
            jax.ShapeDtypeStruct((WC, ny, C1), BF16),
            jax.ShapeDtypeStruct((PIX, C), BF16),
            jax.ShapeDtypeStruct((PIX, C1), BF16),
        ),
        scratch_shapes=[
            pltpu.VMEM((3, 2, rows, WIN), BF16),
            pltpu.VMEM((rows, C1), F32),
            pltpu.VMEM((WC, ny + 8, C1), F32),
            pltpu.VMEM((2, rows, C1), BF16),
            pltpu.VMEM((2, C1, rows), BF16),
            pltpu.VMEM((PIX, C1), F32),
            pltpu.VMEM((WC, C1), F32),
            pltpu.VMEM((4 * quarter, C1), F32),
        ],
        compiler_params=vmem_of(ny),
        cost_estimate=pl.CostEstimate(flops=4 * 10**9, bytes_accessed=6 * 10**6, transcendentals=0),
        name="features",
    )(me, near, far, own, halo, wv, bias, proj_weight, grad, grad_t)


def input_kernel(first_ref, block_ref, wv_ref, out_ref, sides, full):
    last = iota((8, C1), 0) == 7
    grads = [first_ref[...].astype(F32), block_ref[0:PIX, :].astype(F32)]
    border = block_ref[PIX:, :].astype(F32)

    def spread(g):
        here, both = [], []
        for c in range(g, WC, 2):
            for f in range(2):
                own = grads[f][8 * c : 8 * c + 8]
                at = WC * (1 - f) + c
                below = jnp.broadcast_to(border[at : at + 1], (8, C1))
                here.append(own)
                both.append(
                    jnp.concatenate([own, jnp.where(last, below, pltpu.roll(own, 7, 0))], axis=1)
                )
        here = jnp.concatenate(here, axis=0).astype(BF16)
        both = jnp.concatenate(both, axis=0).astype(BF16)
        weights = wv_ref[g]
        outer = jnp.concatenate([weights[:, 2 * C1 : 3 * C1], weights[:, 0:C1]], axis=1)
        return dot_nt(here, weights[:, C1 : 2 * C1]), dot_nt(both, outer)

    even, odd = spread(0), spread(1)
    for parity in range(2):
        for q in range(8):
            sides[parity, :, q * WIN : q * WIN + WIN] = odd[parity][16 * q : 16 * q + 16]
        sides[parity, :, 0:256] += even[parity][0:16, 128:WIN]
        for q in range(1, 8):
            sides[parity, :, q * WIN - 128 : q * WIN + 256] += even[parity][16 * q : 16 * q + 16]
        for f in range(2):
            for j in range(2 * WC * C0 // 128):
                lanes = slice(128 * j, 128 * j + 128)
                full[f, j, pl.ds(parity, 8, stride=2), :] = sides[parity, 8 * f : 8 * f + 8, lanes]
    for f in range(2):
        for j in range(2 * WC * C0 // 128):
            out_ref[f, :, 128 * j : 128 * j + 128] = full[f, j].astype(BF16)


def input_grad(first_grad, block, wv):
    return pl.pallas_call(
        input_kernel,
        out_shape=jax.ShapeDtypeStruct((2, 2 * RD, 2 * WC * C0), BF16),
        scratch_shapes=[
            pltpu.VMEM((2, 2 * RD, 2 * WC * C0), F32),
            pltpu.VMEM((2, 2 * WC * C0 // 128, 2 * RD, 128), F32),
        ],
        compiler_params=vmem_of(0),
        cost_estimate=pl.CostEstimate(flops=10**8, bytes_accessed=10**6, transcendentals=0),
        name="input_grad",
    )(first_grad, block, wv)


def final_kernel(quarter, me_ref, near_ref, far_ref, conv_ref, bias_ref, proj_ref, wsum):
    turned = reverse_bits(me_ref[0] & 3, 2)
    for place in range(4):
        ref = (near_ref, far_ref)[place // 2]
        row = pl.multiple_of((place ^ turned) * quarter, 16)
        wsum[pl.ds(row, quarter), :] = ref[place % 2].astype(F32)
    conv_ref[...] = wsum[0 : 9 * C0, :]
    proj_ref[:, 0:C1] = wsum[9 * C0 : 9 * C0 + C1, :]
    proj_ref[:, C1:] = wsum[9 * C0 + C1 : 9 * C0 + 2 * C1, :]
    bias_ref[...] = wsum[9 * C0 + 2 * C1 : 9 * C0 + 2 * C1 + 1, :]


def final(quarter, me, near, far):
    vmem = pl.BlockSpec(memory_space=pltpu.VMEM)
    return pl.pallas_call(
        functools.partial(final_kernel, quarter),
        in_specs=[pl.BlockSpec(memory_space=pltpu.SMEM), vmem, vmem],
        out_shape=(
            jax.ShapeDtypeStruct((9 * C0, C1), F32),
            jax.ShapeDtypeStruct((1, C1), F32),
            jax.ShapeDtypeStruct((C1, C), F32),
        ),
        scratch_shapes=[pltpu.VMEM((4 * quarter, C1), F32)],
        compiler_params=vmem_of(0),
        name="weight_grads",
    )(me, near, far)


def swap(value, bit, count):
    return lax.ppermute(value, "rows", [(i, i ^ bit) for i in range(count)])


def plus(a, b):
    return (a.astype(F32) + b.astype(F32)).astype(BF16)


def per_device(frames, conv_weight, conv_bias, proj_weight, target_row, target_col, cotangent):
    count = lax.axis_size("rows")
    bits = count.bit_length() - 1
    ny = count * RD
    me_word = lax.axis_index("rows").astype(jnp.int32).reshape(1)
    quarter = -(-(9 * C0 + 2 * C1 + 1) // 64) * 16

    blocks = {0: frames[1]}
    for wave in range(1, bits):
        for mask in reversed(range(2, count, 2)):
            if mask.bit_count() == wave and mask != count - 2:
                bit = mask & -mask
                blocks[mask] = swap(blocks[mask ^ bit], bit, count)
    halo = lax.ppermute(frames[0, 2 * RD - 1 :], "rows", [(i, i + 1) for i in range(count - 1)])
    last = blocks[count - 4]
    target_row, target_col, cotangent, last = lax.optimization_barrier(
        (target_row, target_col, cotangent, last)
    )
    blocks[count - 4] = last
    blocks[count - 2] = swap(last, 2, count)
    grad, grad_t, wv = scatter(ny, target_row, target_col, cotangent, conv_weight)
    near = jnp.concatenate(
        [blocks[2 * reverse_bits(k, bits - 1)] for k in range(count // 2)], axis=0
    )
    near, grad, halo = lax.optimization_barrier((near, grad, halo))
    far = swap(near, 1, count)
    kept, sent, sums_kept, sums_sent, hid, first, first_grad = main(
        count, bits, quarter, me_word, near, far, frames[0], halo, wv,
        conv_bias.reshape(1, C1), proj_weight, grad, grad_t,
    )

    other_sums = swap(sums_sent, 1, count)
    other = swap(sent, 1, count)
    arrived = swap(plus(sums_kept[1], other_sums[1]), 2, count)
    sums = plus(plus(sums_kept[0], other_sums[0]), arrived)
    given = plus(kept[1], other[1])
    pixels = plus(kept[0], other[0])
    given, sums, pixels = lax.optimization_barrier((given, sums, pixels))
    arrived = swap(sums, 4, count)
    pixels_arrived = swap(given, 2, count)
    sums = plus(sums, arrived)
    arrived = None
    lookups = lookup(ny, target_row, target_col, hid, first, proj_weight)
    for bit in range(3, bits):
        sums = plus(sums, swap(sums, 1 << bit, count))
    sums, lookups = lax.optimization_barrier((sums, lookups))
    pixels = plus(pixels, pixels_arrived)
    near = jnp.stack([sums, swap(sums, 2, count)])
    for bit in range(2, bits):
        half = pixels.shape[0] // 2
        other = swap(pixels[half:], 1 << bit, count)
        pixels = plus(pixels[:half], other)
    far = swap(near, 1, count)
    grad_input = input_grad(first_grad, pixels, wv)
    grad_conv, grad_bias, grad_proj = final(quarter, me_word, near, far)
    return lookups, grad_input, grad_conv, grad_bias.reshape(C1), grad_proj


def solution(mesh):
    split = P(None, ("pairs", "rows"))
    return jax.shard_map(
        per_device,
        mesh=mesh,
        in_specs=(P(None, ("pairs", "rows"), None), P(), P(), P(), split, split, split),
        out_specs=(
            split,
            P(None, ("pairs", "rows"), None),
            P("pairs", None),
            P("pairs"),
            P("pairs", None),
        ),
        check_vma=False,
    )
```

time: 82.1 us -> 60.8 us (0.74)
  the two profiles are of different devices: /device:TPU:1 before, /device:TPU:0 now
where the time goes in v3:
time: 60.8 us; the launch traced here: 60.6 us
  starting transfers between devices  23 us (38%)
  waiting for transfers between devices  18.9 us (31%)
  Pallas kernels  14.8 us (24%)
  local copies, waits for them, and re-layouts  2.67 us (4%)
  between operations  0.91 us (1%)
    ppermute x18, starting transfers between devices, swap(): return lax.ppermute(value, 'rows', [(i, i ^ bit) for i in range(count)])  21.8 us
    ppermute x18, waiting for transfers between devices, swap(): return lax.ppermute(value, 'rows', [(i, i ^ bit) for i in range(count)])  18.9 us
    pallas_call x1, Pallas kernels, main(): pl.pallas_call(functools.partial(main_kernel, count, bits, quarter), in_s...  5.41 us
    pallas_call x1, Pallas kernels, scatter(): pl.pallas_call(functools.partial(scatter_kernel, ny), out_shape=(jax.Shap...  3.95 us
    pallas_call x1, Pallas kernels, lookup(): pl.pallas_call(functools.partial(lookup_kernel, ny), out_shape=jax.ShapeD...  3.52 us
    unnamed x21, local copies, waits for them, and re-layouts  1.58 us
    ppermute x1, starting transfers between devices, per_device(): lax.ppermute(frames[0, 2 * RD - 1:], 'rows', [(i, i + 1) for i in range(c...  1.29 us
  transfers between devices with their start and end apart: 19, of which 8 were waited for; matrix products, arithmetic and copies ran while one was open for 0% of the time, Pallas kernels for 14%

profile of v3, /device:TPU:0, one launch (start us, length us, event | category | flops | bytes accessed | tf_op | source)
XLA Modules:
  0.0 60.6 jit_solution(7043403600165842215)
XLA Ops:
  0.7 1.1 %slice_bitcast_fusion = (bf16[16,3072]{1,0:T(8,128)(2,1)S(1)}, bf16[16,3072]{1,0:T(8,128)(2,1)S(1)}) fusion(bf16[2,16,3072]{2,1,0:T(8,128)(2,1)} %param.7), kind=kLoop, calls=%fused_computation.13 | loop fusion | bytes 393216 | tf_op jit(solution)/shard_map/squeeze | solution.py:572
  1.7 3.0 %collective-permute-start.3 = (bf16[16,3072]{1,0:T(8,128)(2,1)S(1)}, bf16[16,3072]{1,0:T(8,128)(2,1)S(1)}, u32[]{:S(2)}, u32[]{:S(2)}) collective-permute-start(bf16[16,3072]{1,0:T(8,128)(2,1)S(1)} %get-tuple-element.58), channel_id=1, source_target_pairs={{0,2},{1,3},{2,0},{3,1},{4,6},{5,7},{6,4},{7,5},{8,10},{9,11},{10,... | collective-permute-start | bytes 294920 | tf_op jit(solution)/shard_map/ppermute | solution.py:538
  4.7 1.6 %collective-permute-start.1 = (bf16[16,3072]{1,0:T(8,128)(2,1)S(1)}, bf16[16,3072]{1,0:T(8,128)(2,1)S(1)}, u32[]{:S(2)}, u32[]{:S(2)}) collective-permute-start(bf16[16,3072]{1,0:T(8,128)(2,1)S(1)} %get-tuple-element.58), channel_id=1, source_target_pairs={{0,4},{1,5},{2,6},{3,7},{4,0},{5,1},{6,2},{7,3},{8,12},{9,13},{10,... | collective-permute-start | bytes 294920 | tf_op jit(solution)/shard_map/ppermute | solution.py:538
  6.3 2.6 %collective-permute-start = (bf16[16,3072]{1,0:T(8,128)(2,1)S(1)}, bf16[16,3072]{1,0:T(8,128)(2,1)S(1)}, u32[]{:S(2)}, u32[]{:S(2)}) collective-permute-start(bf16[16,3072]{1,0:T(8,128)(2,1)S(1)} %get-tuple-element.58), channel_id=1, source_target_pairs={{0,8},{1,9},{2,10},{3,11},{4,12},{5,13},{6,14},{7,15},{8,0},{9,1},... | collective-permute-start | bytes 294920 | tf_op jit(solution)/shard_map/ppermute | solution.py:538
  8.9 1.3 %collective-permute-start.7 = (bf16[1,3072]{1,0:T(2,128)(2,1)S(1)}, bf16[1,3072]{1,0:T(2,128)(2,1)S(1)}, u32[]{:S(2)}, u32[]{:S(2)}) collective-permute-start(bf16[1,3072]{1,0:T(2,128)(2,1)S(1)} %slice_bitcast_fusion.2), channel_id=1, source_target_pairs={{0,1},{1,2},{2,3},{3,4},{4,5},{5,6},{6,7},{7,8},{8,9},{9,10},{10,1... | collective-permute-start | bytes 18440 | tf_op jit(solution)/shard_map/ppermute | solution.py:558
  10.2 3.1 %collective-permute-done = bf16[16,3072]{1,0:T(8,128)(2,1)S(1)} collective-permute-done((bf16[16,3072]{1,0:T(8,128)(2,1)S(1)}, bf16[16,3072]{1,0:T(8,128)(2,1)S(1)}, u32[]{:S(2)}, u32[]{:S(2)}) %collective-permute-start) | collective-permute-done | bytes 98336 | tf_op jit(solution)/shard_map/ppermute | solution.py:538
  13.3 0.5 collective-permute-start.4
  13.8 0.4 collective-permute-start.2
  14.2 1.5 %collective-permute-start.5 = (bf16[16,3072]{1,0:T(8,128)(2,1)S(1)}, bf16[16,3072]{1,0:T(8,128)(2,1)S(1)}, u32[]{:S(2)}, u32[]{:S(2)}) collective-permute-start(bf16[16,3072]{1,0:T(8,128)(2,1)S(1)} %collective-permute-done.1), channel_id=1, source_target_pairs={{0,2},{1,3},{2,0},{3,1},{4,6},{5,7},{6,4},{7,5},{8,10},{9,11},{10,... | collective-permute-start | bytes 294920 | tf_op jit(solution)/shard_map/ppermute | solution.py:538
  15.7 2.7 %collective-permute-done.2 = bf16[16,3072]{1,0:T(8,128)(2,1)S(1)} collective-permute-done((bf16[16,3072]{1,0:T(8,128)(2,1)S(1)}, bf16[16,3072]{1,0:T(8,128)(2,1)S(1)}, u32[]{:S(2)}, u32[]{:S(2)}) %collective-permute-start.2) | collective-permute-done | bytes 98336 | tf_op jit(solution)/shard_map/ppermute | solution.py:538
  18.4 1.5 %collective-permute-start.6 = (bf16[16,3072]{1,0:T(8,128)(2,1)S(1)}, bf16[16,3072]{1,0:T(8,128)(2,1)S(1)}, u32[]{:S(2)}, u32[]{:S(2)}) collective-permute-start(bf16[16,3072]{1,0:T(8,128)(2,1)S(1)} %collective-permute-done.2), channel_id=1, source_target_pairs={{0,2},{1,3},{2,0},{3,1},{4,6},{5,7},{6,4},{7,5},{8,10},{9,11},{10,... | collective-permute-start | bytes 294920 | tf_op jit(solution)/shard_map/ppermute | solution.py:538
  20.1 0.8 %copy-done.1 = bf16[864,128]{1,0:T(8,128)(2,1)S(1)} copy-done((bf16[864,128]{1,0:T(8,128)(2,1)S(1)}, bf16[864,128]{1,0:T(8,128)(2,1)}, u32[]{:S(2)}) %copy-start.1) | copy-done | bytes 221208
  20.9 4.0 %scatter.1 = (bf16[16,128,128]{2,1,0:T(8,128)(2,1)S(1)}, bf16[128,2048]{1,0:T(8,128)(2,1)S(1)}, bf16[2,384,384]{2,1,0:T(8,128)(2,1)S(1)}) custom-call(s32[12,128]{1,0:T(8,128)S(1)} %copy-done.3, s32[12,128]{1,0:T(8,128)S(1)} %copy-done.4, bf16[3888,128]{1,0:T(8,128)(2,1)S(1)} %copy-done, bf16[864,128]{1,0:T(8,128)(2,1)S(1)} %copy-done.1), custom_call_target="tpu_custom_call" | custom-call | flops 1000000000 | bytes 4000000 | tf_op jit(solution)/shard_map/scatter/pallas_call | solution.py:163
  25.0 2.3 %collective-permute-done.8.far_ref = bf16[128,3072]{1,0:T(8,128)(2,1)S(1)} collective-permute-done((bf16[128,3072]{1,0:T(8,128)(2,1)S(1)}, bf16[128,3072]{1,0:T(8,128)(2,1)S(1)}, u32[]{:S(2)}, u32[]{:S(2)}) %collective-permute-start.8) | collective-permute-done | bytes 786464 | tf_op jit(solution)/shard_map/ppermute | solution.py:538
  27.3 0.7 %copy-done.5 = f32[128]{0:T(128)S(1)} copy-done((f32[128]{0:T(128)S(1)}, f32[128]{0:T(128)}, u32[]{:S(2)}) %copy-start.5) | copy-done | bytes 536
  28.0 5.4 %features.1 = (bf16[2,640,128]{2,1,0:T(8,128)(2,1)S(1)}, bf16[2,640,128]{2,1,0:T(8,128)(2,1)S(1)}, bf16[2,288,128]{2,1,0:T(8,128)(2,1)S(1)}, bf16[2,288,128]{2,1...) custom-call(s32[1]{0:T(128)} %bitcast.me_ref, ...), custom_call_target="tpu_custom_call" | custom-call | flops 4000000000 | bytes 6000000 | tf_op jit(solution)/shard_map/features/pallas_call | solution.py:429
  33.6 0.4 collective-permute-start.9
  34.0 0.9 %collective-permute-done.10 = bf16[2,288,128]{2,1,0:T(8,128)(2,1)S(1)} collective-permute-done((bf16[2,288,128]{2,1,0:T(8,128)(2,1)S(1)}, bf16[2,288,128]{2,1,0:T(8,128)(2,1)S(1)}, u32[]{:S(2)}, u32[]{:S(2)}) %collective-permute-start.10) | collective-permute-done | bytes 147488 | tf_op jit(solution)/shard_map/ppermute | solution.py:538
  34.8 0.6 collective-permute-start.11
  35.4 3.8 %collective-permute-done.11 = bf16[288,128]{1,0:T(8,128)(2,1)S(1)} collective-permute-done((bf16[288,128]{1,0:T(8,128)(2,1)S(1)}, bf16[288,128]{1,0:T(8,128)(2,1)S(1)}, u32[]{:S(2)}, u32[]{:S(2)}) %collective-permute-start.11) | collective-permute-done | bytes 73760 | tf_op jit(solution)/shard_map/ppermute | solution.py:538
  39.4 0.5 collective-permute-start.12
  39.9 3.5 %lookup.1 = bf16[3888,128]{1,0:T(8,128)(2,1)} custom-call(s32[12,128]{1,0:T(8,128)S(1)} %copy-done.3, s32[12,128]{1,0:T(8,128)S(1)} %copy-done.4, bf16[16,128,128]{2,1,0:T(8,128)(2,1)S(1)} %get-tuple-element.45.hid_ref, bf16[128,256]{1,0:T(8,128)(2,1)S(1)} %get-tuple-element.46.first_ref, bf16[128,256]{1,0:T(8,128)(2,1)S(1)} %copy-done.2), custom_call_target="tpu_custom_call" | custom-call | flops 1000000000 | bytes 4000000 | tf_op jit(solution)/shard_map/lookup/pallas_call | solution.py:260
  43.4 0.8 %collective-permute-start.14 = (bf16[640,128]{1,0:T(8,128)(2,1)S(1)}, bf16[640,128]{1,0:T(8,128)(2,1)S(1)}, u32[]{:S(2)}, u32[]{:S(2)}) collective-permute-start(bf16[640,128]{1,0:T(8,128)(2,1)S(1)} %get-tuple-element.50), channel_id=1, source_target_pairs={{0,2},{1,3},{2,0},{3,1},{4,6},{5,7},{6,4},{7,5},{8,10},{9,11},{10,... | collective-permute-start | bytes 491528 | tf_op jit(solution)/shard_map/ppermute | solution.py:538
  44.2 2.6 %collective-permute-start.13 = (bf16[288,128]{1,0:T(8,128)(2,1)S(1)}, bf16[288,128]{1,0:T(8,128)(2,1)S(1)}, u32[]{:S(2)}, u32[]{:S(2)}) collective-permute-start(bf16[288,128]{1,0:T(8,128)(2,1)S(1)} %add_convert_fusion.5), channel_id=1, source_target_pairs={{0,8},{1,9},{2,10},{3,11},{4,12},{5,13},{6,14},{7,15},{8,0},{9,1},... | collective-permute-start | bytes 221192 | tf_op jit(solution)/shard_map/ppermute | solution.py:538
  46.8 2.0 %collective-permute-done.14 = bf16[640,128]{1,0:T(8,128)(2,1)S(1)} collective-permute-done((bf16[640,128]{1,0:T(8,128)(2,1)S(1)}, bf16[640,128]{1,0:T(8,128)(2,1)S(1)}, u32[]{:S(2)}, u32[]{:S(2)}) %collective-permute-start.14) | collective-permute-done | bytes 163872 | tf_op jit(solution)/shard_map/ppermute | solution.py:538
  48.9 1.7 %collective-permute-start.15 = (bf16[320,128]{1,0:T(8,128)(2,1)S(1)}, bf16[320,128]{1,0:T(8,128)(2,1)S(1)}, u32[]{:S(2)}, u32[]{:S(2)}) collective-permute-start(bf16[320,128]{1,0:T(8,128)(2,1)S(1)} %slice.65), channel_id=1, source_target_pairs={{0,4},{1,5},{2,6},{3,7},{4,0},{5,1},{6,2},{7,3},{8,12},{9,13},{10,... | collective-permute-start | bytes 245768 | tf_op jit(solution)/shard_map/ppermute | solution.py:538
  50.6 0.6 collective-permute-start.17
  51.1 2.2 %collective-permute-done.15 = bf16[320,128]{1,0:T(8,128)(2,1)S(1)} collective-permute-done((bf16[320,128]{1,0:T(8,128)(2,1)S(1)}, bf16[320,128]{1,0:T(8,128)(2,1)S(1)}, u32[]{:S(2)}, u32[]{:S(2)}) %collective-permute-start.15) | collective-permute-done | bytes 81952 | tf_op jit(solution)/shard_map/ppermute | solution.py:538
  53.4 3.3 %collective-permute-start.16 = (bf16[160,128]{1,0:T(8,128)(2,1)S(1)}, bf16[160,128]{1,0:T(8,128)(2,1)S(1)}, u32[]{:S(2)}, u32[]{:S(2)}) collective-permute-start(bf16[160,128]{1,0:T(8,128)(2,1)S(1)} %slice.67), channel_id=1, source_target_pairs={{0,8},{1,9},{2,10},{3,11},{4,12},{5,13},{6,14},{7,15},{8,0},{9,1},... | collective-permute-start | bytes 122888 | tf_op jit(solution)/shard_map/ppermute | solution.py:538
  56.8 1.9 %collective-permute-done.16 = bf16[160,128]{1,0:T(8,128)(2,1)S(1)} collective-permute-done((bf16[160,128]{1,0:T(8,128)(2,1)S(1)}, bf16[160,128]{1,0:T(8,128)(2,1)S(1)}, u32[]{:S(2)}, u32[]{:S(2)}) %collective-permute-start.16) | collective-permute-done | bytes 40992 | tf_op jit(solution)/shard_map/ppermute | solution.py:538
  58.7 1.0 %input_grad.1 = bf16[2,16,3072]{2,1,0:T(8,128)(2,1)} custom-call(bf16[128,128]{1,0:T(8,128)(2,1)S(1)} %get-tuple-element.48.first_ref, bf16[160,128]{1,0:T(8,128)(2,1)S(1)} %add_convert_fusion.8.block_ref, bf16[2,384,384]{2,1,0:T(8,128)(2,1)S(1)} %get-tuple-element.37.wv_ref), custom_call_target="tpu_custom_call" | custom-call | flops 100000000 | bytes 1000000 | tf_op jit(solution)/shard_map/input_grad/pallas_call | solution.py:496
  59.7 0.9 %weight_grads.1 = (f32[864,128]{1,0:T(8,128)}, f32[1,128]{1,0:T(1,128)}, f32[128,256]{1,0:T(8,128)}) custom-call(s32[1]{0:T(128)} %bitcast.me_ref, bf16[2,288,128]{2,1,0:T(8,128)(2,1)S(1)} %pad_maximum_fusion.near_ref, bf16[2,288,128]{2,1,0:T(8,128)(2,1)S(1)} %collective-permute-done.18.far_ref), custom_call_target="tpu_custom_call" | custom-call | tf_op jit(solution)/shard_map/weight_grads/pallas_call | solution.py:523
  (46 shorter events, 0.8 us)
Async XLA Ops:
  0.6 8.3 %copy-start.6 = (bf16[2,16,3072]{2,1,0:T(8,128)(2,1)S(1)}, bf16[2,16,3072]{2,1,0:T(8,128)(2,1)}, u32[]{:S(2)}) copy-start(bf16[2,16,3072]{2,1,0:T(8,128)(2,1)} %param.7) | copy-start | bytes 589828
  0.6 19.4 %copy-start = (bf16[3888,128]{1,0:T(8,128)(2,1)S(1)}, bf16[3888,128]{1,0:T(8,128)(2,1)}, u32[]{:S(2)}) copy-start(bf16[3888,128]{1,0:T(8,128)(2,1)} %cot_hbm) | copy-start | bytes 2985988
  1.7 18.3 %collective-permute-start.3 = (bf16[16,3072]{1,0:T(8,128)(2,1)S(1)}, bf16[16,3072]{1,0:T(8,128)(2,1)S(1)}, u32[]{:S(2)}, u32[]{:S(2)}) collective-permute-start(bf16[16,3072]{1,0:T(8,128)(2,1)S(1)} %get-tuple-element.58), channel_id=1, source_target_pairs={{0,2},{1,3},{2,0},{3,1},{4,6},{5,7},{6,4},{7,5},{8,10},{9,11},{10,... | collective-permute-start | bytes 294920 | tf_op jit(solution)/shard_map/ppermute | solution.py:538
  4.7 9.5 %collective-permute-start.1 = (bf16[16,3072]{1,0:T(8,128)(2,1)S(1)}, bf16[16,3072]{1,0:T(8,128)(2,1)S(1)}, u32[]{:S(2)}, u32[]{:S(2)}) collective-permute-start(bf16[16,3072]{1,0:T(8,128)(2,1)S(1)} %get-tuple-element.58), channel_id=1, source_target_pairs={{0,4},{1,5},{2,6},{3,7},{4,0},{5,1},{6,2},{7,3},{8,12},{9,13},{10,... | collective-permute-start | bytes 294920 | tf_op jit(solution)/shard_map/ppermute | solution.py:538
  6.3 7.0 %collective-permute-start = (bf16[16,3072]{1,0:T(8,128)(2,1)S(1)}, bf16[16,3072]{1,0:T(8,128)(2,1)S(1)}, u32[]{:S(2)}, u32[]{:S(2)}) collective-permute-start(bf16[16,3072]{1,0:T(8,128)(2,1)S(1)} %get-tuple-element.58), channel_id=1, source_target_pairs={{0,8},{1,9},{2,10},{3,11},{4,12},{5,13},{6,14},{7,15},{8,0},{9,1},... | collective-permute-start | bytes 294920 | tf_op jit(solution)/shard_map/ppermute | solution.py:538
  8.9 16.0 %collective-permute-start.7 = (bf16[1,3072]{1,0:T(2,128)(2,1)S(1)}, bf16[1,3072]{1,0:T(2,128)(2,1)S(1)}, u32[]{:S(2)}, u32[]{:S(2)}) collective-permute-start(bf16[1,3072]{1,0:T(2,128)(2,1)S(1)} %slice_bitcast_fusion.2), channel_id=1, source_target_pairs={{0,1},{1,2},{2,3},{3,4},{4,5},{5,6},{6,7},{7,8},{8,9},{9,10},{10,1... | collective-permute-start | bytes 18440 | tf_op jit(solution)/shard_map/ppermute | solution.py:558
  13.3 6.7 %collective-permute-start.4 = (bf16[16,3072]{1,0:T(8,128)(2,1)S(1)}, bf16[16,3072]{1,0:T(8,128)(2,1)S(1)}, u32[]{:S(2)}, u32[]{:S(2)}) collective-permute-start(bf16[16,3072]{1,0:T(8,128)(2,1)S(1)} %collective-permute-done), channel_id=1, source_target_pairs={{0,2},{1,3},{2,0},{3,1},{4,6},{5,7},{6,4},{7,5},{8,10},{9,11},{10,... | collective-permute-start | bytes 294920 | tf_op jit(solution)/shard_map/ppermute | solution.py:538
  13.8 4.6 %collective-permute-start.2 = (bf16[16,3072]{1,0:T(8,128)(2,1)S(1)}, bf16[16,3072]{1,0:T(8,128)(2,1)S(1)}, u32[]{:S(2)}, u32[]{:S(2)}) collective-permute-start(bf16[16,3072]{1,0:T(8,128)(2,1)S(1)} %collective-permute-done), channel_id=1, source_target_pairs={{0,4},{1,5},{2,6},{3,7},{4,0},{5,1},{6,2},{7,3},{8,12},{9,13},{10,... | collective-permute-start | bytes 294920 | tf_op jit(solution)/shard_map/ppermute | solution.py:538
  14.2 5.9 %collective-permute-start.5 = (bf16[16,3072]{1,0:T(8,128)(2,1)S(1)}, bf16[16,3072]{1,0:T(8,128)(2,1)S(1)}, u32[]{:S(2)}, u32[]{:S(2)}) collective-permute-start(bf16[16,3072]{1,0:T(8,128)(2,1)S(1)} %collective-permute-done.1), channel_id=1, source_target_pairs={{0,2},{1,3},{2,0},{3,1},{4,6},{5,7},{6,4},{7,5},{8,10},{9,11},{10,... | collective-permute-start | bytes 294920 | tf_op jit(solution)/shard_map/ppermute | solution.py:538
  18.4 6.5 %collective-permute-start.6 = (bf16[16,3072]{1,0:T(8,128)(2,1)S(1)}, bf16[16,3072]{1,0:T(8,128)(2,1)S(1)}, u32[]{:S(2)}, u32[]{:S(2)}) collective-permute-start(bf16[16,3072]{1,0:T(8,128)(2,1)S(1)} %collective-permute-done.2), channel_id=1, source_target_pairs={{0,2},{1,3},{2,0},{3,1},{4,6},{5,7},{6,4},{7,5},{8,10},{9,11},{10,... | collective-permute-start | bytes 294920 | tf_op jit(solution)/shard_map/ppermute | solution.py:538
  20.0 0.9 %copy-start.1 = (bf16[864,128]{1,0:T(8,128)(2,1)S(1)}, bf16[864,128]{1,0:T(8,128)(2,1)}, u32[]{:S(2)}) copy-start(bf16[864,128]{1,0:T(8,128)(2,1)} %w_ref.1) | copy-start | bytes 663556
  20.0 0.9 %copy-start.3 = (s32[12,128]{1,0:T(8,128)S(1)}, s32[12,128]{1,0:T(8,128)}, u32[]{:S(2)}) copy-start(s32[12,128]{1,0:T(8,128)} %row_ref.1) | copy-start | bytes 18436
  20.0 0.9 %copy-start.4 = (s32[12,128]{1,0:T(8,128)S(1)}, s32[12,128]{1,0:T(8,128)}, u32[]{:S(2)}) copy-start(s32[12,128]{1,0:T(8,128)} %col_ref.1) | copy-start | bytes 18436
  24.9 2.4 %copy-start.2 = (bf16[128,256]{1,0:T(8,128)(2,1)S(1)}, bf16[128,256]{1,0:T(8,128)(2,1)}, u32[]{:S(2)}) copy-start(bf16[128,256]{1,0:T(8,128)(2,1)} %proj_ref.3) | copy-start | bytes 196612
  25.0 2.4 %collective-permute-start.8 = (bf16[128,3072]{1,0:T(8,128)(2,1)S(1)}, bf16[128,3072]{1,0:T(8,128)(2,1)S(1)}, u32[]{:S(2)}, u32[]{:S(2)}) collective-permute-start(bf16[128,3072]{1,0:T(8,128)(2,1)S(1)} %constant_dynamic-update-slice_fusion.near_ref), channel_id=1, source_target_pairs={{0,1},{1,0},{2,3},{3,2},{4,5},{5,4},{6,7},{7,6},{8,9},{9,8},{10,11... | collective-permute-start | bytes 2359304 | tf_op jit(solution)/shard_map/ppermute | solution.py:538
  27.3 0.7 %copy-start.5 = (f32[128]{0:T(128)S(1)}, f32[128]{0:T(128)}, u32[]{:S(2)}) copy-start(f32[128]{0:T(128)} %param.9) | copy-start | bytes 1540
  33.4 1.4 %collective-permute-start.10 = (bf16[2,288,128]{2,1,0:T(8,128)(2,1)S(1)}, bf16[2,288,128]{2,1,0:T(8,128)(2,1)S(1)}, u32[]{:S(2)}, u32[]{:S(2)}) collective-permute-start(bf16[2,288,128]{2,1,0:T(8,128)(2,1)S(1)} %get-tuple-element.43), channel_id=1, source_target_pairs={{0,1},{1,0},{2,3},{3,2},{4,5},{5,4},{6,7},{7,6},{8,9},{9,8},{10,11... | collective-permute-start | bytes 442376 | tf_op jit(solution)/shard_map/ppermute | solution.py:538
  33.6 5.7 %collective-permute-start.9 = (bf16[2,640,128]{2,1,0:T(8,128)(2,1)S(1)}, bf16[2,640,128]{2,1,0:T(8,128)(2,1)S(1)}, u32[]{:S(2)}, u32[]{:S(2)}) collective-permute-start(bf16[2,640,128]{2,1,0:T(8,128)(2,1)S(1)} %get-tuple-element.41), channel_id=1, source_target_pairs={{0,1},{1,0},{2,3},{3,2},{4,5},{5,4},{6,7},{7,6},{8,9},{9,8},{10,11... | collective-permute-start | bytes 983048 | tf_op jit(solution)/shard_map/ppermute | solution.py:538
  34.8 4.4 %collective-permute-start.11 = (bf16[288,128]{1,0:T(8,128)(2,1)S(1)}, bf16[288,128]{1,0:T(8,128)(2,1)S(1)}, u32[]{:S(2)}, u32[]{:S(2)}) collective-permute-start(bf16[288,128]{1,0:T(8,128)(2,1)S(1)} %fusion.4), channel_id=1, source_target_pairs={{0,2},{1,3},{2,0},{3,1},{4,6},{5,7},{6,4},{7,5},{8,10},{9,11},{10,... | collective-permute-start | bytes 221192 | tf_op jit(solution)/shard_map/ppermute | solution.py:538
  39.4 4.8 %collective-permute-start.12 = (bf16[288,128]{1,0:T(8,128)(2,1)S(1)}, bf16[288,128]{1,0:T(8,128)(2,1)S(1)}, u32[]{:S(2)}, u32[]{:S(2)}) collective-permute-start(bf16[288,128]{1,0:T(8,128)(2,1)S(1)} %fusion.2), channel_id=1, source_target_pairs={{0,4},{1,5},{2,6},{3,7},{4,0},{5,1},{6,2},{7,3},{8,12},{9,13},{10,... | collective-permute-start | bytes 221192 | tf_op jit(solution)/shard_map/ppermute | solution.py:538
  43.4 5.4 %collective-permute-start.14 = (bf16[640,128]{1,0:T(8,128)(2,1)S(1)}, bf16[640,128]{1,0:T(8,128)(2,1)S(1)}, u32[]{:S(2)}, u32[]{:S(2)}) collective-permute-start(bf16[640,128]{1,0:T(8,128)(2,1)S(1)} %get-tuple-element.50), channel_id=1, source_target_pairs={{0,2},{1,3},{2,0},{3,1},{4,6},{5,7},{6,4},{7,5},{8,10},{9,11},{10,... | collective-permute-start | bytes 491528 | tf_op jit(solution)/shard_map/ppermute | solution.py:538
  44.2 6.3 %collective-permute-start.13 = (bf16[288,128]{1,0:T(8,128)(2,1)S(1)}, bf16[288,128]{1,0:T(8,128)(2,1)S(1)}, u32[]{:S(2)}, u32[]{:S(2)}) collective-permute-start(bf16[288,128]{1,0:T(8,128)(2,1)S(1)} %add_convert_fusion.5), channel_id=1, source_target_pairs={{0,8},{1,9},{2,10},{3,11},{4,12},{5,13},{6,14},{7,15},{8,0},{9,1},... | collective-permute-start | bytes 221192 | tf_op jit(solution)/shard_map/ppermute | solution.py:538
  48.9 4.5 %collective-permute-start.15 = (bf16[320,128]{1,0:T(8,128)(2,1)S(1)}, bf16[320,128]{1,0:T(8,128)(2,1)S(1)}, u32[]{:S(2)}, u32[]{:S(2)}) collective-permute-start(bf16[320,128]{1,0:T(8,128)(2,1)S(1)} %slice.65), channel_id=1, source_target_pairs={{0,4},{1,5},{2,6},{3,7},{4,0},{5,1},{6,2},{7,3},{8,12},{9,13},{10,... | collective-permute-start | bytes 245768 | tf_op jit(solution)/shard_map/ppermute | solution.py:538
  50.6 6.1 %collective-permute-start.17 = (bf16[288,128]{1,0:T(8,128)(2,1)S(1)}, bf16[288,128]{1,0:T(8,128)(2,1)S(1)}, u32[]{:S(2)}, u32[]{:S(2)}) collective-permute-start(bf16[288,128]{1,0:T(8,128)(2,1)S(1)} %add_convert_fusion.4), channel_id=1, source_target_pairs={{0,2},{1,3},{2,0},{3,1},{4,6},{5,7},{6,4},{7,5},{8,10},{9,11},{10,... | collective-permute-start | bytes 221192 | tf_op jit(solution)/shard_map/ppermute | solution.py:538
  53.4 5.3 %collective-permute-start.16 = (bf16[160,128]{1,0:T(8,128)(2,1)S(1)}, bf16[160,128]{1,0:T(8,128)(2,1)S(1)}, u32[]{:S(2)}, u32[]{:S(2)}) collective-permute-start(bf16[160,128]{1,0:T(8,128)(2,1)S(1)} %slice.67), channel_id=1, source_target_pairs={{0,8},{1,9},{2,10},{3,11},{4,12},{5,13},{6,14},{7,15},{8,0},{9,1},... | collective-permute-start | bytes 122888 | tf_op jit(solution)/shard_map/ppermute | solution.py:538
  56.7 3.0 %collective-permute-start.18 = (bf16[2,288,128]{2,1,0:T(8,128)(2,1)S(1)}, bf16[2,288,128]{2,1,0:T(8,128)(2,1)S(1)}, u32[]{:S(2)}, u32[]{:S(2)}) collective-permute-start(bf16[2,288,128]{2,1,0:T(8,128)(2,1)S(1)} %pad_maximum_fusion.near_ref), channel_id=1, source_target_pairs={{0,1},{1,0},{2,3},{3,2},{4,5},{5,4},{6,7},{7,6},{8,9},{9,8},{10,11... | collective-permute-start | bytes 442376 | tf_op jit(solution)/shard_map/ppermute | solution.py:538

commit v4 on v3

--- a/solution.py
+++ b/solution.py
@@ -97,7 +97,7 @@
     return values
 
 def scatter_kernel(
-    ny, row_ref, col_ref, cot_hbm, w_ref, grad_ref, grad_t_ref, wv_ref, cot_in, cot, packed, sems, *sums
+    ny, row_ref, col_ref, cot_hbm, grad_ref, grad_t_ref, cot_in, cot, packed, sems, *sums
 ):
     sub = iota((8, PIX), 0)
     loads = [
@@ -108,13 +108,6 @@
         load.start()
     for level in range(LEVELS):
         sums[level][...] = jnp.zeros(sums[level].shape, F32)
-    wv_ref[...] = jnp.zeros(wv_ref.shape, BF16)
-    for tap in range(3):
-        lanes = slice(tap * C1, tap * C1 + C1)
-        rows = w_ref[tap * 288 : tap * 288 + 288, :]
-        wv_ref[0, 32:320, lanes] = rows
-        wv_ref[1, 96:384, lanes] = rows
-
     def step(t, carry):
         row_all, col_all = lane_row(row_ref, t), lane_row(col_ref, t)
         for level in range(LEVELS):
@@ -158,16 +151,15 @@
         grad_ref[v] = (sums[0][v] + added[:, lanes]).astype(BF16)
     grad_t_ref[...] = dot_nt(identity(), grad_ref[...].reshape(WC * ny, PIX)).astype(BF16)
 
-def scatter(ny, target_row, target_col, cotangent, conv_weight):
+def scatter(ny, target_row, target_col, cotangent):
     vmem = pl.BlockSpec(memory_space=pltpu.VMEM)
     return pl.pallas_call(
         functools.partial(scatter_kernel, ny),
         out_shape=(
             jax.ShapeDtypeStruct((WC, ny, PIX), BF16),
             jax.ShapeDtypeStruct((PIX, WC * ny), BF16),
-            jax.ShapeDtypeStruct((2, WIN, WIN), BF16),
         ),
-        in_specs=[vmem, vmem, pl.BlockSpec(memory_space=pl.ANY), vmem],
+        in_specs=[vmem, vmem, pl.BlockSpec(memory_space=pl.ANY)],
         scratch_shapes=[
             pltpu.VMEM((LOOKS, PIX), BF16),
             pltpu.VMEM((LOOKS, PIX), F32),
@@ -178,7 +170,33 @@
         compiler_params=vmem_of(ny),
         cost_estimate=pl.CostEstimate(flops=10**9, bytes_accessed=4 * 10**6, transcendentals=0),
         name="scatter",
-    )(target_row, target_col, cotangent, conv_weight)
+    )(target_row, target_col, cotangent)
+
+def prepare_kernel(row_ref, col_ref, w_ref, bias_ref, proj_ref, row_out, col_out, wv_ref, bias_out, proj_out):
+    row_out[...] = row_ref[...]
+    col_out[...] = col_ref[...]
+    bias_out[...] = bias_ref[...]
+    proj_out[...] = proj_ref[...]
+    wv_ref[...] = jnp.zeros(wv_ref.shape, BF16)
+    for tap in range(3):
+        lanes = slice(tap * C1, tap * C1 + C1)
+        rows = w_ref[tap * 288 : tap * 288 + 288, :]
+        wv_ref[0, 32:320, lanes] = rows
+        wv_ref[1, 96:384, lanes] = rows
+
+
+def prepare(target_row, target_col, conv_weight, conv_bias, proj_weight):
+    same = [jax.ShapeDtypeStruct(a.shape, a.dtype) for a in (target_row, conv_bias, proj_weight)]
+    return pl.pallas_call(
+        prepare_kernel,
+        out_shape=(
+            same[0], same[0], jax.ShapeDtypeStruct((2, WIN, WIN), BF16), same[1], same[2]
+        ),
+        compiler_params=vmem_of(0),
+        cost_estimate=pl.CostEstimate(flops=10**6, bytes_accessed=10**6, transcendentals=0),
+        name="prepare",
+    )(target_row, target_col, conv_weight, conv_bias, proj_weight)
+
 
 def lookup_kernel(
     ny, row_ref, col_ref, hid_ref, first_ref, proj_ref, out_hbm, looked, out, second, wide, pooled,
@@ -549,51 +567,52 @@
     me_word = lax.axis_index("rows").astype(jnp.int32).reshape(1)
     quarter = -(-(9 * C0 + 2 * C1 + 1) // 64) * 16
 
-    blocks = {0: frames[1]}
-    for wave in range(1, bits):
-        for mask in reversed(range(2, count, 2)):
-            if mask.bit_count() == wave and mask != count - 2:
-                bit = mask & -mask
-                blocks[mask] = swap(blocks[mask ^ bit], bit, count)
     halo = lax.ppermute(frames[0, 2 * RD - 1 :], "rows", [(i, i + 1) for i in range(count - 1)])
-    last = blocks[count - 4]
-    target_row, target_col, cotangent, last = lax.optimization_barrier(
-        (target_row, target_col, cotangent, last)
+    target_row, target_col, wv, conv_bias, proj_weight = prepare(
+        target_row, target_col, conv_weight, conv_bias.reshape(1, C1), proj_weight
     )
-    blocks[count - 4] = last
-    blocks[count - 2] = swap(last, 2, count)
-    grad, grad_t, wv = scatter(ny, target_row, target_col, cotangent, conv_weight)
-    near = jnp.concatenate(
-        [blocks[2 * reverse_bits(k, bits - 1)] for k in range(count // 2)], axis=0
+    own = [frames[1]]
+    for bit in reversed(range(3, bits)):
+        own = own + [swap(block, 1 << bit, count) for block in own]
+    across = [swap(own[0], 4, count)]
+    own[-1], target_row, target_col, wv, conv_bias, proj_weight = lax.optimization_barrier(
+        (own[-1], target_row, target_col, wv, conv_bias, proj_weight)
     )
+    across = across + [swap(block, 4, count) for block in own[1:]]
+    own = jnp.concatenate(own, axis=0)
+    own_far = swap(own, 2, count)
+    across = jnp.concatenate(across, axis=0)
+    target_row, target_col, cotangent, across = lax.optimization_barrier(
+        (target_row, target_col, cotangent, across)
+    )
+    across_far = swap(across, 2, count)
+    grad, grad_t = scatter(ny, target_row, target_col, cotangent)
+    near = jnp.concatenate([own, across, own_far, across_far], axis=0)
     near, grad, halo = lax.optimization_barrier((near, grad, halo))
     far = swap(near, 1, count)
     kept, sent, sums_kept, sums_sent, hid, first, first_grad = main(
         count, bits, quarter, me_word, near, far, frames[0], halo, wv,
-        conv_bias.reshape(1, C1), proj_weight, grad, grad_t,
+        conv_bias, proj_weight, grad, grad_t,
     )
 
     other_sums = swap(sums_sent, 1, count)
     other = swap(sent, 1, count)
-    arrived = swap(plus(sums_kept[1], other_sums[1]), 2, count)
-    sums = plus(plus(sums_kept[0], other_sums[0]), arrived)
-    given = plus(kept[1], other[1])
-    pixels = plus(kept[0], other[0])
-    given, sums, pixels = lax.optimization_barrier((given, sums, pixels))
-    arrived = swap(sums, 4, count)
-    pixels_arrived = swap(given, 2, count)
-    sums = plus(sums, arrived)
-    arrived = None
-    lookups = lookup(ny, target_row, target_col, hid, first, proj_weight)
-    for bit in range(3, bits):
+    given_sums, sums = plus(sums_kept[1], other_sums[1]), plus(sums_kept[0], other_sums[0])
+    given, pixels = plus(kept[1], other[1]), plus(kept[0], other[0])
+    given_sums, given = lax.optimization_barrier((given_sums, given))
+    sums = plus(sums, swap(given_sums, 2, count))
+    pixels = plus(pixels, swap(given, 2, count))
+    for bit in range(2, bits):
         sums = plus(sums, swap(sums, 1 << bit, count))
-    sums, lookups = lax.optimization_barrier((sums, lookups))
-    pixels = plus(pixels, pixels_arrived)
+        if bit < bits - 1:
+            sums, pixels, target_row = lax.optimization_barrier((sums, pixels, target_row))
+        else:
+            lookups = lookup(ny, target_row, target_col, hid, first, proj_weight)
+            sums, pixels, lookups = lax.optimization_barrier((sums, pixels, lookups))
+        half = pixels.shape[0] // 2
+        pixels = plus(pixels[:half], swap(pixels[half:], 1 << bit, count))
     near = jnp.stack([sums, swap(sums, 2, count)])
-    for bit in range(2, bits):
-        half = pixels.shape[0] // 2
-        other = swap(pixels[half:], 1 << bit, count)
-        pixels = plus(pixels[:half], other)
+    near, pixels = lax.optimization_barrier((near, pixels))
     far = swap(near, 1, count)
     grad_input = input_grad(first_grad, pixels, wv)
     grad_conv, grad_bias, grad_proj = final(quarter, me_word, near, far)

time: 60.8 us -> 59 us (0.970)
  starting transfers between devices: 23 us -> 18.9 us
  waiting for transfers between devices: 18.9 us -> 22.1 us
  local copies, waits for them, and re-layouts: 2.67 us -> 1.72 us
    ppermute x18 -> x16, starting transfers between devices: 21.8 us -> 17.5 us  [swap(): return lax.ppermute(value, 'rows', [(i, i ^ bit) for i in range(count)])]
    ppermute x18 -> x16, waiting for transfers between devices: 18.9 us -> 22.1 us  [swap(): return lax.ppermute(value, 'rows', [(i, i ^ bit) for i in range(count)])]
    unnamed x21 -> x18, local copies, waits for them, and re-layouts: 1.58 us -> 0.68 us
  transfers between devices with their start and end apart: 19 -> 17, of which waited for: 8 -> 13; matrix products, arithmetic and copies ran while one was open for 0% -> 0% of each run, Pallas kernels for 14% -> 14%
where the time goes in v4:
time: 59 us; the launch traced here: 58.8 us
  waiting for transfers between devices  22.1 us (37%)
  starting transfers between devices  18.9 us (32%)
  Pallas kernels  14.8 us (25%)
  local copies, waits for them, and re-layouts  1.72 us (3%)
  between operations  0.91 us (2%)
    ppermute x16, waiting for transfers between devices, swap(): return lax.ppermute(value, 'rows', [(i, i ^ bit) for i in range(count)])  22.1 us
    ppermute x16, starting transfers between devices, swap(): return lax.ppermute(value, 'rows', [(i, i ^ bit) for i in range(count)])  17.5 us
    pallas_call x1, Pallas kernels, main(): pl.pallas_call(functools.partial(main_kernel, count, bits, quarter), in_s...  5.42 us
    pallas_call x1, Pallas kernels, scatter(): pl.pallas_call(functools.partial(scatter_kernel, ny), out_shape=(jax.Shap...  3.85 us
    pallas_call x1, Pallas kernels, lookup(): pl.pallas_call(functools.partial(lookup_kernel, ny), out_shape=jax.ShapeD...  3.52 us
    ppermute x1, starting transfers between devices, per_device(): lax.ppermute(frames[0, 2 * RD - 1:], 'rows', [(i, i + 1) for i in range(c...  1.42 us
  transfers between devices with their start and end apart: 17, of which 13 were waited for; matrix products, arithmetic and copies ran while one was open for 0% of the time, Pallas kernels for 14%

profile of v4, /device:TPU:0, one launch (start us, length us, event | category | flops | bytes accessed | tf_op | source)
XLA Modules:
  0.0 58.8 jit_solution(17668423009515558935)
XLA Ops:
  0.7 1.0 %slice_bitcast_fusion = (bf16[16,3072]{1,0:T(8,128)(2,1)S(1)}, bf16[16,3072]{1,0:T(8,128)(2,1)S(1)}) fusion(bf16[2,16,3072]{2,1,0:T(8,128)(2,1)} %param.7), kind=kLoop, calls=%fused_computation.16 | loop fusion | bytes 393216 | tf_op jit(solution)/shard_map/squeeze | solution.py:594
  1.7 3.1 %collective-permute-start.1 = (bf16[16,3072]{1,0:T(8,128)(2,1)S(1)}, bf16[16,3072]{1,0:T(8,128)(2,1)S(1)}, u32[]{:S(2)}, u32[]{:S(2)}) collective-permute-start(bf16[16,3072]{1,0:T(8,128)(2,1)S(1)} %get-tuple-element.86), channel_id=1, source_target_pairs={{0,4},{1,5},{2,6},{3,7},{4,0},{5,1},{6,2},{7,3},{8,12},{9,13},{10,... | collective-permute-start | bytes 294920 | tf_op jit(solution)/shard_map/ppermute | solution.py:556
  4.7 2.6 %collective-permute-start = (bf16[16,3072]{1,0:T(8,128)(2,1)S(1)}, bf16[16,3072]{1,0:T(8,128)(2,1)S(1)}, u32[]{:S(2)}, u32[]{:S(2)}) collective-permute-start(bf16[16,3072]{1,0:T(8,128)(2,1)S(1)} %get-tuple-element.86), channel_id=1, source_target_pairs={{0,8},{1,9},{2,10},{3,11},{4,12},{5,13},{6,14},{7,15},{8,0},{9,1},... | collective-permute-start | bytes 294920 | tf_op jit(solution)/shard_map/ppermute | solution.py:556
  7.4 1.4 %collective-permute-start.5 = (bf16[1,3072]{1,0:T(2,128)(2,1)S(1)}, bf16[1,3072]{1,0:T(2,128)(2,1)S(1)}, u32[]{:S(2)}, u32[]{:S(2)}) collective-permute-start(bf16[1,3072]{1,0:T(2,128)(2,1)S(1)} %slice_bitcast_fusion.2), channel_id=1, source_target_pairs={{0,1},{1,2},{2,3},{3,4},{4,5},{5,6},{6,7},{7,8},{8,9},{9,10},{10,1... | collective-permute-start | bytes 18440 | tf_op jit(solution)/shard_map/ppermute | solution.py:570
  8.9 0.6 %copy-done.4 = f32[128]{0:T(128)S(1)} copy-done((f32[128]{0:T(128)S(1)}, f32[128]{0:T(128)}, u32[]{:S(2)}) %copy-start.4) | copy-done | bytes 536
  9.6 2.4 %collective-permute-done = bf16[16,3072]{1,0:T(8,128)(2,1)S(1)} collective-permute-done((bf16[16,3072]{1,0:T(8,128)(2,1)S(1)}, bf16[16,3072]{1,0:T(8,128)(2,1)S(1)}, u32[]{:S(2)}, u32[]{:S(2)}) %collective-permute-start) | collective-permute-done | bytes 98336 | tf_op jit(solution)/shard_map/ppermute | solution.py:556
  12.1 0.4 collective-permute-start.2
  12.5 1.5 %collective-permute-start.3 = (bf16[32,3072]{1,0:T(8,128)(2,1)S(1)}, bf16[32,3072]{1,0:T(8,128)(2,1)S(1)}, u32[]{:S(2)}, u32[]{:S(2)}) collective-permute-start(bf16[32,3072]{1,0:T(8,128)(2,1)S(1)} %pad_maximum_fusion.1), channel_id=1, source_target_pairs={{0,2},{1,3},{2,0},{3,1},{4,6},{5,7},{6,4},{7,5},{8,10},{9,11},{10,... | collective-permute-start | bytes 589832 | tf_op jit(solution)/shard_map/ppermute | solution.py:556
  14.0 2.7 %collective-permute-done.2 = bf16[16,3072]{1,0:T(8,128)(2,1)S(1)} collective-permute-done((bf16[16,3072]{1,0:T(8,128)(2,1)S(1)}, bf16[16,3072]{1,0:T(8,128)(2,1)S(1)}, u32[]{:S(2)}, u32[]{:S(2)}) %collective-permute-start.2) | collective-permute-done | bytes 98336 | tf_op jit(solution)/shard_map/ppermute | solution.py:556
  16.8 1.6 %collective-permute-start.4 = (bf16[32,3072]{1,0:T(8,128)(2,1)S(1)}, bf16[32,3072]{1,0:T(8,128)(2,1)S(1)}, u32[]{:S(2)}, u32[]{:S(2)}) collective-permute-start(bf16[32,3072]{1,0:T(8,128)(2,1)S(1)} %pad_maximum_fusion), channel_id=1, source_target_pairs={{0,2},{1,3},{2,0},{3,1},{4,6},{5,7},{6,4},{7,5},{8,10},{9,11},{10,... | collective-permute-start | bytes 589832 | tf_op jit(solution)/shard_map/ppermute | solution.py:556
  18.4 3.8 %scatter.1 = (bf16[16,128,128]{2,1,0:T(8,128)(2,1)S(1)}, bf16[128,2048]{1,0:T(8,128)(2,1)S(1)}) custom-call(s32[12,128]{1,0:T(8,128)S(1)} %get-tuple-element.73.row_ref, s32[12,128]{1,0:T(8,128)S(1)} %get-tuple-element.55.col_ref, bf16[3888,128]{1,0:T(8,128)(2,1)S(1)} %copy-done.5), custom_call_target="tpu_custom_call" | custom-call | flops 1000000000 | bytes 4000000 | tf_op jit(solution)/shard_map/scatter/pallas_call | solution.py:156
  22.3 0.9 %collective-permute-done.4 = bf16[32,3072]{1,0:T(8,128)(2,1)S(1)} collective-permute-done((bf16[32,3072]{1,0:T(8,128)(2,1)S(1)}, bf16[32,3072]{1,0:T(8,128)(2,1)S(1)}, u32[]{:S(2)}, u32[]{:S(2)}) %collective-permute-start.4) | collective-permute-done | bytes 196640 | tf_op jit(solution)/shard_map/ppermute | solution.py:556
  23.3 2.3 %collective-permute-done.6.far_ref = bf16[128,3072]{1,0:T(8,128)(2,1)S(1)} collective-permute-done((bf16[128,3072]{1,0:T(8,128)(2,1)S(1)}, bf16[128,3072]{1,0:T(8,128)(2,1)S(1)}, u32[]{:S(2)}, u32[]{:S(2)}) %collective-permute-start.6) | collective-permute-done | bytes 786464 | tf_op jit(solution)/shard_map/ppermute | solution.py:556
  25.5 5.4 %features.1 = (bf16[2,640,128]{2,1,0:T(8,128)(2,1)S(1)}, bf16[2,640,128]{2,1,0:T(8,128)(2,1)S(1)}, bf16[2,288,128]{2,1,0:T(8,128)(2,1)S(1)}, bf16[2,288,128]{2,1...) custom-call(s32[1]{0:T(128)} %bitcast.me_ref, ...), custom_call_target="tpu_custom_call" | custom-call | flops 4000000000 | bytes 6000000 | tf_op jit(solution)/shard_map/features/pallas_call | solution.py:447
  31.5 0.9 %collective-permute-done.7 = bf16[2,288,128]{2,1,0:T(8,128)(2,1)S(1)} collective-permute-done((bf16[2,288,128]{2,1,0:T(8,128)(2,1)S(1)}, bf16[2,288,128]{2,1,0:T(8,128)(2,1)S(1)}, u32[]{:S(2)}, u32[]{:S(2)}) %collective-permute-start.7) | collective-permute-done | bytes 147488 | tf_op jit(solution)/shard_map/ppermute | solution.py:556
  32.4 0.4 collective-permute-done.8
  32.9 0.9 %collective-permute-start.9 = (bf16[288,128]{1,0:T(8,128)(2,1)S(1)}, bf16[288,128]{1,0:T(8,128)(2,1)S(1)}, u32[]{:S(2)}, u32[]{:S(2)}) collective-permute-start(bf16[288,128]{1,0:T(8,128)(2,1)S(1)} %fusion.5), channel_id=1, source_target_pairs={{0,2},{1,3},{2,0},{3,1},{4,6},{5,7},{6,4},{7,5},{8,10},{9,11},{10,... | collective-permute-start | bytes 221192 | tf_op jit(solution)/shard_map/ppermute | solution.py:556
  33.9 3.6 %collective-permute-done.9 = bf16[288,128]{1,0:T(8,128)(2,1)S(1)} collective-permute-done((bf16[288,128]{1,0:T(8,128)(2,1)S(1)}, bf16[288,128]{1,0:T(8,128)(2,1)S(1)}, u32[]{:S(2)}, u32[]{:S(2)}) %collective-permute-start.9) | collective-permute-done | bytes 73760 | tf_op jit(solution)/shard_map/ppermute | solution.py:556
  37.5 1.6 %collective-permute-start.10 = (bf16[288,128]{1,0:T(8,128)(2,1)S(1)}, bf16[288,128]{1,0:T(8,128)(2,1)S(1)}, u32[]{:S(2)}, u32[]{:S(2)}) collective-permute-start(bf16[288,128]{1,0:T(8,128)(2,1)S(1)} %fusion.3), channel_id=1, source_target_pairs={{0,4},{1,5},{2,6},{3,7},{4,0},{5,1},{6,2},{7,3},{8,12},{9,13},{10,... | collective-permute-start | bytes 221192 | tf_op jit(solution)/shard_map/ppermute | solution.py:556
  39.1 0.7 %collective-permute-start.11 = (bf16[640,128]{1,0:T(8,128)(2,1)S(1)}, bf16[640,128]{1,0:T(8,128)(2,1)S(1)}, u32[]{:S(2)}, u32[]{:S(2)}) collective-permute-start(bf16[640,128]{1,0:T(8,128)(2,1)S(1)} %fusion.1), channel_id=1, source_target_pairs={{0,2},{1,3},{2,0},{3,1},{4,6},{5,7},{6,4},{7,5},{8,10},{9,11},{10,... | collective-permute-start | bytes 491528 | tf_op jit(solution)/shard_map/ppermute | solution.py:556
  39.9 2.0 %collective-permute-done.10 = bf16[288,128]{1,0:T(8,128)(2,1)S(1)} collective-permute-done((bf16[288,128]{1,0:T(8,128)(2,1)S(1)}, bf16[288,128]{1,0:T(8,128)(2,1)S(1)}, u32[]{:S(2)}, u32[]{:S(2)}) %collective-permute-start.10) | collective-permute-done | bytes 73760 | tf_op jit(solution)/shard_map/ppermute | solution.py:556
  41.9 2.5 %collective-permute-done.11 = bf16[640,128]{1,0:T(8,128)(2,1)S(1)} collective-permute-done((bf16[640,128]{1,0:T(8,128)(2,1)S(1)}, bf16[640,128]{1,0:T(8,128)(2,1)S(1)}, u32[]{:S(2)}, u32[]{:S(2)}) %collective-permute-start.11) | collective-permute-done | bytes 163872 | tf_op jit(solution)/shard_map/ppermute | solution.py:556
  44.5 0.8 %collective-permute-start.12 = (bf16[288,128]{1,0:T(8,128)(2,1)S(1)}, bf16[288,128]{1,0:T(8,128)(2,1)S(1)}, u32[]{:S(2)}, u32[]{:S(2)}) collective-permute-start(bf16[288,128]{1,0:T(8,128)(2,1)S(1)} %add_convert_fusion.4), channel_id=1, source_target_pairs={{0,8},{1,9},{2,10},{3,11},{4,12},{5,13},{6,14},{7,15},{8,0},{9,1},... | collective-permute-start | bytes 221192 | tf_op jit(solution)/shard_map/ppermute | solution.py:556
  45.4 1.3 %collective-permute-start.13 = (bf16[320,128]{1,0:T(8,128)(2,1)S(1)}, bf16[320,128]{1,0:T(8,128)(2,1)S(1)}, u32[]{:S(2)}, u32[]{:S(2)}) collective-permute-start(bf16[320,128]{1,0:T(8,128)(2,1)S(1)} %slice.57), channel_id=1, source_target_pairs={{0,4},{1,5},{2,6},{3,7},{4,0},{5,1},{6,2},{7,3},{8,12},{9,13},{10,... | collective-permute-start | bytes 245768 | tf_op jit(solution)/shard_map/ppermute | solution.py:556
  46.7 3.5 %lookup.1 = bf16[3888,128]{1,0:T(8,128)(2,1)} custom-call(s32[12,128]{1,0:T(8,128)S(1)} %get-tuple-element.73.row_ref, s32[12,128]{1,0:T(8,128)S(1)} %get-tuple-element.55.col_ref, bf16[16,128,128]{2,1,0:T(8,128)(2,1)S(1)} %get-tuple-element.74.hid_ref, bf16[128,256]{1,0:T(8,128)(2,1)S(1)} %get-tuple-element.75.first_ref, ...), custom_call_target="tpu_custom_call" | custom-call | flops 1000000000 | bytes 4000000 | tf_op jit(solution)/shard_map/lookup/pallas_call | solution.py:278
  50.2 0.4 collective-permute-done.12
  50.7 1.4 %collective-permute-start.15 = (bf16[160,128]{1,0:T(8,128)(2,1)S(1)}, bf16[160,128]{1,0:T(8,128)(2,1)S(1)}, u32[]{:S(2)}, u32[]{:S(2)}) collective-permute-start(bf16[160,128]{1,0:T(8,128)(2,1)S(1)} %slice.59), channel_id=1, source_target_pairs={{0,8},{1,9},{2,10},{3,11},{4,12},{5,13},{6,14},{7,15},{8,0},{9,1},... | collective-permute-start | bytes 122888 | tf_op jit(solution)/shard_map/ppermute | solution.py:556
  52.1 0.7 %collective-permute-start.14 = (bf16[288,128]{1,0:T(8,128)(2,1)S(1)}, bf16[288,128]{1,0:T(8,128)(2,1)S(1)}, u32[]{:S(2)}, u32[]{:S(2)}) collective-permute-start(bf16[288,128]{1,0:T(8,128)(2,1)S(1)} %add_convert_fusion.3), channel_id=1, source_target_pairs={{0,2},{1,3},{2,0},{3,1},{4,6},{5,7},{6,4},{7,5},{8,10},{9,11},{10,... | collective-permute-start | bytes 221192 | tf_op jit(solution)/shard_map/ppermute | solution.py:556
  52.8 3.2 %collective-permute-done.15 = bf16[160,128]{1,0:T(8,128)(2,1)S(1)} collective-permute-done((bf16[160,128]{1,0:T(8,128)(2,1)S(1)}, bf16[160,128]{1,0:T(8,128)(2,1)S(1)}, u32[]{:S(2)}, u32[]{:S(2)}) %collective-permute-start.15) | collective-permute-done | bytes 40992 | tf_op jit(solution)/shard_map/ppermute | solution.py:556
  56.0 0.4 collective-permute-done.14
  56.5 1.0 %input_grad.1 = bf16[2,16,3072]{2,1,0:T(8,128)(2,1)} custom-call(bf16[128,128]{1,0:T(8,128)(2,1)S(1)} %get-tuple-element.77.first_ref, bf16[160,128]{1,0:T(8,128)(2,1)S(1)} %add_convert_fusion.7.block_ref, bf16[2,384,384]{2,1,0:T(8,128)(2,1)S(1)} %get-tuple-element.60.wv_ref), custom_call_target="tpu_custom_call" | custom-call | flops 100000000 | bytes 1000000 | tf_op jit(solution)/shard_map/input_grad/pallas_call | solution.py:514
  57.9 0.9 %weight_grads.1 = (f32[864,128]{1,0:T(8,128)}, f32[1,128]{1,0:T(1,128)}, f32[128,256]{1,0:T(8,128)}) custom-call(s32[1]{0:T(128)} %bitcast.me_ref, bf16[2,288,128]{2,1,0:T(8,128)(2,1)S(1)} %pad_maximum_fusion.2.near_ref, bf16[2,288,128]{2,1,0:T(8,128)(2,1)S(1)} %collective-permute-done.16.far_ref), custom_call_target="tpu_custom_call" | custom-call | tf_op jit(solution)/shard_map/weight_grads/pallas_call | solution.py:541
  (42 shorter events, 1.6 us)
Async XLA Ops:
  0.6 6.7 %copy-start.6 = (bf16[2,16,3072]{2,1,0:T(8,128)(2,1)S(1)}, bf16[2,16,3072]{2,1,0:T(8,128)(2,1)}, u32[]{:S(2)}) copy-start(bf16[2,16,3072]{2,1,0:T(8,128)(2,1)} %param.7) | copy-start | bytes 589828
  0.6 8.2 %copy-start = (bf16[864,128]{1,0:T(8,128)(2,1)S(1)}, bf16[864,128]{1,0:T(8,128)(2,1)}, u32[]{:S(2)}) copy-start(bf16[864,128]{1,0:T(8,128)(2,1)} %w_ref.1) | copy-start | bytes 663556
  1.7 12.4 %collective-permute-start.1 = (bf16[16,3072]{1,0:T(8,128)(2,1)S(1)}, bf16[16,3072]{1,0:T(8,128)(2,1)S(1)}, u32[]{:S(2)}, u32[]{:S(2)}) collective-permute-start(bf16[16,3072]{1,0:T(8,128)(2,1)S(1)} %get-tuple-element.86), channel_id=1, source_target_pairs={{0,4},{1,5},{2,6},{3,7},{4,0},{5,1},{6,2},{7,3},{8,12},{9,13},{10,... | collective-permute-start | bytes 294920 | tf_op jit(solution)/shard_map/ppermute | solution.py:556
  4.7 7.3 %collective-permute-start = (bf16[16,3072]{1,0:T(8,128)(2,1)S(1)}, bf16[16,3072]{1,0:T(8,128)(2,1)S(1)}, u32[]{:S(2)}, u32[]{:S(2)}) collective-permute-start(bf16[16,3072]{1,0:T(8,128)(2,1)S(1)} %get-tuple-element.86), channel_id=1, source_target_pairs={{0,8},{1,9},{2,10},{3,11},{4,12},{5,13},{6,14},{7,15},{8,0},{9,1},... | collective-permute-start | bytes 294920 | tf_op jit(solution)/shard_map/ppermute | solution.py:556
  7.4 1.5 %copy-start.1 = (bf16[128,256]{1,0:T(8,128)(2,1)S(1)}, bf16[128,256]{1,0:T(8,128)(2,1)}, u32[]{:S(2)}) copy-start(bf16[128,256]{1,0:T(8,128)(2,1)} %proj_ref.1) | copy-start | bytes 196612
  7.4 1.5 %copy-start.2 = (s32[12,128]{1,0:T(8,128)S(1)}, s32[12,128]{1,0:T(8,128)}, u32[]{:S(2)}) copy-start(s32[12,128]{1,0:T(8,128)} %row_ref.1) | copy-start | bytes 18436
  7.4 1.5 %copy-start.3 = (s32[12,128]{1,0:T(8,128)S(1)}, s32[12,128]{1,0:T(8,128)}, u32[]{:S(2)}) copy-start(s32[12,128]{1,0:T(8,128)} %col_ref.1) | copy-start | bytes 18436
  7.4 15.8 %collective-permute-start.5 = (bf16[1,3072]{1,0:T(2,128)(2,1)S(1)}, bf16[1,3072]{1,0:T(2,128)(2,1)S(1)}, u32[]{:S(2)}, u32[]{:S(2)}) collective-permute-start(bf16[1,3072]{1,0:T(2,128)(2,1)S(1)} %slice_bitcast_fusion.2), channel_id=1, source_target_pairs={{0,1},{1,2},{2,3},{3,4},{4,5},{5,6},{6,7},{7,8},{8,9},{9,10},{10,1... | collective-permute-start | bytes 18440 | tf_op jit(solution)/shard_map/ppermute | solution.py:570
  8.8 0.7 %copy-start.4 = (f32[128]{0:T(128)S(1)}, f32[128]{0:T(128)}, u32[]{:S(2)}) copy-start(f32[128]{0:T(128)} %param.9) | copy-start | bytes 1540
  8.9 9.5 %copy-start.5 = (bf16[3888,128]{1,0:T(8,128)(2,1)S(1)}, bf16[3888,128]{1,0:T(8,128)(2,1)}, u32[]{:S(2)}) copy-start(bf16[3888,128]{1,0:T(8,128)(2,1)} %cot_hbm) | copy-start | bytes 2985988
  12.1 4.7 %collective-permute-start.2 = (bf16[16,3072]{1,0:T(8,128)(2,1)S(1)}, bf16[16,3072]{1,0:T(8,128)(2,1)S(1)}, u32[]{:S(2)}, u32[]{:S(2)}) collective-permute-start(bf16[16,3072]{1,0:T(8,128)(2,1)S(1)} %collective-permute-done), channel_id=1, source_target_pairs={{0,4},{1,5},{2,6},{3,7},{4,0},{5,1},{6,2},{7,3},{8,12},{9,13},{10,... | collective-permute-start | bytes 294920 | tf_op jit(solution)/shard_map/ppermute | solution.py:556
  12.5 9.8 %collective-permute-start.3 = (bf16[32,3072]{1,0:T(8,128)(2,1)S(1)}, bf16[32,3072]{1,0:T(8,128)(2,1)S(1)}, u32[]{:S(2)}, u32[]{:S(2)}) collective-permute-start(bf16[32,3072]{1,0:T(8,128)(2,1)S(1)} %pad_maximum_fusion.1), channel_id=1, source_target_pairs={{0,2},{1,3},{2,0},{3,1},{4,6},{5,7},{6,4},{7,5},{8,10},{9,11},{10,... | collective-permute-start | bytes 589832 | tf_op jit(solution)/shard_map/ppermute | solution.py:556
  16.8 6.4 %collective-permute-start.4 = (bf16[32,3072]{1,0:T(8,128)(2,1)S(1)}, bf16[32,3072]{1,0:T(8,128)(2,1)S(1)}, u32[]{:S(2)}, u32[]{:S(2)}) collective-permute-start(bf16[32,3072]{1,0:T(8,128)(2,1)S(1)} %pad_maximum_fusion), channel_id=1, source_target_pairs={{0,2},{1,3},{2,0},{3,1},{4,6},{5,7},{6,4},{7,5},{8,10},{9,11},{10,... | collective-permute-start | bytes 589832 | tf_op jit(solution)/shard_map/ppermute | solution.py:556
  23.2 2.4 %collective-permute-start.6 = (bf16[128,3072]{1,0:T(8,128)(2,1)S(1)}, bf16[128,3072]{1,0:T(8,128)(2,1)S(1)}, u32[]{:S(2)}, u32[]{:S(2)}) collective-permute-start(bf16[128,3072]{1,0:T(8,128)(2,1)S(1)} %constant_dynamic-update-slice_fusion.near_ref), channel_id=1, source_target_pairs={{0,1},{1,0},{2,3},{3,2},{4,5},{5,4},{6,7},{7,6},{8,9},{9,8},{10,11... | collective-permute-start | bytes 2359304 | tf_op jit(solution)/shard_map/ppermute | solution.py:556
  31.0 1.4 %collective-permute-start.7 = (bf16[2,288,128]{2,1,0:T(8,128)(2,1)S(1)}, bf16[2,288,128]{2,1,0:T(8,128)(2,1)S(1)}, u32[]{:S(2)}, u32[]{:S(2)}) collective-permute-start(bf16[2,288,128]{2,1,0:T(8,128)(2,1)S(1)} %get-tuple-element.66), channel_id=1, source_target_pairs={{0,1},{1,0},{2,3},{3,2},{4,5},{5,4},{6,7},{7,6},{8,9},{9,8},{10,11... | collective-permute-start | bytes 442376 | tf_op jit(solution)/shard_map/ppermute | solution.py:556
  31.2 1.7 %collective-permute-start.8 = (bf16[2,640,128]{2,1,0:T(8,128)(2,1)S(1)}, bf16[2,640,128]{2,1,0:T(8,128)(2,1)S(1)}, u32[]{:S(2)}, u32[]{:S(2)}) collective-permute-start(bf16[2,640,128]{2,1,0:T(8,128)(2,1)S(1)} %get-tuple-element.68), channel_id=1, source_target_pairs={{0,1},{1,0},{2,3},{3,2},{4,5},{5,4},{6,7},{7,6},{8,9},{9,8},{10,11... | collective-permute-start | bytes 983048 | tf_op jit(solution)/shard_map/ppermute | solution.py:556
  32.9 4.5 %collective-permute-start.9 = (bf16[288,128]{1,0:T(8,128)(2,1)S(1)}, bf16[288,128]{1,0:T(8,128)(2,1)S(1)}, u32[]{:S(2)}, u32[]{:S(2)}) collective-permute-start(bf16[288,128]{1,0:T(8,128)(2,1)S(1)} %fusion.5), channel_id=1, source_target_pairs={{0,2},{1,3},{2,0},{3,1},{4,6},{5,7},{6,4},{7,5},{8,10},{9,11},{10,... | collective-permute-start | bytes 221192 | tf_op jit(solution)/shard_map/ppermute | solution.py:556
  37.5 4.4 %collective-permute-start.10 = (bf16[288,128]{1,0:T(8,128)(2,1)S(1)}, bf16[288,128]{1,0:T(8,128)(2,1)S(1)}, u32[]{:S(2)}, u32[]{:S(2)}) collective-permute-start(bf16[288,128]{1,0:T(8,128)(2,1)S(1)} %fusion.3), channel_id=1, source_target_pairs={{0,4},{1,5},{2,6},{3,7},{4,0},{5,1},{6,2},{7,3},{8,12},{9,13},{10,... | collective-permute-start | bytes 221192 | tf_op jit(solution)/shard_map/ppermute | solution.py:556
  39.1 5.3 %collective-permute-start.11 = (bf16[640,128]{1,0:T(8,128)(2,1)S(1)}, bf16[640,128]{1,0:T(8,128)(2,1)S(1)}, u32[]{:S(2)}, u32[]{:S(2)}) collective-permute-start(bf16[640,128]{1,0:T(8,128)(2,1)S(1)} %fusion.1), channel_id=1, source_target_pairs={{0,2},{1,3},{2,0},{3,1},{4,6},{5,7},{6,4},{7,5},{8,10},{9,11},{10,... | collective-permute-start | bytes 491528 | tf_op jit(solution)/shard_map/ppermute | solution.py:556
  44.5 6.1 %collective-permute-start.12 = (bf16[288,128]{1,0:T(8,128)(2,1)S(1)}, bf16[288,128]{1,0:T(8,128)(2,1)S(1)}, u32[]{:S(2)}, u32[]{:S(2)}) collective-permute-start(bf16[288,128]{1,0:T(8,128)(2,1)S(1)} %add_convert_fusion.4), channel_id=1, source_target_pairs={{0,8},{1,9},{2,10},{3,11},{4,12},{5,13},{6,14},{7,15},{8,0},{9,1},... | collective-permute-start | bytes 221192 | tf_op jit(solution)/shard_map/ppermute | solution.py:556
  45.4 5.3 %collective-permute-start.13 = (bf16[320,128]{1,0:T(8,128)(2,1)S(1)}, bf16[320,128]{1,0:T(8,128)(2,1)S(1)}, u32[]{:S(2)}, u32[]{:S(2)}) collective-permute-start(bf16[320,128]{1,0:T(8,128)(2,1)S(1)} %slice.57), channel_id=1, source_target_pairs={{0,4},{1,5},{2,6},{3,7},{4,0},{5,1},{6,2},{7,3},{8,12},{9,13},{10,... | collective-permute-start | bytes 245768 | tf_op jit(solution)/shard_map/ppermute | solution.py:556
  50.7 5.3 %collective-permute-start.15 = (bf16[160,128]{1,0:T(8,128)(2,1)S(1)}, bf16[160,128]{1,0:T(8,128)(2,1)S(1)}, u32[]{:S(2)}, u32[]{:S(2)}) collective-permute-start(bf16[160,128]{1,0:T(8,128)(2,1)S(1)} %slice.59), channel_id=1, source_target_pairs={{0,8},{1,9},{2,10},{3,11},{4,12},{5,13},{6,14},{7,15},{8,0},{9,1},... | collective-permute-start | bytes 122888 | tf_op jit(solution)/shard_map/ppermute | solution.py:556
  52.1 4.4 %collective-permute-start.14 = (bf16[288,128]{1,0:T(8,128)(2,1)S(1)}, bf16[288,128]{1,0:T(8,128)(2,1)S(1)}, u32[]{:S(2)}, u32[]{:S(2)}) collective-permute-start(bf16[288,128]{1,0:T(8,128)(2,1)S(1)} %add_convert_fusion.3), channel_id=1, source_target_pairs={{0,2},{1,3},{2,0},{3,1},{4,6},{5,7},{6,4},{7,5},{8,10},{9,11},{10,... | collective-permute-start | bytes 221192 | tf_op jit(solution)/shard_map/ppermute | solution.py:556
  56.5 1.4 %collective-permute-start.16 = (bf16[2,288,128]{2,1,0:T(8,128)(2,1)S(1)}, bf16[2,288,128]{2,1,0:T(8,128)(2,1)S(1)}, u32[]{:S(2)}, u32[]{:S(2)}) collective-permute-start(bf16[2,288,128]{2,1,0:T(8,128)(2,1)S(1)} %pad_maximum_fusion.2.near_ref), channel_id=1, source_target_pairs={{0,1},{1,0},{2,3},{3,2},{4,5},{5,4},{6,7},{7,6},{8,9},{9,8},{10,11... | collective-permute-start | bytes 442376 | tf_op jit(solution)/shard_map/ppermute | solution.py:556

commit v5 on v4

--- a/solution.py
+++ b/solution.py
@@ -325,7 +325,7 @@
 
 
 def main_kernel(
-    count, bits, quarter, me_ref, near_ref, far_ref, own_ref, halo_ref, wv_ref, bias_ref, proj_ref,
+    count, bits, quarter, me_ref, maps0_ref, maps1_ref, maps2_ref, maps3_ref, own_ref, halo_ref, wv_ref, bias_ref, proj_ref,
     grad_ref, grad_t_ref, kept_ref, sent_ref, sums_kept_ref, sums_sent_ref, hid_ref, first_ref,
     first_grad_ref, views, inner, grads, rows_out, turned, pre0, below, wsum
 ):
@@ -358,7 +358,8 @@
     place_rows(span, 2 * RD, owned)
 
     def gathered(lanes):
-        rows = jnp.concatenate([near_ref[:, lanes], far_ref[:, lanes]], axis=0)
+        refs = (maps0_ref, maps1_ref, maps2_ref, maps3_ref)
+        rows = jnp.concatenate([ref[:, lanes] for ref in refs], axis=0)
         return dot(picks, rows).astype(BF16)
 
     place_rows(0, ny, gathered)
@@ -439,14 +440,14 @@
         dest[place % 2] = wsum[pl.ds(row, quarter), :].astype(BF16)
 
 
-def main(count, bits, quarter, me, near, far, own, halo, wv, bias, proj_weight, grad, grad_t):
+def main(count, bits, quarter, me, maps, own, halo, wv, bias, proj_weight, grad, grad_t):
     ny = count * RD
     rows = 8 * ny + PIX
     vmem = pl.BlockSpec(memory_space=pltpu.VMEM)
     pixels, sums = (2, BLOCK * count // 4, C1), (2, quarter, C1)
     return pl.pallas_call(
         functools.partial(main_kernel, count, bits, quarter),
-        in_specs=[pl.BlockSpec(memory_space=pltpu.SMEM)] + [vmem] * 9,
+        in_specs=[pl.BlockSpec(memory_space=pltpu.SMEM)] + [vmem] * 11,
         out_shape=(
             jax.ShapeDtypeStruct(pixels, BF16),
             jax.ShapeDtypeStruct(pixels, BF16),
@@ -469,7 +470,7 @@
         compiler_params=vmem_of(ny),
         cost_estimate=pl.CostEstimate(flops=4 * 10**9, bytes_accessed=6 * 10**6, transcendentals=0),
         name="features",
-    )(me, near, far, own, halo, wv, bias, proj_weight, grad, grad_t)
+    )(me, *maps, own, halo, wv, bias, proj_weight, grad, grad_t)
 
 
 def input_kernel(first_ref, block_ref, wv_ref, out_ref, sides, full):
@@ -587,11 +588,13 @@
     )
     across_far = swap(across, 2, count)
     grad, grad_t = scatter(ny, target_row, target_col, cotangent)
-    near = jnp.concatenate([own, across, own_far, across_far], axis=0)
-    near, grad, halo = lax.optimization_barrier((near, grad, halo))
-    far = swap(near, 1, count)
+    near = jnp.concatenate([own, across], axis=0)
+    other = swap(near, 1, count)
+    far = jnp.concatenate([own_far, across_far], axis=0)
+    far, grad, halo, other = lax.optimization_barrier((far, grad, halo, other))
+    maps = near, far, other, swap(far, 1, count)
     kept, sent, sums_kept, sums_sent, hid, first, first_grad = main(
-        count, bits, quarter, me_word, near, far, frames[0], halo, wv,
+        count, bits, quarter, me_word, maps, frames[0], halo, wv,
         conv_bias, proj_weight, grad, grad_t,
     )
 

time: 59 us -> 58.7 us (level)
  starting transfers between devices: 18.9 us -> 18.2 us
    squeeze x1, local copies, waits for them, and re-layouts: 0.02 us -> 0.81 us  [per_device(): frames[0, 2 * RD - 1:]]
    ppermute x16 -> x17, starting transfers between devices: 17.5 us -> 16.8 us  [swap(): return lax.ppermute(value, 'rows', [(i, i ^ bit) for i in range(count)])]
    unnamed x18 -> x12, local copies, waits for them, and re-layouts: 0.68 us -> 0.03 us
    ppermute x16 -> x17, waiting for transfers between devices: 22.1 us -> 22.3 us  [swap(): return lax.ppermute(value, 'rows', [(i, i ^ bit) for i in range(count)])]
  transfers between devices with their start and end apart: 17 -> 18, of which waited for: 13 -> 13; matrix products, arithmetic and copies ran while one was open for 0% -> 2% of each run, Pallas kernels for 14% -> 15%
where the time goes in v5:
time: 58.7 us; the launch traced here: 58.5 us
  waiting for transfers between devices  22.3 us (38%)
  starting transfers between devices  18.2 us (31%)
  Pallas kernels  14.8 us (25%)
  local copies, waits for them, and re-layouts  1.86 us (3%)
  between operations  0.91 us (2%)
    ppermute x17, waiting for transfers between devices, swap(): return lax.ppermute(value, 'rows', [(i, i ^ bit) for i in range(count)])  22.3 us
    ppermute x17, starting transfers between devices, swap(): return lax.ppermute(value, 'rows', [(i, i ^ bit) for i in range(count)])  16.8 us
    pallas_call x1, Pallas kernels, main(): pl.pallas_call(functools.partial(main_kernel, count, bits, quarter), in_s...  5.42 us
    pallas_call x1, Pallas kernels, scatter(): pl.pallas_call(functools.partial(scatter_kernel, ny), out_shape=(jax.Shap...  3.85 us
    pallas_call x1, Pallas kernels, lookup(): pl.pallas_call(functools.partial(lookup_kernel, ny), out_shape=jax.ShapeD...  3.52 us
    ppermute x1, starting transfers between devices, per_device(): lax.ppermute(frames[0, 2 * RD - 1:], 'rows', [(i, i + 1) for i in range(c...  1.42 us
  transfers between devices with their start and end apart: 18, of which 13 were waited for; matrix products, arithmetic and copies ran while one was open for 2% of the time, Pallas kernels for 15%

profile of v5, /device:TPU:0, one launch (start us, length us, event | category | flops | bytes accessed | tf_op | source)
XLA Modules:
  0.0 58.5 jit_solution(15751777624428106232)
XLA Ops:
  0.7 1.0 %slice_bitcast_fusion = (bf16[16,3072]{1,0:T(8,128)(2,1)S(1)}, bf16[16,3072]{1,0:T(8,128)(2,1)S(1)}) fusion(bf16[2,16,3072]{2,1,0:T(8,128)(2,1)} %param.7), kind=kLoop, calls=%fused_computation.18 | loop fusion | bytes 393216 | tf_op jit(solution)/shard_map/squeeze | solution.py:597
  1.7 3.1 %collective-permute-start.1 = (bf16[16,3072]{1,0:T(8,128)(2,1)S(1)}, bf16[16,3072]{1,0:T(8,128)(2,1)S(1)}, u32[]{:S(2)}, u32[]{:S(2)}) collective-permute-start(bf16[16,3072]{1,0:T(8,128)(2,1)S(1)} %get-tuple-element.88), channel_id=1, source_target_pairs={{0,4},{1,5},{2,6},{3,7},{4,0},{5,1},{6,2},{7,3},{8,12},{9,13},{10,... | collective-permute-start | bytes 294920 | tf_op jit(solution)/shard_map/ppermute | solution.py:557
  4.8 2.6 %collective-permute-start = (bf16[16,3072]{1,0:T(8,128)(2,1)S(1)}, bf16[16,3072]{1,0:T(8,128)(2,1)S(1)}, u32[]{:S(2)}, u32[]{:S(2)}) collective-permute-start(bf16[16,3072]{1,0:T(8,128)(2,1)S(1)} %get-tuple-element.88), channel_id=1, source_target_pairs={{0,8},{1,9},{2,10},{3,11},{4,12},{5,13},{6,14},{7,15},{8,0},{9,1},... | collective-permute-start | bytes 294920 | tf_op jit(solution)/shard_map/ppermute | solution.py:557
  7.4 0.8 %slice_bitcast_fusion.2 = bf16[1,3072]{1,0:T(2,128)(2,1)S(1)} fusion(bf16[2,16,3072]{2,1,0:T(8,128)(2,1)} %param.7), kind=kLoop, calls=%fused_computation.23 | loop fusion | bytes 12288 | tf_op jit(solution)/shard_map/squeeze | solution.py:571
  8.2 1.4 %collective-permute-start.5 = (bf16[1,3072]{1,0:T(2,128)(2,1)S(1)}, bf16[1,3072]{1,0:T(2,128)(2,1)S(1)}, u32[]{:S(2)}, u32[]{:S(2)}) collective-permute-start(bf16[1,3072]{1,0:T(2,128)(2,1)S(1)} %slice_bitcast_fusion.2), channel_id=1, source_target_pairs={{0,1},{1,2},{2,3},{3,4},{4,5},{5,6},{6,7},{7,8},{8,9},{9,10},{10,1... | collective-permute-start | bytes 18440 | tf_op jit(solution)/shard_map/ppermute | solution.py:571
  9.8 2.3 %collective-permute-done = bf16[16,3072]{1,0:T(8,128)(2,1)S(1)} collective-permute-done((bf16[16,3072]{1,0:T(8,128)(2,1)S(1)}, bf16[16,3072]{1,0:T(8,128)(2,1)S(1)}, u32[]{:S(2)}, u32[]{:S(2)}) %collective-permute-start) | collective-permute-done | bytes 98336 | tf_op jit(solution)/shard_map/ppermute | solution.py:557
  12.4 1.6 %collective-permute-start.3 = (bf16[32,3072]{1,0:T(8,128)(2,1)S(1)}, bf16[32,3072]{1,0:T(8,128)(2,1)S(1)}, u32[]{:S(2)}, u32[]{:S(2)}) collective-permute-start(bf16[32,3072]{1,0:T(8,128)(2,1)S(1)} %pad_maximum_fusion.3), channel_id=1, source_target_pairs={{0,2},{1,3},{2,0},{3,1},{4,6},{5,7},{6,4},{7,5},{8,10},{9,11},{10,... | collective-permute-start | bytes 589832 | tf_op jit(solution)/shard_map/ppermute | solution.py:557
  14.0 2.8 %collective-permute-done.2 = bf16[16,3072]{1,0:T(8,128)(2,1)S(1)} collective-permute-done((bf16[16,3072]{1,0:T(8,128)(2,1)S(1)}, bf16[16,3072]{1,0:T(8,128)(2,1)S(1)}, u32[]{:S(2)}, u32[]{:S(2)}) %collective-permute-start.2) | collective-permute-done | bytes 98336 | tf_op jit(solution)/shard_map/ppermute | solution.py:557
  16.8 1.4 %collective-permute-start.4 = (bf16[32,3072]{1,0:T(8,128)(2,1)S(1)}, bf16[32,3072]{1,0:T(8,128)(2,1)S(1)}, u32[]{:S(2)}, u32[]{:S(2)}) collective-permute-start(bf16[32,3072]{1,0:T(8,128)(2,1)S(1)} %pad_maximum_fusion.2), channel_id=1, source_target_pairs={{0,2},{1,3},{2,0},{3,1},{4,6},{5,7},{6,4},{7,5},{8,10},{9,11},{10,... | collective-permute-start | bytes 589832 | tf_op jit(solution)/shard_map/ppermute | solution.py:557
  18.4 3.8 %scatter.1 = (bf16[16,128,128]{2,1,0:T(8,128)(2,1)S(1)}, bf16[128,2048]{1,0:T(8,128)(2,1)S(1)}) custom-call(s32[12,128]{1,0:T(8,128)S(1)} %get-tuple-element.75.row_ref, s32[12,128]{1,0:T(8,128)S(1)} %get-tuple-element.56.col_ref, bf16[3888,128]{1,0:T(8,128)(2,1)S(1)} %copy-done.5), custom_call_target="tpu_custom_call" | custom-call | flops 1000000000 | bytes 4000000 | tf_op jit(solution)/shard_map/scatter/pallas_call | solution.py:156
  22.3 1.1 %collective-permute-done.4 = bf16[32,3072]{1,0:T(8,128)(2,1)S(1)} collective-permute-done((bf16[32,3072]{1,0:T(8,128)(2,1)S(1)}, bf16[32,3072]{1,0:T(8,128)(2,1)S(1)}, u32[]{:S(2)}, u32[]{:S(2)}) %collective-permute-start.4) | collective-permute-done | bytes 196640 | tf_op jit(solution)/shard_map/ppermute | solution.py:557
  23.5 1.7 %collective-permute-done.7.maps3_ref = bf16[64,3072]{1,0:T(8,128)(2,1)S(1)} collective-permute-done((bf16[64,3072]{1,0:T(8,128)(2,1)S(1)}, bf16[64,3072]{1,0:T(8,128)(2,1)S(1)}, u32[]{:S(2)}, u32[]{:S(2)}) %collective-permute-start.7) | collective-permute-done | bytes 393248 | tf_op jit(solution)/shard_map/ppermute | solution.py:557
  25.2 5.4 %features.1 = (bf16[2,640,128]{2,1,0:T(8,128)(2,1)S(1)}, bf16[2,640,128]{2,1,0:T(8,128)(2,1)S(1)}, bf16[2,288,128]{2,1,0:T(8,128)(2,1)S(1)}, bf16[2,288,128]{2,1...) custom-call(s32[1]{0:T(128)} %bitcast.me_ref, ...), custom_call_target="tpu_custom_call" | custom-call | flops 4000000000 | bytes 6000000 | tf_op jit(solution)/shard_map/features/pallas_call | solution.py:448
  30.9 0.4 collective-permute-start.9
  31.2 0.9 %collective-permute-done.8 = bf16[2,288,128]{2,1,0:T(8,128)(2,1)S(1)} collective-permute-done((bf16[2,288,128]{2,1,0:T(8,128)(2,1)S(1)}, bf16[2,288,128]{2,1,0:T(8,128)(2,1)S(1)}, u32[]{:S(2)}, u32[]{:S(2)}) %collective-permute-start.8) | collective-permute-done | bytes 147488 | tf_op jit(solution)/shard_map/ppermute | solution.py:557
  32.1 0.4 collective-permute-done.9
  32.6 0.6 %collective-permute-start.10 = (bf16[288,128]{1,0:T(8,128)(2,1)S(1)}, bf16[288,128]{1,0:T(8,128)(2,1)S(1)}, u32[]{:S(2)}, u32[]{:S(2)}) collective-permute-start(bf16[288,128]{1,0:T(8,128)(2,1)S(1)} %fusion.5), channel_id=1, source_target_pairs={{0,2},{1,3},{2,0},{3,1},{4,6},{5,7},{6,4},{7,5},{8,10},{9,11},{10,... | collective-permute-start | bytes 221192 | tf_op jit(solution)/shard_map/ppermute | solution.py:557
  33.2 3.9 %collective-permute-done.10 = bf16[288,128]{1,0:T(8,128)(2,1)S(1)} collective-permute-done((bf16[288,128]{1,0:T(8,128)(2,1)S(1)}, bf16[288,128]{1,0:T(8,128)(2,1)S(1)}, u32[]{:S(2)}, u32[]{:S(2)}) %collective-permute-start.10) | collective-permute-done | bytes 73760 | tf_op jit(solution)/shard_map/ppermute | solution.py:557
  37.2 1.6 %collective-permute-start.11 = (bf16[288,128]{1,0:T(8,128)(2,1)S(1)}, bf16[288,128]{1,0:T(8,128)(2,1)S(1)}, u32[]{:S(2)}, u32[]{:S(2)}) collective-permute-start(bf16[288,128]{1,0:T(8,128)(2,1)S(1)} %fusion.3), channel_id=1, source_target_pairs={{0,4},{1,5},{2,6},{3,7},{4,0},{5,1},{6,2},{7,3},{8,12},{9,13},{10,... | collective-permute-start | bytes 221192 | tf_op jit(solution)/shard_map/ppermute | solution.py:557
  38.8 0.6 %collective-permute-start.12 = (bf16[640,128]{1,0:T(8,128)(2,1)S(1)}, bf16[640,128]{1,0:T(8,128)(2,1)S(1)}, u32[]{:S(2)}, u32[]{:S(2)}) collective-permute-start(bf16[640,128]{1,0:T(8,128)(2,1)S(1)} %fusion.1), channel_id=1, source_target_pairs={{0,2},{1,3},{2,0},{3,1},{4,6},{5,7},{6,4},{7,5},{8,10},{9,11},{10,... | collective-permute-start | bytes 491528 | tf_op jit(solution)/shard_map/ppermute | solution.py:557
  39.5 2.2 %collective-permute-done.11 = bf16[288,128]{1,0:T(8,128)(2,1)S(1)} collective-permute-done((bf16[288,128]{1,0:T(8,128)(2,1)S(1)}, bf16[288,128]{1,0:T(8,128)(2,1)S(1)}, u32[]{:S(2)}, u32[]{:S(2)}) %collective-permute-start.11) | collective-permute-done | bytes 73760 | tf_op jit(solution)/shard_map/ppermute | solution.py:557
  41.6 2.5 %collective-permute-done.12 = bf16[640,128]{1,0:T(8,128)(2,1)S(1)} collective-permute-done((bf16[640,128]{1,0:T(8,128)(2,1)S(1)}, bf16[640,128]{1,0:T(8,128)(2,1)S(1)}, u32[]{:S(2)}, u32[]{:S(2)}) %collective-permute-start.12) | collective-permute-done | bytes 163872 | tf_op jit(solution)/shard_map/ppermute | solution.py:557
  44.2 0.6 %collective-permute-start.13 = (bf16[288,128]{1,0:T(8,128)(2,1)S(1)}, bf16[288,128]{1,0:T(8,128)(2,1)S(1)}, u32[]{:S(2)}, u32[]{:S(2)}) collective-permute-start(bf16[288,128]{1,0:T(8,128)(2,1)S(1)} %add_convert_fusion.4), channel_id=1, source_target_pairs={{0,8},{1,9},{2,10},{3,11},{4,12},{5,13},{6,14},{7,15},{8,0},{9,1},... | collective-permute-start | bytes 221192 | tf_op jit(solution)/shard_map/ppermute | solution.py:557
  44.9 1.4 %collective-permute-start.14 = (bf16[320,128]{1,0:T(8,128)(2,1)S(1)}, bf16[320,128]{1,0:T(8,128)(2,1)S(1)}, u32[]{:S(2)}, u32[]{:S(2)}) collective-permute-start(bf16[320,128]{1,0:T(8,128)(2,1)S(1)} %slice.57), channel_id=1, source_target_pairs={{0,4},{1,5},{2,6},{3,7},{4,0},{5,1},{6,2},{7,3},{8,12},{9,13},{10,... | collective-permute-start | bytes 245768 | tf_op jit(solution)/shard_map/ppermute | solution.py:557
  46.3 3.5 %lookup.1 = bf16[3888,128]{1,0:T(8,128)(2,1)} custom-call(s32[12,128]{1,0:T(8,128)S(1)} %get-tuple-element.75.row_ref, s32[12,128]{1,0:T(8,128)S(1)} %get-tuple-element.56.col_ref, bf16[16,128,128]{2,1,0:T(8,128)(2,1)S(1)} %get-tuple-element.76.hid_ref, bf16[128,256]{1,0:T(8,128)(2,1)S(1)} %get-tuple-element.77.first_ref, ...), custom_call_target="tpu_custom_call" | custom-call | flops 1000000000 | bytes 4000000 | tf_op jit(solution)/shard_map/lookup/pallas_call | solution.py:278
  49.8 0.4 collective-permute-done.13
  50.3 1.5 %collective-permute-start.16 = (bf16[160,128]{1,0:T(8,128)(2,1)S(1)}, bf16[160,128]{1,0:T(8,128)(2,1)S(1)}, u32[]{:S(2)}, u32[]{:S(2)}) collective-permute-start(bf16[160,128]{1,0:T(8,128)(2,1)S(1)} %slice.59), channel_id=1, source_target_pairs={{0,8},{1,9},{2,10},{3,11},{4,12},{5,13},{6,14},{7,15},{8,0},{9,1},... | collective-permute-start | bytes 122888 | tf_op jit(solution)/shard_map/ppermute | solution.py:557
  51.8 0.6 %collective-permute-start.15 = (bf16[288,128]{1,0:T(8,128)(2,1)S(1)}, bf16[288,128]{1,0:T(8,128)(2,1)S(1)}, u32[]{:S(2)}, u32[]{:S(2)}) collective-permute-start(bf16[288,128]{1,0:T(8,128)(2,1)S(1)} %add_convert_fusion.3), channel_id=1, source_target_pairs={{0,2},{1,3},{2,0},{3,1},{4,6},{5,7},{6,4},{7,5},{8,10},{9,11},{10,... | collective-permute-start | bytes 221192 | tf_op jit(solution)/shard_map/ppermute | solution.py:557
  52.4 3.2 %collective-permute-done.16 = bf16[160,128]{1,0:T(8,128)(2,1)S(1)} collective-permute-done((bf16[160,128]{1,0:T(8,128)(2,1)S(1)}, bf16[160,128]{1,0:T(8,128)(2,1)S(1)}, u32[]{:S(2)}, u32[]{:S(2)}) %collective-permute-start.16) | collective-permute-done | bytes 40992 | tf_op jit(solution)/shard_map/ppermute | solution.py:557
  55.6 0.5 collective-permute-done.15
  56.2 1.0 %input_grad.1 = bf16[2,16,3072]{2,1,0:T(8,128)(2,1)} custom-call(bf16[128,128]{1,0:T(8,128)(2,1)S(1)} %get-tuple-element.79.first_ref, bf16[160,128]{1,0:T(8,128)(2,1)S(1)} %add_convert_fusion.7.block_ref, bf16[2,384,384]{2,1,0:T(8,128)(2,1)S(1)} %get-tuple-element.62.wv_ref), custom_call_target="tpu_custom_call" | custom-call | flops 100000000 | bytes 1000000 | tf_op jit(solution)/shard_map/input_grad/pallas_call | solution.py:515
  57.6 0.9 %weight_grads.1 = (f32[864,128]{1,0:T(8,128)}, f32[1,128]{1,0:T(1,128)}, f32[128,256]{1,0:T(8,128)}) custom-call(s32[1]{0:T(128)} %bitcast.me_ref, bf16[2,288,128]{2,1,0:T(8,128)(2,1)S(1)} %pad_maximum_fusion.4.near_ref, bf16[2,288,128]{2,1,0:T(8,128)(2,1)S(1)} %collective-permute-done.17.far_ref), custom_call_target="tpu_custom_call" | custom-call | tf_op jit(solution)/shard_map/weight_grads/pallas_call | solution.py:542
  (39 shorter events, 1.6 us)
Async XLA Ops:
  0.6 9.0 %copy-start = (bf16[864,128]{1,0:T(8,128)(2,1)S(1)}, bf16[864,128]{1,0:T(8,128)(2,1)}, u32[]{:S(2)}) copy-start(bf16[864,128]{1,0:T(8,128)(2,1)} %w_ref.1) | copy-start | bytes 663556
  0.6 9.0 %copy-start.1 = (bf16[128,256]{1,0:T(8,128)(2,1)S(1)}, bf16[128,256]{1,0:T(8,128)(2,1)}, u32[]{:S(2)}) copy-start(bf16[128,256]{1,0:T(8,128)(2,1)} %proj_ref.1) | copy-start | bytes 196612
  1.7 8.0 %copy-start.2 = (s32[12,128]{1,0:T(8,128)S(1)}, s32[12,128]{1,0:T(8,128)}, u32[]{:S(2)}) copy-start(s32[12,128]{1,0:T(8,128)} %row_ref.1) | copy-start | bytes 18436
  1.7 8.0 %copy-start.3 = (s32[12,128]{1,0:T(8,128)S(1)}, s32[12,128]{1,0:T(8,128)}, u32[]{:S(2)}) copy-start(s32[12,128]{1,0:T(8,128)} %col_ref.1) | copy-start | bytes 18436
  1.7 12.3 %collective-permute-start.1 = (bf16[16,3072]{1,0:T(8,128)(2,1)S(1)}, bf16[16,3072]{1,0:T(8,128)(2,1)S(1)}, u32[]{:S(2)}, u32[]{:S(2)}) collective-permute-start(bf16[16,3072]{1,0:T(8,128)(2,1)S(1)} %get-tuple-element.88), channel_id=1, source_target_pairs={{0,4},{1,5},{2,6},{3,7},{4,0},{5,1},{6,2},{7,3},{8,12},{9,13},{10,... | collective-permute-start | bytes 294920 | tf_op jit(solution)/shard_map/ppermute | solution.py:557
  4.8 7.3 %collective-permute-start = (bf16[16,3072]{1,0:T(8,128)(2,1)S(1)}, bf16[16,3072]{1,0:T(8,128)(2,1)S(1)}, u32[]{:S(2)}, u32[]{:S(2)}) collective-permute-start(bf16[16,3072]{1,0:T(8,128)(2,1)S(1)} %get-tuple-element.88), channel_id=1, source_target_pairs={{0,8},{1,9},{2,10},{3,11},{4,12},{5,13},{6,14},{7,15},{8,0},{9,1},... | collective-permute-start | bytes 294920 | tf_op jit(solution)/shard_map/ppermute | solution.py:557
  8.2 1.5 %copy-start.4 = (f32[128]{0:T(128)S(1)}, f32[128]{0:T(128)}, u32[]{:S(2)}) copy-start(f32[128]{0:T(128)} %param.9) | copy-start | bytes 1540
  8.2 10.2 %copy-start.5 = (bf16[3888,128]{1,0:T(8,128)(2,1)S(1)}, bf16[3888,128]{1,0:T(8,128)(2,1)}, u32[]{:S(2)}) copy-start(bf16[3888,128]{1,0:T(8,128)(2,1)} %cot_hbm) | copy-start | bytes 2985988
  8.2 15.2 %collective-permute-start.5 = (bf16[1,3072]{1,0:T(2,128)(2,1)S(1)}, bf16[1,3072]{1,0:T(2,128)(2,1)S(1)}, u32[]{:S(2)}, u32[]{:S(2)}) collective-permute-start(bf16[1,3072]{1,0:T(2,128)(2,1)S(1)} %slice_bitcast_fusion.2), channel_id=1, source_target_pairs={{0,1},{1,2},{2,3},{3,4},{4,5},{5,6},{6,7},{7,8},{8,9},{9,10},{10,1... | collective-permute-start | bytes 18440 | tf_op jit(solution)/shard_map/ppermute | solution.py:571
  12.1 4.8 %collective-permute-start.2 = (bf16[16,3072]{1,0:T(8,128)(2,1)S(1)}, bf16[16,3072]{1,0:T(8,128)(2,1)S(1)}, u32[]{:S(2)}, u32[]{:S(2)}) collective-permute-start(bf16[16,3072]{1,0:T(8,128)(2,1)S(1)} %collective-permute-done), channel_id=1, source_target_pairs={{0,4},{1,5},{2,6},{3,7},{4,0},{5,1},{6,2},{7,3},{8,12},{9,13},{10,... | collective-permute-start | bytes 294920 | tf_op jit(solution)/shard_map/ppermute | solution.py:557
  12.4 9.8 %collective-permute-start.3 = (bf16[32,3072]{1,0:T(8,128)(2,1)S(1)}, bf16[32,3072]{1,0:T(8,128)(2,1)S(1)}, u32[]{:S(2)}, u32[]{:S(2)}) collective-permute-start(bf16[32,3072]{1,0:T(8,128)(2,1)S(1)} %pad_maximum_fusion.3), channel_id=1, source_target_pairs={{0,2},{1,3},{2,0},{3,1},{4,6},{5,7},{6,4},{7,5},{8,10},{9,11},{10,... | collective-permute-start | bytes 589832 | tf_op jit(solution)/shard_map/ppermute | solution.py:557
  16.8 6.6 %collective-permute-start.4 = (bf16[32,3072]{1,0:T(8,128)(2,1)S(1)}, bf16[32,3072]{1,0:T(8,128)(2,1)S(1)}, u32[]{:S(2)}, u32[]{:S(2)}) collective-permute-start(bf16[32,3072]{1,0:T(8,128)(2,1)S(1)} %pad_maximum_fusion.2), channel_id=1, source_target_pairs={{0,2},{1,3},{2,0},{3,1},{4,6},{5,7},{6,4},{7,5},{8,10},{9,11},{10,... | collective-permute-start | bytes 589832 | tf_op jit(solution)/shard_map/ppermute | solution.py:557
  18.3 5.1 %collective-permute-start.6 = (bf16[64,3072]{1,0:T(8,128)(2,1)S(1)}, bf16[64,3072]{1,0:T(8,128)(2,1)S(1)}, u32[]{:S(2)}, u32[]{:S(2)}) collective-permute-start(bf16[64,3072]{1,0:T(8,128)(2,1)S(1)} %pad_maximum_fusion.maps0_ref), channel_id=1, source_target_pairs={{0,1},{1,0},{2,3},{3,2},{4,5},{5,4},{6,7},{7,6},{8,9},{9,8},{10,11... | collective-permute-start | bytes 1179656 | tf_op jit(solution)/shard_map/ppermute | solution.py:557
  23.5 1.8 %collective-permute-start.7 = (bf16[64,3072]{1,0:T(8,128)(2,1)S(1)}, bf16[64,3072]{1,0:T(8,128)(2,1)S(1)}, u32[]{:S(2)}, u32[]{:S(2)}) collective-permute-start(bf16[64,3072]{1,0:T(8,128)(2,1)S(1)} %pad_maximum_fusion.1.maps1_ref), channel_id=1, source_target_pairs={{0,1},{1,0},{2,3},{3,2},{4,5},{5,4},{6,7},{7,6},{8,9},{9,8},{10,11... | collective-permute-start | bytes 1179656 | tf_op jit(solution)/shard_map/ppermute | solution.py:557
  30.7 1.4 %collective-permute-start.8 = (bf16[2,288,128]{2,1,0:T(8,128)(2,1)S(1)}, bf16[2,288,128]{2,1,0:T(8,128)(2,1)S(1)}, u32[]{:S(2)}, u32[]{:S(2)}) collective-permute-start(bf16[2,288,128]{2,1,0:T(8,128)(2,1)S(1)} %get-tuple-element.68), channel_id=1, source_target_pairs={{0,1},{1,0},{2,3},{3,2},{4,5},{5,4},{6,7},{7,6},{8,9},{9,8},{10,11... | collective-permute-start | bytes 442376 | tf_op jit(solution)/shard_map/ppermute | solution.py:557
  30.9 1.7 %collective-permute-start.9 = (bf16[2,640,128]{2,1,0:T(8,128)(2,1)S(1)}, bf16[2,640,128]{2,1,0:T(8,128)(2,1)S(1)}, u32[]{:S(2)}, u32[]{:S(2)}) collective-permute-start(bf16[2,640,128]{2,1,0:T(8,128)(2,1)S(1)} %get-tuple-element.70), channel_id=1, source_target_pairs={{0,1},{1,0},{2,3},{3,2},{4,5},{5,4},{6,7},{7,6},{8,9},{9,8},{10,11... | collective-permute-start | bytes 983048 | tf_op jit(solution)/shard_map/ppermute | solution.py:557
  32.6 4.5 %collective-permute-start.10 = (bf16[288,128]{1,0:T(8,128)(2,1)S(1)}, bf16[288,128]{1,0:T(8,128)(2,1)S(1)}, u32[]{:S(2)}, u32[]{:S(2)}) collective-permute-start(bf16[288,128]{1,0:T(8,128)(2,1)S(1)} %fusion.5), channel_id=1, source_target_pairs={{0,2},{1,3},{2,0},{3,1},{4,6},{5,7},{6,4},{7,5},{8,10},{9,11},{10,... | collective-permute-start | bytes 221192 | tf_op jit(solution)/shard_map/ppermute | solution.py:557
  37.2 4.4 %collective-permute-start.11 = (bf16[288,128]{1,0:T(8,128)(2,1)S(1)}, bf16[288,128]{1,0:T(8,128)(2,1)S(1)}, u32[]{:S(2)}, u32[]{:S(2)}) collective-permute-start(bf16[288,128]{1,0:T(8,128)(2,1)S(1)} %fusion.3), channel_id=1, source_target_pairs={{0,4},{1,5},{2,6},{3,7},{4,0},{5,1},{6,2},{7,3},{8,12},{9,13},{10,... | collective-permute-start | bytes 221192 | tf_op jit(solution)/shard_map/ppermute | solution.py:557
  38.8 5.3 %collective-permute-start.12 = (bf16[640,128]{1,0:T(8,128)(2,1)S(1)}, bf16[640,128]{1,0:T(8,128)(2,1)S(1)}, u32[]{:S(2)}, u32[]{:S(2)}) collective-permute-start(bf16[640,128]{1,0:T(8,128)(2,1)S(1)} %fusion.1), channel_id=1, source_target_pairs={{0,2},{1,3},{2,0},{3,1},{4,6},{5,7},{6,4},{7,5},{8,10},{9,11},{10,... | collective-permute-start | bytes 491528 | tf_op jit(solution)/shard_map/ppermute | solution.py:557
  44.2 6.0 %collective-permute-start.13 = (bf16[288,128]{1,0:T(8,128)(2,1)S(1)}, bf16[288,128]{1,0:T(8,128)(2,1)S(1)}, u32[]{:S(2)}, u32[]{:S(2)}) collective-permute-start(bf16[288,128]{1,0:T(8,128)(2,1)S(1)} %add_convert_fusion.4), channel_id=1, source_target_pairs={{0,8},{1,9},{2,10},{3,11},{4,12},{5,13},{6,14},{7,15},{8,0},{9,1},... | collective-permute-start | bytes 221192 | tf_op jit(solution)/shard_map/ppermute | solution.py:557
  44.9 5.4 %collective-permute-start.14 = (bf16[320,128]{1,0:T(8,128)(2,1)S(1)}, bf16[320,128]{1,0:T(8,128)(2,1)S(1)}, u32[]{:S(2)}, u32[]{:S(2)}) collective-permute-start(bf16[320,128]{1,0:T(8,128)(2,1)S(1)} %slice.57), channel_id=1, source_target_pairs={{0,4},{1,5},{2,6},{3,7},{4,0},{5,1},{6,2},{7,3},{8,12},{9,13},{10,... | collective-permute-start | bytes 245768 | tf_op jit(solution)/shard_map/ppermute | solution.py:557
  50.3 5.3 %collective-permute-start.16 = (bf16[160,128]{1,0:T(8,128)(2,1)S(1)}, bf16[160,128]{1,0:T(8,128)(2,1)S(1)}, u32[]{:S(2)}, u32[]{:S(2)}) collective-permute-start(bf16[160,128]{1,0:T(8,128)(2,1)S(1)} %slice.59), channel_id=1, source_target_pairs={{0,8},{1,9},{2,10},{3,11},{4,12},{5,13},{6,14},{7,15},{8,0},{9,1},... | collective-permute-start | bytes 122888 | tf_op jit(solution)/shard_map/ppermute | solution.py:557
  51.8 4.4 %collective-permute-start.15 = (bf16[288,128]{1,0:T(8,128)(2,1)S(1)}, bf16[288,128]{1,0:T(8,128)(2,1)S(1)}, u32[]{:S(2)}, u32[]{:S(2)}) collective-permute-start(bf16[288,128]{1,0:T(8,128)(2,1)S(1)} %add_convert_fusion.3), channel_id=1, source_target_pairs={{0,2},{1,3},{2,0},{3,1},{4,6},{5,7},{6,4},{7,5},{8,10},{9,11},{10,... | collective-permute-start | bytes 221192 | tf_op jit(solution)/shard_map/ppermute | solution.py:557
  56.2 1.4 %collective-permute-start.17 = (bf16[2,288,128]{2,1,0:T(8,128)(2,1)S(1)}, bf16[2,288,128]{2,1,0:T(8,128)(2,1)S(1)}, u32[]{:S(2)}, u32[]{:S(2)}) collective-permute-start(bf16[2,288,128]{2,1,0:T(8,128)(2,1)S(1)} %pad_maximum_fusion.4.near_ref), channel_id=1, source_target_pairs={{0,1},{1,0},{2,3},{3,2},{4,5},{5,4},{6,7},{7,6},{8,9},{9,8},{10,11... | collective-permute-start | bytes 442376 | tf_op jit(solution)/shard_map/ppermute | solution.py:557

commit v6 on v5

--- a/solution.py
+++ b/solution.py
@@ -179,10 +179,10 @@
     proj_out[...] = proj_ref[...]
     wv_ref[...] = jnp.zeros(wv_ref.shape, BF16)
     for tap in range(3):
-        lanes = slice(tap * C1, tap * C1 + C1)
+        at = (tap - 1) % 3 * WIN
         rows = w_ref[tap * 288 : tap * 288 + 288, :]
-        wv_ref[0, 32:320, lanes] = rows
-        wv_ref[1, 96:384, lanes] = rows
+        wv_ref[0, at + 32 : at + 320, :] = rows
+        wv_ref[1, at + 96 : at + 384, :] = rows
 
 
 def prepare(target_row, target_col, conv_weight, conv_bias, proj_weight):
@@ -190,7 +190,7 @@
     return pl.pallas_call(
         prepare_kernel,
         out_shape=(
-            same[0], same[0], jax.ShapeDtypeStruct((2, WIN, WIN), BF16), same[1], same[2]
+            same[0], same[0], jax.ShapeDtypeStruct((2, 3 * WIN, C1), BF16), same[1], same[2]
         ),
         compiler_params=vmem_of(0),
         cost_estimate=pl.CostEstimate(flops=10**6, bytes_accessed=10**6, transcendentals=0),
@@ -340,12 +340,13 @@
             value = lanes_of(slice(q * WIN, q * WIN + WIN))
             for kind in range(3):
                 part = value[step * kind : step * kind + step]
-                views[kind, 1, rows, :] = part
-                views[kind, 0, rows, 128:WIN] = part[:, 0:256]
+                lane = kind * WIN
+                views[1, rows, lane : lane + WIN] = part
+                views[0, rows, lane + 128 : lane + WIN] = part[:, 0:256]
                 if q == 0:
-                    views[kind, 0, rows, 0:128] = jnp.zeros((step, 128), BF16)
+                    views[0, rows, lane : lane + 128] = jnp.zeros((step, 128), BF16)
                 if q < 7:
-                    views[kind, 0, after, 0:128] = part[:, 256:WIN]
+                    views[0, after, lane : lane + 128] = part[:, 256:WIN]
 
     picks = row_pick(me, count, bits)
     own_picks = own_pick()
@@ -366,12 +367,7 @@
 
     bias = bias_ref[...]
     for g in range(2):
-        inner[...] = (
-            dot(views[0, g], wv_ref[g, :, C1 : 2 * C1])
-            + dot(views[1, g], wv_ref[g, :, 2 * C1 : 3 * C1])
-            + dot(views[2, g], wv_ref[g, :, 0:C1])
-            + bias
-        )
+        inner[...] = dot(views[g], wv_ref[g]) + bias
         for q in range(8):
             c = 2 * q + g
             hid_ref[c] = jnp.maximum(inner[q * ny : q * ny + ny, :], 0.0).astype(BF16)
@@ -426,10 +422,11 @@
             device + 1 == me, first_tops, 0.0
         ).astype(BF16)
 
-    parts = [[dot(turned[g], views[kind, g]) for g in range(2)] for kind in range(3)]
+    parts = [dot(turned[g], views[g]) for g in range(2)]
     wsum[9 * C0 + 2 * C1 :, :] = jnp.zeros((4 * quarter - 9 * C0 - 2 * C1, C1), F32)
     for tap in range(3):
-        left, right = parts[(tap - 1) % 3]
+        lanes = slice((tap - 1) % 3 * WIN, (tap - 1) % 3 * WIN + WIN)
+        left, right = parts[0][:, lanes], parts[1][:, lanes]
         wsum[tap * 288 : tap * 288 + 288, :] = left.T[32:320] + right.T[96:384]
     wsum[9 * C0 : 9 * C0 + C1, :] = grad_proj[:, 0:C1]
     wsum[9 * C0 + C1 : 9 * C0 + 2 * C1, :] = grad_proj[:, C1:]
@@ -458,7 +455,7 @@
             jax.ShapeDtypeStruct((PIX, C1), BF16),
         ),
         scratch_shapes=[
-            pltpu.VMEM((3, 2, rows, WIN), BF16),
+            pltpu.VMEM((2, rows, 3 * WIN), BF16),
             pltpu.VMEM((rows, C1), F32),
             pltpu.VMEM((WC, ny + 8, C1), F32),
             pltpu.VMEM((2, rows, C1), BF16),
@@ -492,8 +489,8 @@
         here = jnp.concatenate(here, axis=0).astype(BF16)
         both = jnp.concatenate(both, axis=0).astype(BF16)
         weights = wv_ref[g]
-        outer = jnp.concatenate([weights[:, 2 * C1 : 3 * C1], weights[:, 0:C1]], axis=1)
-        return dot_nt(here, weights[:, C1 : 2 * C1]), dot_nt(both, outer)
+        outer = jnp.concatenate([weights[WIN : 2 * WIN], weights[2 * WIN :]], axis=1)
+        return dot_nt(here, weights[0:WIN]), dot_nt(both, outer)
 
     even, odd = spread(0), spread(1)
     for parity in range(2):
@@ -604,14 +601,12 @@
     given, pixels = plus(kept[1], other[1]), plus(kept[0], other[0])
     given_sums, given = lax.optimization_barrier((given_sums, given))
     sums = plus(sums, swap(given_sums, 2, count))
+    lookups = lookup(ny, target_row, target_col, hid, first, proj_weight)
+    sums, lookups = lax.optimization_barrier((sums, lookups))
     pixels = plus(pixels, swap(given, 2, count))
     for bit in range(2, bits):
         sums = plus(sums, swap(sums, 1 << bit, count))
-        if bit < bits - 1:
-            sums, pixels, target_row = lax.optimization_barrier((sums, pixels, target_row))
-        else:
-            lookups = lookup(ny, target_row, target_col, hid, first, proj_weight)
-            sums, pixels, lookups = lax.optimization_barrier((sums, pixels, lookups))
+        sums, pixels = lax.optimization_barrier((sums, pixels))
         half = pixels.shape[0] // 2
         pixels = plus(pixels[:half], swap(pixels[half:], 1 << bit, count))
     near = jnp.stack([sums, swap(sums, 2, count)])

time: 58.7 us -> 58.8 us (level)
  transfers between devices with their start and end apart: 18 -> 18, of which waited for: 13 -> 14; matrix products, arithmetic and copies ran while one was open for 2% -> 2% of each run, Pallas kernels for 15% -> 15%
where the time goes in v6:
time: 58.8 us; the launch traced here: 58.5 us
  waiting for transfers between devices  22 us (37%)
  starting transfers between devices  18.7 us (32%)
  Pallas kernels  14.7 us (25%)
  local copies, waits for them, and re-layouts  1.86 us (3%)
  between operations  0.89 us (2%)
    ppermute x17, waiting for transfers between devices, swap(): return lax.ppermute(value, 'rows', [(i, i ^ bit) for i in range(count)])  22 us
    ppermute x17, starting transfers between devices, swap(): return lax.ppermute(value, 'rows', [(i, i ^ bit) for i in range(count)])  17.3 us
    pallas_call x1, Pallas kernels, main(): pl.pallas_call(functools.partial(main_kernel, count, bits, quarter), in_s...  5.29 us
    pallas_call x1, Pallas kernels, scatter(): pl.pallas_call(functools.partial(scatter_kernel, ny), out_shape=(jax.Shap...  3.85 us
    pallas_call x1, Pallas kernels, lookup(): pl.pallas_call(functools.partial(lookup_kernel, ny), out_shape=jax.ShapeD...  3.52 us
    ppermute x1, starting transfers between devices, per_device(): lax.ppermute(frames[0, 2 * RD - 1:], 'rows', [(i, i + 1) for i in range(c...  1.42 us
  transfers between devices with their start and end apart: 18, of which 14 were waited for; matrix products, arithmetic and copies ran while one was open for 2% of the time, Pallas kernels for 15%

profile of v6, /device:TPU:0, one launch (start us, length us, event | category | flops | bytes accessed | tf_op | source)
XLA Modules:
  0.0 58.5 jit_solution(2426590583726675547)
XLA Ops:
  0.7 1.0 %slice_bitcast_fusion = (bf16[16,3072]{1,0:T(8,128)(2,1)S(1)}, bf16[16,3072]{1,0:T(8,128)(2,1)S(1)}) fusion(bf16[2,16,3072]{2,1,0:T(8,128)(2,1)} %param.7), kind=kLoop, calls=%fused_computation.18 | loop fusion | bytes 393216 | tf_op jit(solution)/shard_map/squeeze | solution.py:594
  1.7 3.1 %collective-permute-start.1 = (bf16[16,3072]{1,0:T(8,128)(2,1)S(1)}, bf16[16,3072]{1,0:T(8,128)(2,1)S(1)}, u32[]{:S(2)}, u32[]{:S(2)}) collective-permute-start(bf16[16,3072]{1,0:T(8,128)(2,1)S(1)} %get-tuple-element.88), channel_id=1, source_target_pairs={{0,4},{1,5},{2,6},{3,7},{4,0},{5,1},{6,2},{7,3},{8,12},{9,13},{10,... | collective-permute-start | bytes 294920 | tf_op jit(solution)/shard_map/ppermute | solution.py:554
  4.8 2.6 %collective-permute-start = (bf16[16,3072]{1,0:T(8,128)(2,1)S(1)}, bf16[16,3072]{1,0:T(8,128)(2,1)S(1)}, u32[]{:S(2)}, u32[]{:S(2)}) collective-permute-start(bf16[16,3072]{1,0:T(8,128)(2,1)S(1)} %get-tuple-element.88), channel_id=1, source_target_pairs={{0,8},{1,9},{2,10},{3,11},{4,12},{5,13},{6,14},{7,15},{8,0},{9,1},... | collective-permute-start | bytes 294920 | tf_op jit(solution)/shard_map/ppermute | solution.py:554
  7.4 0.8 %slice_bitcast_fusion.2 = bf16[1,3072]{1,0:T(2,128)(2,1)S(1)} fusion(bf16[2,16,3072]{2,1,0:T(8,128)(2,1)} %param.7), kind=kLoop, calls=%fused_computation.23 | loop fusion | bytes 12288 | tf_op jit(solution)/shard_map/squeeze | solution.py:568
  8.2 1.4 %collective-permute-start.5 = (bf16[1,3072]{1,0:T(2,128)(2,1)S(1)}, bf16[1,3072]{1,0:T(2,128)(2,1)S(1)}, u32[]{:S(2)}, u32[]{:S(2)}) collective-permute-start(bf16[1,3072]{1,0:T(2,128)(2,1)S(1)} %slice_bitcast_fusion.2), channel_id=1, source_target_pairs={{0,1},{1,2},{2,3},{3,4},{4,5},{5,6},{6,7},{7,8},{8,9},{9,10},{10,1... | collective-permute-start | bytes 18440 | tf_op jit(solution)/shard_map/ppermute | solution.py:568
  9.8 2.2 %collective-permute-done = bf16[16,3072]{1,0:T(8,128)(2,1)S(1)} collective-permute-done((bf16[16,3072]{1,0:T(8,128)(2,1)S(1)}, bf16[16,3072]{1,0:T(8,128)(2,1)S(1)}, u32[]{:S(2)}, u32[]{:S(2)}) %collective-permute-start) | collective-permute-done | bytes 98336 | tf_op jit(solution)/shard_map/ppermute | solution.py:554
  12.4 1.6 %collective-permute-start.3 = (bf16[32,3072]{1,0:T(8,128)(2,1)S(1)}, bf16[32,3072]{1,0:T(8,128)(2,1)S(1)}, u32[]{:S(2)}, u32[]{:S(2)}) collective-permute-start(bf16[32,3072]{1,0:T(8,128)(2,1)S(1)} %pad_maximum_fusion.3), channel_id=1, source_target_pairs={{0,2},{1,3},{2,0},{3,1},{4,6},{5,7},{6,4},{7,5},{8,10},{9,11},{10,... | collective-permute-start | bytes 589832 | tf_op jit(solution)/shard_map/ppermute | solution.py:554
  14.0 2.8 %collective-permute-done.2 = bf16[16,3072]{1,0:T(8,128)(2,1)S(1)} collective-permute-done((bf16[16,3072]{1,0:T(8,128)(2,1)S(1)}, bf16[16,3072]{1,0:T(8,128)(2,1)S(1)}, u32[]{:S(2)}, u32[]{:S(2)}) %collective-permute-start.2) | collective-permute-done | bytes 98336 | tf_op jit(solution)/shard_map/ppermute | solution.py:554
  16.9 1.4 %collective-permute-start.4 = (bf16[32,3072]{1,0:T(8,128)(2,1)S(1)}, bf16[32,3072]{1,0:T(8,128)(2,1)S(1)}, u32[]{:S(2)}, u32[]{:S(2)}) collective-permute-start(bf16[32,3072]{1,0:T(8,128)(2,1)S(1)} %pad_maximum_fusion.2), channel_id=1, source_target_pairs={{0,2},{1,3},{2,0},{3,1},{4,6},{5,7},{6,4},{7,5},{8,10},{9,11},{10,... | collective-permute-start | bytes 589832 | tf_op jit(solution)/shard_map/ppermute | solution.py:554
  18.4 3.8 %scatter.1 = (bf16[16,128,128]{2,1,0:T(8,128)(2,1)S(1)}, bf16[128,2048]{1,0:T(8,128)(2,1)S(1)}) custom-call(s32[12,128]{1,0:T(8,128)S(1)} %get-tuple-element.55.row_ref, s32[12,128]{1,0:T(8,128)S(1)} %get-tuple-element.56.col_ref, bf16[3888,128]{1,0:T(8,128)(2,1)S(1)} %copy-done.5), custom_call_target="tpu_custom_call" | custom-call | flops 1000000000 | bytes 4000000 | tf_op jit(solution)/shard_map/scatter/pallas_call | solution.py:156
  22.3 1.1 %collective-permute-done.4 = bf16[32,3072]{1,0:T(8,128)(2,1)S(1)} collective-permute-done((bf16[32,3072]{1,0:T(8,128)(2,1)S(1)}, bf16[32,3072]{1,0:T(8,128)(2,1)S(1)}, u32[]{:S(2)}, u32[]{:S(2)}) %collective-permute-start.4) | collective-permute-done | bytes 196640 | tf_op jit(solution)/shard_map/ppermute | solution.py:554
  23.6 1.7 %collective-permute-done.7.maps3_ref = bf16[64,3072]{1,0:T(8,128)(2,1)S(1)} collective-permute-done((bf16[64,3072]{1,0:T(8,128)(2,1)S(1)}, bf16[64,3072]{1,0:T(8,128)(2,1)S(1)}, u32[]{:S(2)}, u32[]{:S(2)}) %collective-permute-start.7) | collective-permute-done | bytes 393248 | tf_op jit(solution)/shard_map/ppermute | solution.py:554
  25.3 5.3 %features.1 = (bf16[2,640,128]{2,1,0:T(8,128)(2,1)S(1)}, bf16[2,640,128]{2,1,0:T(8,128)(2,1)S(1)}, bf16[2,288,128]{2,1,0:T(8,128)(2,1)S(1)}, bf16[2,288,128]{2,1...) custom-call(s32[1]{0:T(128)} %bitcast.me_ref, ...), custom_call_target="tpu_custom_call" | custom-call | flops 4000000000 | bytes 6000000 | tf_op jit(solution)/shard_map/features/pallas_call | solution.py:445
  30.8 0.4 collective-permute-start.9
  31.1 0.9 %collective-permute-done.8 = bf16[2,288,128]{2,1,0:T(8,128)(2,1)S(1)} collective-permute-done((bf16[2,288,128]{2,1,0:T(8,128)(2,1)S(1)}, bf16[2,288,128]{2,1,0:T(8,128)(2,1)S(1)}, u32[]{:S(2)}, u32[]{:S(2)}) %collective-permute-start.8) | collective-permute-done | bytes 147488 | tf_op jit(solution)/shard_map/ppermute | solution.py:554
  32.0 0.4 collective-permute-done.9
  32.5 0.6 %collective-permute-start.10 = (bf16[288,128]{1,0:T(8,128)(2,1)S(1)}, bf16[288,128]{1,0:T(8,128)(2,1)S(1)}, u32[]{:S(2)}, u32[]{:S(2)}) collective-permute-start(bf16[288,128]{1,0:T(8,128)(2,1)S(1)} %fusion.5), channel_id=1, source_target_pairs={{0,2},{1,3},{2,0},{3,1},{4,6},{5,7},{6,4},{7,5},{8,10},{9,11},{10,... | collective-permute-start | bytes 221192 | tf_op jit(solution)/shard_map/ppermute | solution.py:554
  33.1 3.5 %lookup.1 = bf16[3888,128]{1,0:T(8,128)(2,1)} custom-call(s32[12,128]{1,0:T(8,128)S(1)} %get-tuple-element.55.row_ref, s32[12,128]{1,0:T(8,128)S(1)} %get-tuple-element.56.col_ref, bf16[16,128,128]{2,1,0:T(8,128)(2,1)S(1)} %get-tuple-element.72.hid_ref, bf16[128,256]{1,0:T(8,128)(2,1)S(1)} %get-tuple-element.73.first_ref, ...), custom_call_target="tpu_custom_call" | custom-call | flops 1000000000 | bytes 4000000 | tf_op jit(solution)/shard_map/lookup/pallas_call | solution.py:278
  36.7 0.4 collective-permute-done.10
  37.1 1.6 %collective-permute-start.11 = (bf16[288,128]{1,0:T(8,128)(2,1)S(1)}, bf16[288,128]{1,0:T(8,128)(2,1)S(1)}, u32[]{:S(2)}, u32[]{:S(2)}) collective-permute-start(bf16[288,128]{1,0:T(8,128)(2,1)S(1)} %fusion.3), channel_id=1, source_target_pairs={{0,4},{1,5},{2,6},{3,7},{4,0},{5,1},{6,2},{7,3},{8,12},{9,13},{10,... | collective-permute-start | bytes 221192 | tf_op jit(solution)/shard_map/ppermute | solution.py:554
  38.7 1.1 %collective-permute-start.12 = (bf16[640,128]{1,0:T(8,128)(2,1)S(1)}, bf16[640,128]{1,0:T(8,128)(2,1)S(1)}, u32[]{:S(2)}, u32[]{:S(2)}) collective-permute-start(bf16[640,128]{1,0:T(8,128)(2,1)S(1)} %fusion.1), channel_id=1, source_target_pairs={{0,2},{1,3},{2,0},{3,1},{4,6},{5,7},{6,4},{7,5},{8,10},{9,11},{10,... | collective-permute-start | bytes 491528 | tf_op jit(solution)/shard_map/ppermute | solution.py:554
  39.8 1.7 %collective-permute-done.11 = bf16[288,128]{1,0:T(8,128)(2,1)S(1)} collective-permute-done((bf16[288,128]{1,0:T(8,128)(2,1)S(1)}, bf16[288,128]{1,0:T(8,128)(2,1)S(1)}, u32[]{:S(2)}, u32[]{:S(2)}) %collective-permute-start.11) | collective-permute-done | bytes 73760 | tf_op jit(solution)/shard_map/ppermute | solution.py:554
  41.5 2.7 %collective-permute-done.12 = bf16[640,128]{1,0:T(8,128)(2,1)S(1)} collective-permute-done((bf16[640,128]{1,0:T(8,128)(2,1)S(1)}, bf16[640,128]{1,0:T(8,128)(2,1)S(1)}, u32[]{:S(2)}, u32[]{:S(2)}) %collective-permute-start.12) | collective-permute-done | bytes 163872 | tf_op jit(solution)/shard_map/ppermute | solution.py:554
  44.3 1.5 %collective-permute-start.13 = (bf16[288,128]{1,0:T(8,128)(2,1)S(1)}, bf16[288,128]{1,0:T(8,128)(2,1)S(1)}, u32[]{:S(2)}, u32[]{:S(2)}) collective-permute-start(bf16[288,128]{1,0:T(8,128)(2,1)S(1)} %add_convert_fusion.4), channel_id=1, source_target_pairs={{0,8},{1,9},{2,10},{3,11},{4,12},{5,13},{6,14},{7,15},{8,0},{9,1},... | collective-permute-start | bytes 221192 | tf_op jit(solution)/shard_map/ppermute | solution.py:554
  45.8 0.4 collective-permute-start.14
  46.2 4.2 %collective-permute-done.13 = bf16[288,128]{1,0:T(8,128)(2,1)S(1)} collective-permute-done((bf16[288,128]{1,0:T(8,128)(2,1)S(1)}, bf16[288,128]{1,0:T(8,128)(2,1)S(1)}, u32[]{:S(2)}, u32[]{:S(2)}) %collective-permute-start.13) | collective-permute-done | bytes 73760 | tf_op jit(solution)/shard_map/ppermute | solution.py:554
  50.4 0.6 %collective-permute-done.14 = bf16[320,128]{1,0:T(8,128)(2,1)S(1)} collective-permute-done((bf16[320,128]{1,0:T(8,128)(2,1)S(1)}, bf16[320,128]{1,0:T(8,128)(2,1)S(1)}, u32[]{:S(2)}, u32[]{:S(2)}) %collective-permute-start.14) | collective-permute-done | bytes 81952 | tf_op jit(solution)/shard_map/ppermute | solution.py:554
  51.1 0.8 %collective-permute-start.16 = (bf16[160,128]{1,0:T(8,128)(2,1)S(1)}, bf16[160,128]{1,0:T(8,128)(2,1)S(1)}, u32[]{:S(2)}, u32[]{:S(2)}) collective-permute-start(bf16[160,128]{1,0:T(8,128)(2,1)S(1)} %slice.59), channel_id=1, source_target_pairs={{0,8},{1,9},{2,10},{3,11},{4,12},{5,13},{6,14},{7,15},{8,0},{9,1},... | collective-permute-start | bytes 122888 | tf_op jit(solution)/shard_map/ppermute | solution.py:554
  51.9 1.4 %collective-permute-start.15 = (bf16[288,128]{1,0:T(8,128)(2,1)S(1)}, bf16[288,128]{1,0:T(8,128)(2,1)S(1)}, u32[]{:S(2)}, u32[]{:S(2)}) collective-permute-start(bf16[288,128]{1,0:T(8,128)(2,1)S(1)} %add_convert_fusion.3), channel_id=1, source_target_pairs={{0,2},{1,3},{2,0},{3,1},{4,6},{5,7},{6,4},{7,5},{8,10},{9,11},{10,... | collective-permute-start | bytes 221192 | tf_op jit(solution)/shard_map/ppermute | solution.py:554
  53.3 2.7 %collective-permute-done.16 = bf16[160,128]{1,0:T(8,128)(2,1)S(1)} collective-permute-done((bf16[160,128]{1,0:T(8,128)(2,1)S(1)}, bf16[160,128]{1,0:T(8,128)(2,1)S(1)}, u32[]{:S(2)}, u32[]{:S(2)}) %collective-permute-start.16) | collective-permute-done | bytes 40992 | tf_op jit(solution)/shard_map/ppermute | solution.py:554
  56.3 1.0 %input_grad.1 = bf16[2,16,3072]{2,1,0:T(8,128)(2,1)} custom-call(bf16[128,128]{1,0:T(8,128)(2,1)S(1)} %get-tuple-element.75.first_ref, bf16[160,128]{1,0:T(8,128)(2,1)S(1)} %add_convert_fusion.7.block_ref, bf16[2,1152,128]{2,1,0:T(8,128)(2,1)S(1)} %get-tuple-element.62.wv_ref), custom_call_target="tpu_custom_call" | custom-call | flops 100000000 | bytes 1000000 | tf_op jit(solution)/shard_map/input_grad/pallas_call | solution.py:512
  57.7 0.9 %weight_grads.1 = (f32[864,128]{1,0:T(8,128)}, f32[1,128]{1,0:T(1,128)}, f32[128,256]{1,0:T(8,128)}) custom-call(s32[1]{0:T(128)} %bitcast.me_ref, bf16[2,288,128]{2,1,0:T(8,128)(2,1)S(1)} %pad_maximum_fusion.4.near_ref, bf16[2,288,128]{2,1,0:T(8,128)(2,1)S(1)} %collective-permute-done.17.far_ref), custom_call_target="tpu_custom_call" | custom-call | tf_op jit(solution)/shard_map/weight_grads/pallas_call | solution.py:539
  (39 shorter events, 1.8 us)
Async XLA Ops:
  0.6 9.0 %copy-start = (bf16[864,128]{1,0:T(8,128)(2,1)S(1)}, bf16[864,128]{1,0:T(8,128)(2,1)}, u32[]{:S(2)}) copy-start(bf16[864,128]{1,0:T(8,128)(2,1)} %w_ref.1) | copy-start | bytes 663556
  0.6 9.0 %copy-start.1 = (bf16[128,256]{1,0:T(8,128)(2,1)S(1)}, bf16[128,256]{1,0:T(8,128)(2,1)}, u32[]{:S(2)}) copy-start(bf16[128,256]{1,0:T(8,128)(2,1)} %proj_ref.1) | copy-start | bytes 196612
  1.7 8.0 %copy-start.2 = (s32[12,128]{1,0:T(8,128)S(1)}, s32[12,128]{1,0:T(8,128)}, u32[]{:S(2)}) copy-start(s32[12,128]{1,0:T(8,128)} %row_ref.1) | copy-start | bytes 18436
  1.7 8.0 %copy-start.3 = (s32[12,128]{1,0:T(8,128)S(1)}, s32[12,128]{1,0:T(8,128)}, u32[]{:S(2)}) copy-start(s32[12,128]{1,0:T(8,128)} %col_ref.1) | copy-start | bytes 18436
  1.7 12.3 %collective-permute-start.1 = (bf16[16,3072]{1,0:T(8,128)(2,1)S(1)}, bf16[16,3072]{1,0:T(8,128)(2,1)S(1)}, u32[]{:S(2)}, u32[]{:S(2)}) collective-permute-start(bf16[16,3072]{1,0:T(8,128)(2,1)S(1)} %get-tuple-element.88), channel_id=1, source_target_pairs={{0,4},{1,5},{2,6},{3,7},{4,0},{5,1},{6,2},{7,3},{8,12},{9,13},{10,... | collective-permute-start | bytes 294920 | tf_op jit(solution)/shard_map/ppermute | solution.py:554
  4.8 7.3 %collective-permute-start = (bf16[16,3072]{1,0:T(8,128)(2,1)S(1)}, bf16[16,3072]{1,0:T(8,128)(2,1)S(1)}, u32[]{:S(2)}, u32[]{:S(2)}) collective-permute-start(bf16[16,3072]{1,0:T(8,128)(2,1)S(1)} %get-tuple-element.88), channel_id=1, source_target_pairs={{0,8},{1,9},{2,10},{3,11},{4,12},{5,13},{6,14},{7,15},{8,0},{9,1},... | collective-permute-start | bytes 294920 | tf_op jit(solution)/shard_map/ppermute | solution.py:554
  8.2 1.5 %copy-start.4 = (f32[128]{0:T(128)S(1)}, f32[128]{0:T(128)}, u32[]{:S(2)}) copy-start(f32[128]{0:T(128)} %param.9) | copy-start | bytes 1540
  8.2 10.2 %copy-start.5 = (bf16[3888,128]{1,0:T(8,128)(2,1)S(1)}, bf16[3888,128]{1,0:T(8,128)(2,1)}, u32[]{:S(2)}) copy-start(bf16[3888,128]{1,0:T(8,128)(2,1)} %cot_hbm) | copy-start | bytes 2985988
  8.2 15.3 %collective-permute-start.5 = (bf16[1,3072]{1,0:T(2,128)(2,1)S(1)}, bf16[1,3072]{1,0:T(2,128)(2,1)S(1)}, u32[]{:S(2)}, u32[]{:S(2)}) collective-permute-start(bf16[1,3072]{1,0:T(2,128)(2,1)S(1)} %slice_bitcast_fusion.2), channel_id=1, source_target_pairs={{0,1},{1,2},{2,3},{3,4},{4,5},{5,6},{6,7},{7,8},{8,9},{9,10},{10,1... | collective-permute-start | bytes 18440 | tf_op jit(solution)/shard_map/ppermute | solution.py:568
  12.1 4.8 %collective-permute-start.2 = (bf16[16,3072]{1,0:T(8,128)(2,1)S(1)}, bf16[16,3072]{1,0:T(8,128)(2,1)S(1)}, u32[]{:S(2)}, u32[]{:S(2)}) collective-permute-start(bf16[16,3072]{1,0:T(8,128)(2,1)S(1)} %collective-permute-done), channel_id=1, source_target_pairs={{0,4},{1,5},{2,6},{3,7},{4,0},{5,1},{6,2},{7,3},{8,12},{9,13},{10,... | collective-permute-start | bytes 294920 | tf_op jit(solution)/shard_map/ppermute | solution.py:554
  12.4 9.8 %collective-permute-start.3 = (bf16[32,3072]{1,0:T(8,128)(2,1)S(1)}, bf16[32,3072]{1,0:T(8,128)(2,1)S(1)}, u32[]{:S(2)}, u32[]{:S(2)}) collective-permute-start(bf16[32,3072]{1,0:T(8,128)(2,1)S(1)} %pad_maximum_fusion.3), channel_id=1, source_target_pairs={{0,2},{1,3},{2,0},{3,1},{4,6},{5,7},{6,4},{7,5},{8,10},{9,11},{10,... | collective-permute-start | bytes 589832 | tf_op jit(solution)/shard_map/ppermute | solution.py:554
  16.9 6.6 %collective-permute-start.4 = (bf16[32,3072]{1,0:T(8,128)(2,1)S(1)}, bf16[32,3072]{1,0:T(8,128)(2,1)S(1)}, u32[]{:S(2)}, u32[]{:S(2)}) collective-permute-start(bf16[32,3072]{1,0:T(8,128)(2,1)S(1)} %pad_maximum_fusion.2), channel_id=1, source_target_pairs={{0,2},{1,3},{2,0},{3,1},{4,6},{5,7},{6,4},{7,5},{8,10},{9,11},{10,... | collective-permute-start | bytes 589832 | tf_op jit(solution)/shard_map/ppermute | solution.py:554
  18.3 5.1 %collective-permute-start.6 = (bf16[64,3072]{1,0:T(8,128)(2,1)S(1)}, bf16[64,3072]{1,0:T(8,128)(2,1)S(1)}, u32[]{:S(2)}, u32[]{:S(2)}) collective-permute-start(bf16[64,3072]{1,0:T(8,128)(2,1)S(1)} %pad_maximum_fusion.maps0_ref), channel_id=1, source_target_pairs={{0,1},{1,0},{2,3},{3,2},{4,5},{5,4},{6,7},{7,6},{8,9},{9,8},{10,11... | collective-permute-start | bytes 1179656 | tf_op jit(solution)/shard_map/ppermute | solution.py:554
  23.5 1.8 %collective-permute-start.7 = (bf16[64,3072]{1,0:T(8,128)(2,1)S(1)}, bf16[64,3072]{1,0:T(8,128)(2,1)S(1)}, u32[]{:S(2)}, u32[]{:S(2)}) collective-permute-start(bf16[64,3072]{1,0:T(8,128)(2,1)S(1)} %pad_maximum_fusion.1.maps1_ref), channel_id=1, source_target_pairs={{0,1},{1,0},{2,3},{3,2},{4,5},{5,4},{6,7},{7,6},{8,9},{9,8},{10,11... | collective-permute-start | bytes 1179656 | tf_op jit(solution)/shard_map/ppermute | solution.py:554
  30.6 1.4 %collective-permute-start.8 = (bf16[2,288,128]{2,1,0:T(8,128)(2,1)S(1)}, bf16[2,288,128]{2,1,0:T(8,128)(2,1)S(1)}, u32[]{:S(2)}, u32[]{:S(2)}) collective-permute-start(bf16[2,288,128]{2,1,0:T(8,128)(2,1)S(1)} %get-tuple-element.68), channel_id=1, source_target_pairs={{0,1},{1,0},{2,3},{3,2},{4,5},{5,4},{6,7},{7,6},{8,9},{9,8},{10,11... | collective-permute-start | bytes 442376 | tf_op jit(solution)/shard_map/ppermute | solution.py:554
  30.8 1.7 %collective-permute-start.9 = (bf16[2,640,128]{2,1,0:T(8,128)(2,1)S(1)}, bf16[2,640,128]{2,1,0:T(8,128)(2,1)S(1)}, u32[]{:S(2)}, u32[]{:S(2)}) collective-permute-start(bf16[2,640,128]{2,1,0:T(8,128)(2,1)S(1)} %get-tuple-element.70), channel_id=1, source_target_pairs={{0,1},{1,0},{2,3},{3,2},{4,5},{5,4},{6,7},{7,6},{8,9},{9,8},{10,11... | collective-permute-start | bytes 983048 | tf_op jit(solution)/shard_map/ppermute | solution.py:554
  32.5 4.5 %collective-permute-start.10 = (bf16[288,128]{1,0:T(8,128)(2,1)S(1)}, bf16[288,128]{1,0:T(8,128)(2,1)S(1)}, u32[]{:S(2)}, u32[]{:S(2)}) collective-permute-start(bf16[288,128]{1,0:T(8,128)(2,1)S(1)} %fusion.5), channel_id=1, source_target_pairs={{0,2},{1,3},{2,0},{3,1},{4,6},{5,7},{6,4},{7,5},{8,10},{9,11},{10,... | collective-permute-start | bytes 221192 | tf_op jit(solution)/shard_map/ppermute | solution.py:554
  37.1 4.4 %collective-permute-start.11 = (bf16[288,128]{1,0:T(8,128)(2,1)S(1)}, bf16[288,128]{1,0:T(8,128)(2,1)S(1)}, u32[]{:S(2)}, u32[]{:S(2)}) collective-permute-start(bf16[288,128]{1,0:T(8,128)(2,1)S(1)} %fusion.3), channel_id=1, source_target_pairs={{0,4},{1,5},{2,6},{3,7},{4,0},{5,1},{6,2},{7,3},{8,12},{9,13},{10,... | collective-permute-start | bytes 221192 | tf_op jit(solution)/shard_map/ppermute | solution.py:554
  38.7 5.5 %collective-permute-start.12 = (bf16[640,128]{1,0:T(8,128)(2,1)S(1)}, bf16[640,128]{1,0:T(8,128)(2,1)S(1)}, u32[]{:S(2)}, u32[]{:S(2)}) collective-permute-start(bf16[640,128]{1,0:T(8,128)(2,1)S(1)} %fusion.1), channel_id=1, source_target_pairs={{0,2},{1,3},{2,0},{3,1},{4,6},{5,7},{6,4},{7,5},{8,10},{9,11},{10,... | collective-permute-start | bytes 491528 | tf_op jit(solution)/shard_map/ppermute | solution.py:554
  44.3 6.1 %collective-permute-start.13 = (bf16[288,128]{1,0:T(8,128)(2,1)S(1)}, bf16[288,128]{1,0:T(8,128)(2,1)S(1)}, u32[]{:S(2)}, u32[]{:S(2)}) collective-permute-start(bf16[288,128]{1,0:T(8,128)(2,1)S(1)} %add_convert_fusion.4), channel_id=1, source_target_pairs={{0,8},{1,9},{2,10},{3,11},{4,12},{5,13},{6,14},{7,15},{8,0},{9,1},... | collective-permute-start | bytes 221192 | tf_op jit(solution)/shard_map/ppermute | solution.py:554
  45.8 5.2 %collective-permute-start.14 = (bf16[320,128]{1,0:T(8,128)(2,1)S(1)}, bf16[320,128]{1,0:T(8,128)(2,1)S(1)}, u32[]{:S(2)}, u32[]{:S(2)}) collective-permute-start(bf16[320,128]{1,0:T(8,128)(2,1)S(1)} %slice.57), channel_id=1, source_target_pairs={{0,4},{1,5},{2,6},{3,7},{4,0},{5,1},{6,2},{7,3},{8,12},{9,13},{10,... | collective-permute-start | bytes 245768 | tf_op jit(solution)/shard_map/ppermute | solution.py:554
  51.1 5.0 %collective-permute-start.16 = (bf16[160,128]{1,0:T(8,128)(2,1)S(1)}, bf16[160,128]{1,0:T(8,128)(2,1)S(1)}, u32[]{:S(2)}, u32[]{:S(2)}) collective-permute-start(bf16[160,128]{1,0:T(8,128)(2,1)S(1)} %slice.59), channel_id=1, source_target_pairs={{0,8},{1,9},{2,10},{3,11},{4,12},{5,13},{6,14},{7,15},{8,0},{9,1},... | collective-permute-start | bytes 122888 | tf_op jit(solution)/shard_map/ppermute | solution.py:554
  51.9 4.4 %collective-permute-start.15 = (bf16[288,128]{1,0:T(8,128)(2,1)S(1)}, bf16[288,128]{1,0:T(8,128)(2,1)S(1)}, u32[]{:S(2)}, u32[]{:S(2)}) collective-permute-start(bf16[288,128]{1,0:T(8,128)(2,1)S(1)} %add_convert_fusion.3), channel_id=1, source_target_pairs={{0,2},{1,3},{2,0},{3,1},{4,6},{5,7},{6,4},{7,5},{8,10},{9,11},{10,... | collective-permute-start | bytes 221192 | tf_op jit(solution)/shard_map/ppermute | solution.py:554
  56.2 1.4 %collective-permute-start.17 = (bf16[2,288,128]{2,1,0:T(8,128)(2,1)S(1)}, bf16[2,288,128]{2,1,0:T(8,128)(2,1)S(1)}, u32[]{:S(2)}, u32[]{:S(2)}) collective-permute-start(bf16[2,288,128]{2,1,0:T(8,128)(2,1)S(1)} %pad_maximum_fusion.4.near_ref), channel_id=1, source_target_pairs={{0,1},{1,0},{2,3},{3,2},{4,5},{5,4},{6,7},{7,6},{8,9},{9,8},{10,11... | collective-permute-start | bytes 442376 | tf_op jit(solution)/shard_map/ppermute | solution.py:554
